TPU v7x, 32 devices: a whole 2x2x4 slice. The times are simulated.
32 devices in a mesh: dp: 4 (over y, x), wide: 8 (over z, core).
Axes of the slice: x: 2, y: 2, z: 4, core: 2. Of those that a mesh axis runs over, the one named last changes fastest.
Arguments:
- inputs: float32 [4, 73, 32, 720], P('dp', None, 'wide'), may hold values from -6 to 6
- targets: float32 [4, 73, 32, 720], P('dp', None, 'wide'), may hold values from -6 to 6
- land_mask: int32 [32, 720], P('wide'), may hold values 0 or 1
- missing_mask: int32 [4, 32, 720], P('dp', 'wide'), may hold values from 0 to 1, as said below
- order_map: int32 [360], replicated, may hold values from 0 to 359, each once
- degree_map: int32 [360], replicated, may hold values from 0 to 359, each once
- forward_table: float32 [360, 32, 360], P('wide'), may hold values from -1 to 1
- inverse_table: float32 [360, 360, 32], P('wide'), may hold values from -0.3125 to 0.3125
- spectral_weight: float32 [360, 2, 256, 256], P('wide'), may hold values from -0.25 to 0.25
- spectral_first: float32 [360, 2, 256, 256], P('wide'), may hold values from -8.940697e-08 to 8.940697e-08
- spectral_second: float32 [360, 2, 256, 256], P('wide'), may hold values from 2.10586e-17 to 8.42344e-17
- io_weight: float32 [2, 73, 256], replicated, may hold values from -0.5 to 0.5
- io_first: float32 [2, 73, 256], replicated, may hold values from -8.940697e-08 to 8.940697e-08
- io_second: float32 [2, 73, 256], replicated, may hold values from 2.10586e-17 to 8.42344e-17
- mlp_weight: float32 [2, 256, 512], replicated, may hold values from -0.375 to 0.375
- mlp_first: float32 [2, 256, 512], replicated, may hold values from -8.940697e-08 to 8.940697e-08
- mlp_second: float32 [2, 256, 512], replicated, may hold values from 2.10586e-17 to 8.42344e-17
- biases: float32 [1097], replicated, may hold values from -3 to 3
- bias_first: float32 [1097], replicated, may hold values from -2.9802322e-07 to 2.9802322e-07
- bias_second: float32 [1097], replicated, may hold values from 1.8952741e-16 to 7.5810963e-16
Outputs:
- loss_sum: float32 [], replicated
- valid_weight: float32 [], replicated
- grad_norm: float32 [], replicated
- spectral_new: float32 [360, 2, 256, 256], P('wide')
- spectral_first_new: float32 [360, 2, 256, 256], P('wide')
- spectral_second_new: float32 [360, 2, 256, 256], P('wide')
- spectral_low: bfloat16 [360, 2, 256, 256], P('wide')
- io_new: float32 [2, 73, 256], replicated
- io_first_new: float32 [2, 73, 256], replicated
- io_second_new: float32 [2, 73, 256], replicated
- io_low: bfloat16 [2, 73, 256], replicated
- mlp_new: float32 [2, 256, 512], replicated
- mlp_first_new: float32 [2, 256, 512], replicated
- mlp_second_new: float32 [2, 256, 512], replicated
- mlp_low: bfloat16 [2, 256, 512], replicated
- bias_new: float32 [1097], replicated
- bias_first_new: float32 [1097], replicated
- bias_second_new: float32 [1097], replicated
- bias_low: bfloat16 [1097], replicated
Inputs may be any that keep to these rules, and one draw needn't show every extreme that they name: `missing_mask`: 1 marks a missing value. `order_map`: a permutation of 0 to 359; order slot s is held by index s // (360 / size of wide) of the wide axis. `degree_map`: a permutation of 0 to 359; degree slot t is held by index t // (360 / size of wide) of the wide axis.
All inputs are finite; a program needn't handle non-finite values. No bound on the sum of `land_mask` on one device may be relied on, other than what follows from the above.
Results may differ from a plain program's by a relative error of at most 0.001.
Values sent between devices are 32-bit elements; how exact they have to be, the bound alone decides.
No kernel may reach another device: no remote copies, remote signals or barrier semaphores. Data moves between devices by JAX's collectives and lax.ppermute only.
A program may use at most 640 MiB of HBM per device.

v0:
```python
import math

import jax
import jax.numpy as jnp
from jax import lax
from jax.sharding import PartitionSpec as P

M = 360
L = 360
SEA_CH = 1
STEP = 5


HIGHEST = lax.Precision.HIGHEST
CLIP_LIMIT = 0.001
LEARN_RATE = 0.1
BETA_ONE = 0.9
BETA_TWO = 0.999
EPSILON = 1e-08
WEIGHT_DECAY = 0.1


def smooth(values):
    return jax.nn.gelu(values, approximate=True)


def dft_tables(order_map, lon_count):
    columns = jnp.arange(lon_count, dtype=jnp.int32)
    phase_angle = (order_map[:, None] * columns[None, :] % lon_count).astype(jnp.float32) * (
        2.0 * math.pi / lon_count
    )
    cosine = jnp.cos(phase_angle)
    sine_part = jnp.sin(phase_angle)
    forward = jnp.stack([cosine, -sine_part], axis=1) / lon_count
    factor = jnp.where(order_map == 0, 1.0, 2.0).astype(jnp.float32)
    inverse = factor[:, None, None] * jnp.stack([cosine, -sine_part], axis=1)
    return (forward, inverse)


def triangle_mask(orders, degree_map):
    live = (
        (degree_map[None, :] >= orders[:, None]) & (orders[:, None] < M) & (degree_map[None, :] < L)
    )
    return live.astype(jnp.float32)


def complex_block(weight):
    real_part = weight[:, 0]
    imag_part = weight[:, 1]
    top_half = jnp.concatenate([real_part, imag_part], axis=2)
    bottom_half = jnp.concatenate([-imag_part, real_part], axis=2)
    return jnp.concatenate([top_half, bottom_half], axis=1)


def pixel_weights(land_mask, missing_rows, first_row, lat_total, channels):
    lat_dev = land_mask.shape[0]
    latitude = (first_row + jnp.arange(lat_dev, dtype=jnp.int32)).astype(jnp.float32)
    cos_lat = jnp.sin(math.pi * (latitude + 0.5) / lat_total)
    sea_part = (1 - land_mask).astype(jnp.float32)
    valid_part = (1 - missing_rows).astype(jnp.float32) * cos_lat[:, None]
    sea_only = (jnp.arange(channels, dtype=jnp.int32) < SEA_CH)[:, None, None]
    return jnp.where(sea_only, sea_part[None], 1.0) * valid_part[None]


def adam_step(weight, moment_one, moment_two, gradient, decay_rate):
    first_new = BETA_ONE * moment_one + (1.0 - BETA_ONE) * gradient
    second_new = BETA_TWO * moment_two + (1.0 - BETA_TWO) * gradient * gradient
    first_hat = first_new / (1.0 - BETA_ONE**STEP)
    second_hat = second_new / (1.0 - BETA_TWO**STEP)
    weight_new = weight - LEARN_RATE * (
        first_hat / (jnp.sqrt(second_hat) + EPSILON) + decay_rate * weight
    )
    return (weight_new, first_new, second_new)


def degree_coefficients(grid_field, forward, fwd_masked):
    lat_dev = grid_field.shape[0]
    embed_width = grid_field.shape[2]
    spectra = jnp.einsum("ajc,spj->aspc", grid_field, forward, precision=HIGHEST).reshape(
        lat_dev, forward.shape[0], 2 * embed_width
    )
    spectra = lax.all_to_all(spectra, "wide", split_axis=1, concat_axis=0, tiled=True)
    coeffs = jnp.einsum("sat,ask->tsk", fwd_masked, spectra, precision=HIGHEST)
    return lax.all_to_all(coeffs, "wide", split_axis=0, concat_axis=1, tiled=True)


def spectral_apply(grid_field, coef_degree, weight_block, inverse, inv_masked):
    lat_dev = grid_field.shape[0]
    embed_width = grid_field.shape[2]
    mixed_coef = jnp.einsum("tsk,tkj->tsj", coef_degree, weight_block, precision=HIGHEST)
    mixed_coef = lax.all_to_all(mixed_coef, "wide", split_axis=1, concat_axis=0, tiled=True)
    grid_coef = jnp.einsum("sta,tsk->ask", inv_masked, mixed_coef, precision=HIGHEST)
    grid_coef = lax.all_to_all(grid_coef, "wide", split_axis=0, concat_axis=1, tiled=True)
    grid_coef = grid_coef.reshape(lat_dev, inverse.shape[0], 2, embed_width)
    return jnp.einsum("aspc,spj->ajc", grid_coef, inverse, precision=HIGHEST)


def spectral_grad(field_grad, coef_degree, weight_block, forward, inverse, fwd_masked, inv_masked):
    lat_dev = field_grad.shape[0]
    embed_width = field_grad.shape[2]
    order_count = forward.shape[0]
    grid_grad = jnp.einsum("ajc,spj->aspc", field_grad, inverse, precision=HIGHEST).reshape(
        lat_dev, order_count, 2 * embed_width
    )
    grid_grad = lax.all_to_all(grid_grad, "wide", split_axis=1, concat_axis=0, tiled=True)
    mixed_grad = jnp.einsum("sta,ask->tsk", inv_masked, grid_grad, precision=HIGHEST)
    mixed_grad = lax.all_to_all(mixed_grad, "wide", split_axis=0, concat_axis=1, tiled=True)
    block_grad = jnp.einsum("tsk,tsj->tkj", coef_degree, mixed_grad, precision=HIGHEST)
    coef_grad = jnp.einsum("tsj,tkj->tsk", mixed_grad, weight_block, precision=HIGHEST)
    coef_grad = lax.all_to_all(coef_grad, "wide", split_axis=1, concat_axis=0, tiled=True)
    spectra_grad = jnp.einsum("sat,tsk->ask", fwd_masked, coef_grad, precision=HIGHEST)
    spectra_grad = lax.all_to_all(spectra_grad, "wide", split_axis=0, concat_axis=1, tiled=True)
    spectra_grad = spectra_grad.reshape(lat_dev, order_count, 2, embed_width)
    input_grad = jnp.einsum("aspc,spj->ajc", spectra_grad, forward, precision=HIGHEST)
    real_grad = (
        block_grad[:, :embed_width, :embed_width] + block_grad[:, embed_width:, embed_width:]
    )
    imag_grad = (
        block_grad[:, :embed_width, embed_width:] - block_grad[:, embed_width:, :embed_width]
    )
    return (input_grad, jnp.stack([real_grad, imag_grad], axis=1))


def body(
    inputs,
    targets,
    land_mask,
    missing_mask,
    order_map,
    degree_map,
    forward_table,
    inverse_table,
    spectral_weight,
    spectral_first,
    spectral_second,
    io_weight,
    io_first,
    io_second,
    mlp_weight,
    mlp_first,
    mlp_second,
    biases,
    bias_first,
    bias_second,
):
    fields = inputs[0]
    truth = targets[0]
    lat_dev = fields.shape[1]
    lon_count = fields.shape[2]
    channels = io_weight.shape[1]
    embed_width = io_weight.shape[2]
    hidden_units = mlp_weight.shape[2]
    wide_count = lax.axis_size("wide")
    position = lax.axis_index("wide")
    order_slots = forward_table.shape[0]
    my_orders = lax.dynamic_slice_in_dim(order_map, position * order_slots, order_slots)
    triangle = triangle_mask(my_orders, degree_map)
    fwd_masked = forward_table * triangle[:, None, :]
    inv_masked = inverse_table * triangle[:, :, None]
    forward, inverse = dft_tables(order_map, lon_count)
    pixel_weight = pixel_weights(
        land_mask, missing_mask[0], position * lat_dev, lat_dev * wide_count, channels
    )
    count_local = jnp.sum(pixel_weight)
    valid_weight = lax.psum(count_local, ("dp", "wide"))
    loss_scale = 1.0 / valid_weight
    enc_bias = biases[:embed_width]
    hidden_bias = biases[embed_width : embed_width + hidden_units]
    mlp_bias = biases[embed_width + hidden_units : 2 * embed_width + hidden_units]
    out_bias = biases[2 * embed_width + hidden_units :]
    weight_block = complex_block(spectral_weight)
    encoded = jnp.einsum("caj,ck->ajk", fields, io_weight[0], precision=HIGHEST) + enc_bias
    coef_degree = degree_coefficients(encoded, forward, fwd_masked)
    mixed_in = encoded + spectral_apply(encoded, coef_degree, weight_block, inverse, inv_masked)
    hidden_pre = jnp.einsum("ajk,kh->ajh", mixed_in, mlp_weight[0], precision=HIGHEST) + hidden_bias
    hidden_act, smooth_back = jax.vjp(smooth, hidden_pre)
    latent = (
        mixed_in
        + jnp.einsum("ajh,kh->ajk", hidden_act, mlp_weight[1], precision=HIGHEST)
        + mlp_bias
    )
    predicted = (
        jnp.einsum("ajk,ck->caj", latent, io_weight[1], precision=HIGHEST) + out_bias[:, None, None]
    )
    misfit = predicted - truth
    loss_local = jnp.sum(pixel_weight * misfit * misfit)
    pred_grad = 2.0 * pixel_weight * misfit * loss_scale
    out_bias_grad = jnp.sum(pred_grad, axis=(1, 2))
    decoder_grad = jnp.einsum("caj,ajk->ck", pred_grad, latent, precision=HIGHEST)
    latent_grad = jnp.einsum("caj,ck->ajk", pred_grad, io_weight[1], precision=HIGHEST)
    mlp_bias_grad = jnp.sum(latent_grad, axis=(0, 1))
    down_grad = jnp.einsum("ajk,ajh->kh", latent_grad, hidden_act, precision=HIGHEST)
    act_grad = jnp.einsum("ajk,kh->ajh", latent_grad, mlp_weight[1], precision=HIGHEST)
    pre_grad = smooth_back(act_grad)[0]
    hidden_bias_grad = jnp.sum(pre_grad, axis=(0, 1))
    up_grad = jnp.einsum("ajk,ajh->kh", mixed_in, pre_grad, precision=HIGHEST)
    mixed_grad = latent_grad + jnp.einsum("ajh,kh->ajk", pre_grad, mlp_weight[0], precision=HIGHEST)
    coef_again = degree_coefficients(lax.optimization_barrier(encoded), forward, fwd_masked)
    spectral_back, spectral_local = spectral_grad(
        mixed_grad, coef_again, weight_block, forward, inverse, fwd_masked, inv_masked
    )
    encoded_grad = mixed_grad + spectral_back
    enc_bias_grad = jnp.sum(encoded_grad, axis=(0, 1))
    encoder_grad = jnp.einsum("caj,ajk->ck", fields, encoded_grad, precision=HIGHEST)
    io_grad = jnp.stack([encoder_grad, decoder_grad])
    mlp_grad = jnp.stack([up_grad, down_grad])
    bias_grad = jnp.concatenate([enc_bias_grad, hidden_bias_grad, mlp_bias_grad, out_bias_grad])
    io_grad, mlp_grad, bias_grad, loss_sum = lax.psum(
        (io_grad, mlp_grad, bias_grad, loss_local), ("dp", "wide")
    )
    spectral_total = lax.psum(spectral_local, "dp")
    spectral_squares = lax.psum(jnp.sum(spectral_total * spectral_total), "wide")
    squares = (
        spectral_squares
        + jnp.sum(io_grad * io_grad)
        + jnp.sum(mlp_grad * mlp_grad)
        + jnp.sum(bias_grad * bias_grad)
    )
    grad_norm = jnp.sqrt(squares)
    factor = CLIP_LIMIT / jnp.maximum(grad_norm, CLIP_LIMIT)
    spectral_new, spectral_first_new, spectral_second_new = adam_step(
        spectral_weight, spectral_first, spectral_second, spectral_total * factor, WEIGHT_DECAY
    )
    io_new, io_first_new, io_second_new = adam_step(
        io_weight, io_first, io_second, io_grad * factor, WEIGHT_DECAY
    )
    mlp_new, mlp_first_new, mlp_second_new = adam_step(
        mlp_weight, mlp_first, mlp_second, mlp_grad * factor, WEIGHT_DECAY
    )
    bias_new, bias_first_new, bias_second_new = adam_step(
        biases, bias_first, bias_second, bias_grad * factor, 0.0
    )
    return (
        loss_sum,
        valid_weight,
        grad_norm,
        spectral_new,
        spectral_first_new,
        spectral_second_new,
        spectral_new.astype(jnp.bfloat16),
        io_new,
        io_first_new,
        io_second_new,
        io_new.astype(jnp.bfloat16),
        mlp_new,
        mlp_first_new,
        mlp_second_new,
        mlp_new.astype(jnp.bfloat16),
        bias_new,
        bias_first_new,
        bias_second_new,
        bias_new.astype(jnp.bfloat16),
    )


def solution(mesh):
    in_specs = (
        P("dp", None, "wide", None),
        P("dp", None, "wide", None),
        P("wide", None),
        P("dp", "wide", None),
        P(),
        P(),
        P("wide", None, None),
        P("wide", None, None),
        P("wide", None, None, None),
        P("wide", None, None, None),
        P("wide", None, None, None),
        P(),
        P(),
        P(),
        P(),
        P(),
        P(),
        P(),
        P(),
        P(),
    )
    out_specs = (
        P(),
        P(),
        P(),
        P("wide", None, None, None),
        P("wide", None, None, None),
        P("wide", None, None, None),
        P("wide", None, None, None),
        P(),
        P(),
        P(),
        P(),
        P(),
        P(),
        P(),
        P(),
        P(),
        P(),
        P(),
        P(),
    )
    return jax.shard_map(body, mesh=mesh, in_specs=in_specs, out_specs=out_specs, check_vma=False)
```

profile of v0, /device:TPU:0, one launch (start us, length us, event | category | flops | bytes accessed | tf_op | source)
XLA Modules:
  0.0 5069.3 jit_solution(7369075870740293918)
XLA Ops:
  53.2 66.5 %all-to-all-done = f32[4,360,512]{2,0,1:T(4,128)S(1)} async-done(((f32[4,360,512]{2,0,1:T(4,128)}), f32[4,360,512]{2,0,1:T(4,128)S(1)}, u32[]{:S(2)}, u32[]{:S(2)}) %all-to-all-start) | async-done | bytes 2949152 | tf_op jit(solution)/shard_map/all_to_all | solution.py:82
  130.4 27.7 convolution_bitcast_fusion.2
  158.0 40.3 copy.117
  233.5 734.7 %all-to-all-done.1 = f32[360,45,512]{2,1,0:T(8,128)} async-done(((f32[360,45,512]{2,1,0:T(8,128)}), f32[360,45,512]{2,1,0:T(8,128)}, u32[]{:S(2)}, u32[]{:S(2)}) %all-to-all-start.1) | async-done | bytes 33177632 | tf_op jit(solution)/shard_map/all_to_all | solution.py:84
  968.2 27.5 copy.119
  995.7 31.7 all_to_all.133
  1027.4 62.0 %fusion.1 = f32[45,360,512]{2,1,0:T(8,128)} fusion(f32[45,360,512]{2,1,0:T(8,128)} %all_to_all.133, f32[45,256,256]{2,1,0:T(8,128)} %get-tuple-element.103, f32[45,256,256]{2,1,0:T(8,128)} %fusion.126, f32[45,256,256]{2,1,0:T(8,128)} %get-tuple-element.102), kind=kOutput, calls=%fused_computation.3 | convolution fusion | flops 50996183040 | bytes 101744640 | tf_op jit(solution)/shard_map/tsk,tkj->tsj/dot_general | solution.py:90
  1089.3 37.4 copy.122
  1126.8 768.7 %all_to_all.174 = f32[45,360,512]{2,0,1:T(8,128)} all-to-all(f32[45,360,512]{2,0,1:T(8,128)S(1)} %copy.122), channel_id=1, replica_groups=mesh['dp'=4,'wide'=8] {'wide'}, dimensions={1} | all-to-all | bytes 66355200 | tf_op jit(solution)/shard_map/all_to_all | solution.py:91
  1923.0 31.8 all_to_all.137
  1986.1 90.6 %psum.50 = f32[]{:T(128)} all-reduce(f32[]{:T(128)} %fusion.91), channel_id=1, replica_groups=mesh['dp'=4,'wide'=8] {'dp','wide'}, use_global_device_ids=true, to_apply=%region_3.4 | all-reduce | flops 1 | bytes 8 | tf_op jit(solution)/shard_map/psum | solution.py:165
  2176.2 52.1 %all-to-all-done.6 = f32[4,360,512]{2,0,1:T(4,128)} async-done(((f32[4,360,512]{2,0,1:T(4,128)}), f32[4,360,512]{2,0,1:T(4,128)}, u32[]{:S(2)}, u32[]{:S(2)}) %all-to-all-start.6) | async-done | bytes 2949152 | tf_op jit(solution)/shard_map/all_to_all | solution.py:105
  2242.1 27.7 convolution_bitcast_fusion
  2269.7 40.2 copy.140
  2326.4 27.6 convolution_bitcast_fusion.1
  2354.0 40.1 copy.134
  2394.1 685.7 %all-to-all-done.7 = f32[360,45,512]{2,1,0:T(8,128)} async-done(((f32[360,45,512]{2,1,0:T(8,128)}), f32[360,45,512]{2,1,0:T(8,128)}, u32[]{:S(2)}, u32[]{:S(2)}) %all-to-all-start.7) | async-done | bytes 33177632 | tf_op jit(solution)/shard_map/all_to_all | solution.py:107
  3087.1 27.5 copy.142
  3114.6 31.7 all_to_all.156
  3146.3 61.9 %fusion = f32[45,360,512]{2,1,0:T(8,128)} fusion(f32[45,360,512]{2,1,0:T(8,128)} %all_to_all.156, f32[45,256,256]{2,1,0:T(8,128)} %get-tuple-element.103, f32[45,256,256]{2,1,0:T(8,128)} %fusion.126, f32[45,256,256]{2,1,0:T(8,128)} %get-tuple-element.102), kind=kOutput, calls=%fused_computation.2 | convolution fusion | flops 50996183040 | bytes 101744640 | tf_op jit(solution)/shard_map/tsj,tkj->tsk/dot_general | solution.py:109
  3208.1 39.4 copy.143
  3247.6 602.0 %all-to-all-done.5 = f32[360,45,512]{2,1,0:T(8,128)} async-done(((f32[360,45,512]{2,1,0:T(8,128)}), f32[360,45,512]{2,1,0:T(8,128)}, u32[]{:S(2)}, u32[]{:S(2)}) %all-to-all-start.5) | async-done | bytes 33177632 | tf_op jit(solution)/shard_map/all_to_all | solution.py:84
  3856.9 27.9 copy.136
  3884.8 31.7 all_to_all.148
  3916.5 81.9 %fusion.141 = f32[45,512,512]{2,1,0:T(8,128)} fusion(f32[45,360,512]{2,1,0:T(8,128)} %all_to_all.148, f32[45,360,512]{2,1,0:T(8,128)} %all_to_all.156), kind=kOutput, calls=%fused_computation.172 | convolution fusion | flops 50960793600 | bytes 113541120 | tf_op jit(solution)/shard_map/tsk,tsj->tkj/dot_general | solution.py:108
  4040.6 578.8 %all-to-all-done.8 = f32[45,360,512]{2,0,1:T(8,128)} async-done(((f32[45,360,512]{2,0,1:T(8,128)}), f32[45,360,512]{2,0,1:T(8,128)}, u32[]{:S(2)}, u32[]{:S(2)}) %all-to-all-start.8) | async-done | bytes 33177632 | tf_op jit(solution)/shard_map/all_to_all | solution.py:110
  4619.4 27.5 copy.145
  4646.9 31.8 all_to_all.160
  4739.9 41.5 all-to-all-done.9
  4833.7 38.2 all-reduce
  4872.5 63.9 %all-reduce.7.cloned.1.call-done = (f32[2,73,256]{2,1,0:T(8,128)}, f32[2,256,512]{2,1,0:T(8,128)}) async-done(((f32[2,73,256]{2,1,0:T(8,128)}, f32[2,256,512]{2,1,0:T(8,128)}), (f32[2,73,256]{2,1,0:T(8,128)}, f32[2,256,512]{2,1,0:T(8,128)})) %all-reduce.7.cloned.1.call-update) | async-done | bytes 1198096 | tf_op jit(solution)/shard_map/psum | solution.py:208
  4946.9 56.6 %fusion.134 = (bf16[45,2,256,256]{3,2,0,1:T(8,128)(2,1)}, f32[45,2,256,256]{3,2,0,1:T(8,128)}, f32[45,2,256,256]{3,2,0,1:T(8,128)}, f32[45,2,256,256]{3,2,0,1:T(8,128)}) fusion(f32[45,2,256,256]{3,2,1,0:T(8,128)} %param.28, f32[45,2,256,256]{3,2,0,1:T(8,128)} %all-reduce.5.cloned.1.call-done, f32[]{:T(128)S(6)} %div.82, f32[45,2,256,256]{3,2,1,0:T(8,128)} %param.29, ...), kind=kLoop, calls=%fused_computation.167 | loop fusion | flops 100270080 | bytes 176947200 | tf_op jit(solution)/shard_map/convert_element_type | solution.py:240
  (228 shorter events, 514.9 us)
Async XLA Ops:
  46.0 73.7 %all-to-all-start = ((f32[4,360,512]{2,0,1:T(4,128)}), f32[4,360,512]{2,0,1:T(4,128)S(1)}, u32[]{:S(2)}, u32[]{:S(2)}) async-start(f32[4,360,512]{2,0,1:T(4,128)} %reshape.279), calls=%async_computation | async-start | bytes 5898240 | tf_op jit(solution)/shard_map/all_to_all | solution.py:82
  53.2 104.8 %copy-start.26 = (f32[45,360]{1,0:T(8,128)}, f32[45,360]{1,0:T(8,128)S(1)}, u32[]{:S(2)}) copy-start(f32[45,360]{1,0:T(8,128)S(1)} %and_convert_fusion) | copy-start | bytes 194404
  198.3 769.8 %all-to-all-start.1 = ((f32[360,45,512]{2,1,0:T(8,128)}), f32[360,45,512]{2,1,0:T(8,128)}, u32[]{:S(2)}, u32[]{:S(2)}) async-start(f32[360,45,512]{2,1,0:T(8,128)} %copy.117), calls=%async_computation.1 | async-start | bytes 70778880 | tf_op jit(solution)/shard_map/all_to_all | solution.py:84
  1923.0 31.8 copy-start.16
  1923.0 31.8 copy-start.27
  1978.0 98.8 %copy-start.46 = (f32[1097]{0:T(1024)S(1)}, f32[1097]{0:T(1024)}, u32[]{:S(2)}) copy-start(f32[1097]{0:T(1024)} %param.37) | copy-start | bytes 13168
  1978.0 99.5 %copy-start.50 = (s32[360]{0:T(512)S(1)}, s32[360]{0:T(512)}, u32[]{:S(2)}) copy-start(s32[360]{0:T(512)} %param.24) | copy-start | bytes 4324
  1981.4 96.2 %all-to-all-start.3 = ((f32[32,45,512]{2,1,0:T(8,128)}), f32[32,45,512]{2,1,0:T(8,128)S(1)}, u32[]{:S(2)}, u32[]{:S(2)}) async-start(f32[32,45,512]{2,1,0:T(8,128)} %copy.125), calls=%async_computation.3 | async-start | bytes 6291456 | tf_op jit(solution)/shard_map/all_to_all | solution.py:93
  1985.0 131.2 %copy-start.51 = (pred[73]{0:T(512)(128)(4,1)}, pred[73]{0:T(512)(128)(4,1)S(1)}, u32[]{:S(2)}) copy-start(pred[73]{0:T(512)(128)(4,1)S(1)} %iota_compare_fusion) | copy-start | bytes 223
  1985.1 131.1 %copy-start.40 = (f32[4,720]{1,0:T(4,128)}, f32[4,720]{1,0:T(4,128)S(1)}, u32[]{:S(2)}) copy-start(f32[4,720]{1,0:T(4,128)S(1)} %subtract_convert_fusion) | copy-start | bytes 34564
  1985.2 131.0 %copy-start.42 = (f32[4,720]{1,0:T(4,128)}, f32[4,720]{1,0:T(4,128)S(1)}, u32[]{:S(2)}) copy-start(f32[4,720]{1,0:T(4,128)S(1)} %multiply_bitcast_fusion) | copy-start | bytes 34564
  2076.8 42.8 copy-start.59
  2156.6 71.8 %all-to-all-start.6 = ((f32[4,360,512]{2,0,1:T(4,128)}), f32[4,360,512]{2,0,1:T(4,128)}, u32[]{:S(2)}, u32[]{:S(2)}) async-start(f32[4,360,512]{2,0,1:T(4,128)} %reshape.281), calls=%async_computation.6 | async-start | bytes 5898240 | tf_op jit(solution)/shard_map/all_to_all | solution.py:105
  2228.3 81.6 %all-to-all-start.4 = ((f32[4,360,512]{2,0,1:T(4,128)}), f32[4,360,512]{2,0,1:T(4,128)}, u32[]{:S(2)}, u32[]{:S(2)}) async-start(f32[4,360,512]{2,0,1:T(4,128)} %reshape.280), calls=%async_computation.4 | async-start | bytes 5898240 | tf_op jit(solution)/shard_map/all_to_all | solution.py:82
  2310.0 769.8 %all-to-all-start.7 = ((f32[360,45,512]{2,1,0:T(8,128)}), f32[360,45,512]{2,1,0:T(8,128)}, u32[]{:S(2)}, u32[]{:S(2)}) async-start(f32[360,45,512]{2,1,0:T(8,128)} %copy.140), calls=%async_computation.7 | async-start | bytes 70778880 | tf_op jit(solution)/shard_map/all_to_all | solution.py:107
  3079.8 769.8 %all-to-all-start.5 = ((f32[360,45,512]{2,1,0:T(8,128)}), f32[360,45,512]{2,1,0:T(8,128)}, u32[]{:S(2)}, u32[]{:S(2)}) async-start(f32[360,45,512]{2,1,0:T(8,128)} %copy.134), calls=%async_computation.5 | async-start | bytes 70778880 | tf_op jit(solution)/shard_map/all_to_all | solution.py:84
  3849.6 769.8 %all-to-all-start.8 = ((f32[45,360,512]{2,0,1:T(8,128)}), f32[45,360,512]{2,0,1:T(8,128)}, u32[]{:S(2)}, u32[]{:S(2)}) async-start(f32[45,360,512]{2,0,1:T(8,128)} %copy.143), calls=%async_computation.8 | async-start | bytes 70778880 | tf_op jit(solution)/shard_map/all_to_all | solution.py:110
  3856.9 949.8 %all-reduce.5.cloned.1.call-start = ((), (), s32[]{:S(2)}) async-start(), calls=%async_computation.10 | async-start | bytes 47185920 | tf_op jit(solution)/shard_map/psum | solution.py:211
  4646.9 31.8 copy-start.11
  4646.9 31.8 copy-start.28
  4705.4 76.0 %all-to-all-start.9 = ((f32[32,45,512]{2,1,0:T(8,128)}), f32[32,45,512]{2,1,0:T(8,128)}, u32[]{:S(2)}, u32[]{:S(2)}) async-start(f32[32,45,512]{2,1,0:T(8,128)} %copy.146), calls=%async_computation.9 | async-start | bytes 6291456 | tf_op jit(solution)/shard_map/all_to_all | solution.py:112
  4709.9 226.5 %all-reduce.7.cloned.1.call-start = ((), (), s32[]{:S(2)}) async-start(), calls=%async_computation.11 | async-start | bytes 2424832 | tf_op jit(solution)/shard_map/psum | solution.py:208
  4806.6 27.1 copy-start.56
  4806.6 27.1 copy-start.57
  4806.6 27.1 copy-start.58
  4806.6 136.1 %copy-start.39 = (f32[2,73,256]{2,0,1:T(2,128)S(1)}, f32[2,73,256]{2,0,1:T(2,128)}, u32[]{:S(2)}) copy-start(f32[2,73,256]{2,0,1:T(2,128)} %param.31) | copy-start | bytes 448516
  4806.7 136.1 %copy-start.44 = (f32[2,73,256]{2,0,1:T(2,128)S(1)}, f32[2,73,256]{2,0,1:T(2,128)}, u32[]{:S(2)}) copy-start(f32[2,73,256]{2,0,1:T(2,128)} %param.32) | copy-start | bytes 448516
  4806.7 136.1 %copy-start.45 = (f32[2,73,256]{2,0,1:T(2,128)S(1)}, f32[2,73,256]{2,0,1:T(2,128)}, u32[]{:S(2)}) copy-start(f32[2,73,256]{2,0,1:T(2,128)} %param.33) | copy-start | bytes 448516
  5019.0 30.1 slice-start
  5019.0 30.1 slice-start.1
  5019.0 30.1 slice-start.2
  5030.7 18.5 slice-start.5
  (48 other events, 451.4 us)
Sparse Core Ops, SparseCore 0:
  4040.7 418.5 all-reduce.4
  4806.7 129.6 all-reduce.6
where the time goes:
time: 5080 us; the launch traced here: 5070 us
  waiting for transfers between devices  2830 us (56%)
  blocking collectives  913 us (18%)
  local copies, waits for them, and re-layouts  657 us (13%)
  matrix products  464 us (9%)
  other arithmetic  138 us (3%)
  starting transfers between devices  52.7 us (1%)
    all_to_all x2, waiting for transfers between devices, degree_coefficients(): lax.all_to_all(coeffs, 'wide', split_axis=0, concat_axis=1, tiled=True)  1340 us
    all_to_all x1, blocking collectives, spectral_apply(): lax.all_to_all(mixed_coef, 'wide', split_axis=1, concat_axis=0, tiled=True)  769 us
    all_to_all x1, waiting for transfers between devices, spectral_grad(): lax.all_to_all(mixed_grad, 'wide', split_axis=0, concat_axis=1, tiled=True)  686 us
    all_to_all x1, waiting for transfers between devices, spectral_grad(): lax.all_to_all(coef_grad, 'wide', split_axis=1, concat_axis=0, tiled=True)  579 us
    all_to_all x4, local copies, waits for them, and re-layouts, degree_coefficients(): lax.all_to_all(coeffs, 'wide', split_axis=0, concat_axis=1, tiled=True)  119 us
  transfers between devices with their start and end apart: 11, of which 8 were waited for; matrix products, arithmetic and copies ran while one was open for 12% of the time, Pallas kernels for 0%

commit v1 on v0

v1 whole, which is shorter than its diff:
```python
import math

import jax
import jax.numpy as jnp
import numpy as np
from jax import lax
from jax.sharding import PartitionSpec as P

M = 360
L = 360
SEA_CH = 1
STEP = 5


HIGH = lax.Precision.HIGH
CLIP_LIMIT = 0.001
LEARN_RATE = 0.1
BETA_ONE = 0.9
BETA_TWO = 0.999
EPSILON = 1e-08
WEIGHT_DECAY = 0.1


def smooth(values):
    return jax.nn.gelu(values, approximate=True)


def dot(spec, left, right):
    return jnp.einsum(spec, left, right, precision=HIGH)


def dft_tables(order_count, lon_count):
    orders = np.arange(order_count, dtype=np.int64)[:, None]
    columns = np.arange(lon_count, dtype=np.int64)[None, :]
    angle = (orders * columns % lon_count) * (2.0 * math.pi / lon_count)
    both = np.stack([np.cos(angle), -np.sin(angle)], axis=1)
    factor = np.where(orders == 0, 1.0, 2.0)[:, :, None]
    return (both / lon_count).astype(np.float32), (factor * both).astype(np.float32)


def pixel_weights(land_mask, missing_rows, first_row, lat_total, channels):
    lat_dev = land_mask.shape[0]
    latitude = (first_row + jnp.arange(lat_dev, dtype=jnp.int32)).astype(jnp.float32)
    cos_lat = jnp.sin(math.pi * (latitude + 0.5) / lat_total)
    sea_part = (1 - land_mask).astype(jnp.float32)
    valid_part = (1 - missing_rows).astype(jnp.float32) * cos_lat[:, None]
    sea_only = (jnp.arange(channels, dtype=jnp.int32) < SEA_CH)[:, None, None]
    return jnp.where(sea_only, sea_part[None], 1.0) * valid_part[None]


def adam_step(weight, moment_one, moment_two, gradient, decay_rate):
    first_new = BETA_ONE * moment_one + (1.0 - BETA_ONE) * gradient
    second_new = BETA_TWO * moment_two + (1.0 - BETA_TWO) * gradient * gradient
    first_hat = first_new / (1.0 - BETA_ONE**STEP)
    second_hat = second_new / (1.0 - BETA_TWO**STEP)
    weight_new = weight - LEARN_RATE * (
        first_hat / (jnp.sqrt(second_hat) + EPSILON) + decay_rate * weight
    )
    return (weight_new, first_new, second_new)


def body(
    inputs,
    targets,
    land_mask,
    missing_mask,
    order_map,
    degree_map,
    forward_table,
    inverse_table,
    spectral_weight,
    spectral_first,
    spectral_second,
    io_weight,
    io_first,
    io_second,
    mlp_weight,
    mlp_first,
    mlp_second,
    biases,
    bias_first,
    bias_second,
):
    fields = inputs[0]
    truth = targets[0]
    lat_dev = fields.shape[1]
    lon_count = fields.shape[2]
    channels = io_weight.shape[1]
    width = io_weight.shape[2]
    hidden_units = mlp_weight.shape[2]
    wide_count = lax.axis_size("wide")
    position = lax.axis_index("wide")
    order_count = order_map.shape[0]
    degree_slots = spectral_weight.shape[0]
    lat_total = lat_dev * wide_count
    entries = lax.axis_size("dp") * channels * lat_total * lon_count
    forward, inverse = dft_tables(order_count, lon_count)

    enc_bias = biases[:width]
    hidden_bias = biases[width : width + hidden_units]
    mlp_bias = biases[width + hidden_units : 2 * width + hidden_units]
    out_bias = biases[2 * width + hidden_units :]
    encoder = jnp.concatenate([io_weight[0], enc_bias[None]], axis=0)

    my_degrees = lax.dynamic_slice_in_dim(degree_map, position * degree_slots, degree_slots)
    slot_of = jnp.argsort(order_map)
    fwd_table = lax.all_to_all(forward_table, "wide", split_axis=2, concat_axis=0, tiled=True)
    inv_table = lax.all_to_all(inverse_table, "wide", split_axis=1, concat_axis=0, tiled=True)
    orders = jnp.arange(order_count, dtype=jnp.int32)
    live = (
        (my_degrees[None, :] >= orders[:, None]) & (orders[:, None] < M) & (my_degrees[None, :] < L)
    ).astype(jnp.float32)
    fwd_masked = fwd_table[slot_of] * live[:, None, :]
    inv_masked = inv_table[slot_of] * live[:, :, None]

    spectra = dot("caj,spj->aspc", fields, forward)
    spectra = lax.all_gather(spectra, "wide", axis=0, tiled=True)
    ones_row = jnp.asarray(forward.astype(np.float64).sum(axis=2).astype(np.float32))
    spectra = jnp.concatenate(
        [spectra, jnp.broadcast_to(ones_row[None, :, :, None], (lat_total, order_count, 2, 1))], axis=3
    )
    coeffs = dot("sat,aspc->tspc", fwd_masked, spectra)
    folded = dot("cd,tpdk->tpck", encoder, spectral_weight)
    out_re = dot("tsc,tck->tsk", coeffs[:, :, 0], folded[:, 0]) - dot(
        "tsc,tck->tsk", coeffs[:, :, 1], folded[:, 1]
    )
    out_im = dot("tsc,tck->tsk", coeffs[:, :, 0], folded[:, 1]) + dot(
        "tsc,tck->tsk", coeffs[:, :, 1], folded[:, 0]
    )
    mixed_coef = jnp.concatenate([out_re, out_im], axis=2)
    grid_coef = dot("sta,tsk->ask", inv_masked, mixed_coef)
    grid_coef = lax.psum_scatter(grid_coef, "wide", scatter_dimension=0, tiled=True)
    grid_coef = grid_coef.reshape(lat_dev, order_count, 2, width)

    encoded = dot("caj,ck->ajk", fields, io_weight[0]) + enc_bias
    mixed_in = encoded + dot("aspc,spj->ajc", grid_coef, inverse)
    hidden_pre = dot("ajk,kh->ajh", mixed_in, mlp_weight[0]) + hidden_bias
    hidden_act, smooth_back = jax.vjp(smooth, hidden_pre)
    latent = mixed_in + dot("ajh,kh->ajk", hidden_act, mlp_weight[1]) + mlp_bias
    predicted = dot("ajk,ck->caj", latent, io_weight[1]) + out_bias[:, None, None]
    misfit = predicted - truth
    pixel_weight = pixel_weights(land_mask, missing_mask[0], position * lat_dev, lat_total, channels)
    count_local = jnp.sum(pixel_weight)
    weighted = pixel_weight * misfit
    loss_local = jnp.sum(weighted * misfit)
    pred_grad = weighted * (2.0 / entries)
    out_bias_grad = jnp.sum(pred_grad, axis=(1, 2))
    decoder_grad = dot("caj,ajk->ck", pred_grad, latent)
    latent_grad = dot("caj,ck->ajk", pred_grad, io_weight[1])
    mlp_bias_grad = jnp.sum(latent_grad, axis=(0, 1))
    down_grad = dot("ajk,ajh->kh", latent_grad, hidden_act)
    act_grad = dot("ajk,kh->ajh", latent_grad, mlp_weight[1])
    pre_grad = smooth_back(act_grad)[0]
    hidden_bias_grad = jnp.sum(pre_grad, axis=(0, 1))
    up_grad = dot("ajk,ajh->kh", mixed_in, pre_grad)
    mixed_grad = latent_grad + dot("ajh,kh->ajk", pre_grad, mlp_weight[0])

    grid_grad = dot("ajc,spj->aspc", mixed_grad, inverse).reshape(lat_dev, order_count, 2 * width)
    grid_grad = lax.all_gather(grid_grad, "wide", axis=0, tiled=True)
    out_grad = dot("sta,ask->tsk", inv_masked, grid_grad)
    out_re_grad, out_im_grad = out_grad[:, :, :width], out_grad[:, :, width:]
    real_part = dot("tsc,tsk->tck", coeffs[:, :, 0], out_re_grad) + dot(
        "tsc,tsk->tck", coeffs[:, :, 1], out_im_grad
    )
    imag_part = dot("tsc,tsk->tck", coeffs[:, :, 0], out_im_grad) - dot(
        "tsc,tsk->tck", coeffs[:, :, 1], out_re_grad
    )
    thin = jnp.stack([real_part, imag_part], axis=1)
    encoder_grad = dot("tpck,tpdk->cd", thin, spectral_weight)
    direct = dot("caj,ajk->ck", fields, mixed_grad)
    direct_bias = jnp.sum(mixed_grad, axis=(0, 1))
    encoder_grad = encoder_grad + jnp.concatenate([direct, direct_bias[None]], axis=0)
    io_grad = jnp.stack([encoder_grad[:channels], decoder_grad])
    mlp_grad = jnp.stack([up_grad, down_grad])
    bias_grad = jnp.concatenate(
        [encoder_grad[channels], hidden_bias_grad, mlp_bias_grad, out_bias_grad]
    )
    io_grad, mlp_grad, bias_grad, loss_sum, valid_weight = lax.psum(
        (io_grad, mlp_grad, bias_grad, loss_local, count_local), ("dp", "wide")
    )
    thin = lax.psum(thin, "dp")
    gram = jnp.einsum("ck,dk->cd", encoder, encoder, precision=lax.Precision.HIGHEST)
    spectral_squares = jnp.sum(thin * jnp.einsum("cd,tpdk->tpck", gram, thin, precision=lax.Precision.HIGHEST))
    spectral_squares = lax.psum(spectral_squares, "wide")
    rescale = entries / valid_weight
    squares = (
        spectral_squares
        + jnp.sum(io_grad * io_grad)
        + jnp.sum(mlp_grad * mlp_grad)
        + jnp.sum(bias_grad * bias_grad)
    )
    grad_norm = jnp.sqrt(squares) * rescale
    factor = rescale * CLIP_LIMIT / jnp.maximum(grad_norm, CLIP_LIMIT)
    spectral_total = dot("cd,tpck->tpdk", encoder, thin)
    spectral_new, spectral_first_new, spectral_second_new = adam_step(
        spectral_weight, spectral_first, spectral_second, spectral_total * factor, WEIGHT_DECAY
    )
    io_new, io_first_new, io_second_new = adam_step(
        io_weight, io_first, io_second, io_grad * factor, WEIGHT_DECAY
    )
    mlp_new, mlp_first_new, mlp_second_new = adam_step(
        mlp_weight, mlp_first, mlp_second, mlp_grad * factor, WEIGHT_DECAY
    )
    bias_new, bias_first_new, bias_second_new = adam_step(
        biases, bias_first, bias_second, bias_grad * factor, 0.0
    )
    return (
        loss_sum,
        valid_weight,
        grad_norm,
        spectral_new,
        spectral_first_new,
        spectral_second_new,
        spectral_new.astype(jnp.bfloat16),
        io_new,
        io_first_new,
        io_second_new,
        io_new.astype(jnp.bfloat16),
        mlp_new,
        mlp_first_new,
        mlp_second_new,
        mlp_new.astype(jnp.bfloat16),
        bias_new,
        bias_first_new,
        bias_second_new,
        bias_new.astype(jnp.bfloat16),
    )


def solution(mesh):
    wide4 = P("wide", None, None, None)
    in_specs = (
        P("dp", None, "wide", None),
        P("dp", None, "wide", None),
        P("wide", None),
        P("dp", "wide", None),
        P(),
        P(),
        P("wide", None, None),
        P("wide", None, None),
        wide4,
        wide4,
        wide4,
    ) + (P(),) * 9
    out_specs = (P(),) * 3 + (wide4,) * 4 + (P(),) * 12
    return jax.shard_map(body, mesh=mesh, in_specs=in_specs, out_specs=out_specs, check_vma=False)
```

time: 5080 us -> 1610 us (0.32)
  waiting for transfers between devices: 2830 us -> 663 us
  blocking collectives: 913 us -> 55.9 us
  local copies, waits for them, and re-layouts: 657 us -> 345 us
  other arithmetic: 138 us -> 69.5 us
    all_to_all x9 -> x2, waiting for transfers between devices: 2760 us -> 80.4 us  [the longest x1 80.4 us: body(): lax.all_to_all(forward_table, 'wide', split_axis=2, concat_axis=0, tiled=...]
    all_to_all x1 -> x0, blocking collectives: 769 us -> none  [spectral_apply(): lax.all_to_all(mixed_coef, 'wide', split_axis=1, concat_axis=0, tiled=True)]
    all_to_all x18 -> x3, local copies, waits for them, and re-layouts: 335 us -> 18.6 us  [the longest x2 9.66 us: body(): lax.all_to_all(forward_table, 'wide', split_axis=2, concat_axis=0, tiled=...]
    reduce_scatter x0 -> x1, waiting for transfers between devices: none -> 230 us  [body(): lax.psum_scatter(grid_coef, 'wide', scatter_dimension=0, tiled=True)]
    all_gather x0 -> x2, waiting for transfers between devices: none -> 185 us  [the longest x1 185 us: body(): grid_grad = lax.all_gather(grid_grad, 'wide', axis=0, tiled=True)]
    unnamed x145 -> x108, local copies, waits for them, and re-layouts: 65.1 us -> 222 us
    transpose x5 -> x1, local copies, waits for them, and re-layouts: 127 us -> 23.6 us  [dot(): return jnp.einsum(spec, left, right, precision=HIGH)]
    psum x2, waiting for transfers between devices: 63.9 us -> 167 us  [the longest x1 158 us: body(): thin = lax.psum(thin, 'dp')]
  transfers between devices with their start and end apart: 11 -> 7, of which waited for: 8 -> 5; matrix products, arithmetic and copies ran while one was open for 12% -> 14% of each run, Pallas kernels for 0% -> 0%
where the time goes in v1:
time: 1610 us; the launch traced here: 1600 us
  waiting for transfers between devices  663 us (41%)
  matrix products  438 us (27%)
  local copies, waits for them, and re-layouts  345 us (21%)
  other arithmetic  69.5 us (4%)
  blocking collectives  55.9 us (3%)
  between operations  19.1 us (1%)
    dot_general x28, matrix products, dot(): return jnp.einsum(spec, left, right, precision=HIGH)  426 us
    reduce_scatter x1, waiting for transfers between devices, body(): lax.psum_scatter(grid_coef, 'wide', scatter_dimension=0, tiled=True)  230 us
    unnamed x108, local copies, waits for them, and re-layouts  222 us
    all_gather x1, waiting for transfers between devices, body(): grid_grad = lax.all_gather(grid_grad, 'wide', axis=0, tiled=True)  185 us
    psum x1, waiting for transfers between devices, body(): thin = lax.psum(thin, 'dp')  158 us
    all_to_all x1, waiting for transfers between devices, body(): lax.all_to_all(forward_table, 'wide', split_axis=2, concat_axis=0, tiled=...  80.4 us
    psum x1, blocking collectives, body(): lax.psum((io_grad, mlp_grad, bias_grad, loss_local, count_local), ('dp',...  38.7 us
  transfers between devices with their start and end apart: 7, of which 5 were waited for; matrix products, arithmetic and copies ran while one was open for 14% of the time, Pallas kernels for 0%

profile of v1, /device:TPU:0, one launch (start us, length us, event | category | flops | bytes accessed | tf_op | source)
XLA Modules:
  0.0 1601.3 jit_solution(14293623971887134742)
XLA Ops:
  50.6 80.4 %all-to-all-done = f32[8,1,64800]{2,1,0:T(1,128)S(1)} async-done(((f32[8,1,64800]{2,1,0:T(1,128)}), f32[8,1,64800]{2,1,0:T(1,128)S(1)}, u32[]{:S(2)}, u32[]{:S(2)}) %all-to-all-start) | async-done | bytes 2073632 | tf_op jit(solution)/shard_map/all_to_all | solution.py:107
  140.7 15.0 convolution_bitcast_fusion.1
  163.8 12.0 reshape.200
  241.9 15.3 convolution_bitcast_fusion
  257.2 12.5 slice_bitcast_fusion
  278.5 16.9 %fusion.36 = f32[45,360,256]{2,1,0:T(8,128)} fusion(f32[45,360,74]{1,2,0:T(8,128)} %copy.222, f32[45,2,74,256]{3,2,1,0:T(8,128)} %convolution_bitcast_fusion.1), kind=kOutput, calls=%fused_computation.53 | convolution fusion | flops 1841356800 | bytes 25804800 | tf_op jit(solution)/shard_map/tsc,tck->tsk/dot_general | solution.py:29
  314.2 21.9 %convolution_add_fusion = f32[45,360,256]{2,1,0:T(8,128)} fusion(f32[45,360,256]{2,1,0:T(8,128)} %fusion.36, f32[45,360,74]{1,2,0:T(8,128)} %copy.223, f32[45,2,74,256]{3,2,1,0:T(8,128)} %convolution_bitcast_fusion.1), kind=kOutput, calls=%fused_computation.23 | convolution fusion | flops 1845504000 | bytes 42393600 | tf_op jit(solution)/shard_map/tsc,tck->tsk/dot_general | solution.py:29
  336.2 21.9 %convolution_subtract_fusion = f32[45,360,256]{2,1,0:T(8,128)} fusion(f32[45,360,256]{2,1,0:T(8,128)} %fusion.35, f32[45,360,74]{1,2,0:T(8,128)} %copy.223, f32[45,2,74,256]{3,2,1,0:T(8,128)} %convolution_bitcast_fusion.1), kind=kOutput, calls=%fused_computation.24 | convolution fusion | flops 1845504000 | bytes 42393600 | tf_op jit(solution)/shard_map/tsc,tck->tsk/dot_general | solution.py:29
  358.1 25.7 %pad_maximum_fusion = f32[45,360,512]{2,1,0:T(8,128)} fusion(f32[45,360,256]{2,1,0:T(8,128)} %convolution_add_fusion, f32[45,360,256]{2,1,0:T(8,128)} %convolution_subtract_fusion), kind=kLoop, calls=%fused_computation.5 | loop fusion | flops 8294400 | bytes 66355200 | tf_op jit(solution)/shard_map/concatenate | solution.py:130
  383.8 52.0 %fusion.19 = f32[32,360,512]{2,0,1:T(8,128)} fusion(f32[45,360,512]{2,1,0:T(8,128)} %pad_maximum_fusion, f32[360,45,32]{1,2,0:T(8,128)} %gather_fusion.1, f32[360,45]{1,0:T(8,128)S(1)} %fusion.99), kind=kOutput, calls=%fused_computation.28 | convolution fusion | flops 1593043200 | bytes 58908960 | tf_op jit(solution)/shard_map/sta,tsk->ask/dot_general | solution.py:29
  435.8 23.6 %copy.230 = f32[32,360,512]{2,1,0:T(8,128)} copy(f32[32,360,512]{2,0,1:T(8,128)} %fusion.19) | data formatting | bytes 47185920 | tf_op jit(solution)/shard_map/sta,tsk->ask/transpose | solution.py:29
  463.6 229.6 %reduce-scatter.2.cloned.1.call-done = f32[4,360,512]{2,1,0:T(8,128)} async-done(((f32[32,360,512]{2,1,0:T(8,128)}), f32[4,360,512]{2,1,0:T(8,128)}) %reduce-scatter.2.cloned.1.call-update) | async-done | bytes 2949136 | tf_op jit(solution)/shard_map/reduce_scatter | solution.py:132
  751.0 185.4 %all-gather.5.cloned.1.call-done = f32[32,360,512]{2,1,0:T(8,128)} async-done(((f32[4,360,512]{2,1,0:T(8,128)}), f32[32,360,512]{2,1,0:T(8,128)}) %all-gather.5.cloned.1.call-update) | async-done | bytes 23592976 | tf_op jit(solution)/shard_map/all_gather | solution.py:159
  936.4 41.1 %fusion.16 = f32[45,360,512]{2,0,1:T(8,128)} fusion(f32[32,360,512]{2,1,0:T(8,128)} %all-gather.5.cloned.1.call-done, f32[360,45,32]{1,2,0:T(8,128)} %gather_fusion.1, f32[360,45]{1,0:T(8,128)S(1)} %fusion.99), kind=kOutput, calls=%fused_computation.22 | convolution fusion | flops 1593043200 | bytes 58908960 | tf_op jit(solution)/shard_map/sta,ask->tsk/dot_general | solution.py:29
  977.5 24.9 %fusion.132 = (f32[45,360,256]{2,0,1:T(8,128)}, f32[45,360,256]{2,0,1:T(8,128)}) fusion(f32[45,360,512]{2,0,1:T(8,128)} %fusion.16), kind=kLoop, calls=%fused_computation.170 | loop fusion | bytes 66355200 | tf_op jit(solution)/shard_map/slice | solution.py:161
  1002.4 23.8 %fusion.8 = f32[45,74,256]{2,1,0:T(8,128)} fusion(f32[45,360,74]{1,2,0:T(8,128)} %copy.222, f32[45,360,256]{2,0,1:T(8,128)} %get-tuple-element.143), kind=kOutput, calls=%fused_computation.14 | convolution fusion | flops 1841356800 | bytes 24793920 | tf_op jit(solution)/shard_map/tsc,tsk->tck/dot_general | solution.py:29
  1026.2 24.1 %fusion.10 = f32[45,74,256]{2,1,0:T(8,128)} fusion(f32[45,360,74]{1,2,0:T(8,128)} %copy.223, f32[45,360,256]{2,0,1:T(8,128)} %get-tuple-element.143), kind=kOutput, calls=%fused_computation.16 | convolution fusion | flops 1841356800 | bytes 24793920 | tf_op jit(solution)/shard_map/tsc,tsk->tck/dot_general | solution.py:29
  1050.3 24.8 %subtract_bitcast_fusion = f32[45,1,74,256]{3,2,0,1:T(8,128)} fusion(f32[45,74,256]{2,1,0:T(8,128)} %fusion.8, f32[45,360,74]{1,2,0:T(8,128)} %copy.223, f32[45,360,256]{2,0,1:T(8,128)} %get-tuple-element.142), kind=kOutput, calls=%fused_computation.50 | convolution fusion | flops 1842209280 | bytes 28203840 | tf_op jit(solution)/shard_map/tsc,tsk->tck/dot_general | solution.py:29
  1075.2 24.8 %add_bitcast_fusion = f32[45,1,74,256]{3,2,0,1:T(8,128)} fusion(f32[45,74,256]{2,1,0:T(8,128)} %fusion.10, f32[45,360,74]{1,2,0:T(8,128)} %copy.222, f32[45,360,256]{2,0,1:T(8,128)} %get-tuple-element.142), kind=kOutput, calls=%fused_computation.51 | convolution fusion | flops 1842209280 | bytes 28203840 | tf_op jit(solution)/shard_map/tsc,tsk->tck/dot_general | solution.py:29
  1100.0 17.0 %fusion.62 = f32[74,256]{1,0:T(8,128)S(1)} fusion(f32[45,2,256,256]{3,2,1,0:T(8,128)} %param.32, f32[1,256]{1,0:T(1,128)S(1)} %bitcast.202, f32[73,256]{1,0:T(8,128)S(1)} %convolution_bitcast_fusion.5, f32[45,1,74,256]{3,2,0,1:T(8,128)} %subtract_bitcast_fusion, f32[45,1,74,256]{3,2,0,1:T(8,128)} %add_bitcast_fusion), kind=kOutput, calls=%fused_computation.79 | convolution fusion | flops 2620561408 | bytes 30564352 | tf_op jit(solution)/shard_map/tpck,tpdk->cd/dot_general | solution.py:29
  1124.5 24.2 %copy.251 = f32[45,2,256,256]{2,3,1,0:T(8,128)} copy(f32[45,2,256,256]{3,2,1,0:T(8,128)} %param.32) | data formatting | bytes 47185920 | tf_op args[8]
  1148.7 24.2 %copy.247 = f32[45,2,256,256]{2,3,1,0:T(8,128)} copy(f32[45,2,256,256]{3,2,1,0:T(8,128)} %param.33) | data formatting | bytes 47185920 | tf_op args[9]
  1172.9 24.3 %copy.249 = f32[45,2,256,256]{2,3,1,0:T(8,128)} copy(f32[45,2,256,256]{3,2,1,0:T(8,128)} %param.34) | data formatting | bytes 47185920 | tf_op args[10]
  1197.5 38.7 %all-reduce = (f32[]{:T(128)}, f32[]{:T(128)}, f32[1097]{0:T(1024)S(1)}) all-reduce(f32[]{:T(128)} %get-tuple-element.117, f32[]{:T(128)} %get-tuple-element.118, f32[1097]{0:T(1024)S(1)} %pad_maximum_fusion.9), channel_id=1, replica_groups=mesh['dp'=4,'wide'=8] {'dp','wide'}, use_global_device_ids=true, to_apply=%region_3.4 | all-reduce | flops 1099 | bytes 8792 | tf_op jit(solution)/shard_map/psum | solution.py:178
  1248.8 158.1 %all-reduce.5.cloned.1.call-done = f32[45,2,74,256]{3,2,0,1:T(8,128)} async-done(((f32[45,2,74,256]{3,2,0,1:T(8,128)}), f32[45,2,74,256]{3,2,0,1:T(8,128)}) %all-reduce.5.cloned.1.call-update) | async-done | bytes 6819856 | tf_op jit(solution)/shard_map/psum | solution.py:181
  1407.0 11.9 fusion.22
  1419.5 17.1 %psum.52 = f32[]{:T(128)} all-reduce(f32[]{:T(128)} %fusion.22), channel_id=1, replica_groups=mesh['dp'=4,'wide'=8] {'wide'}, use_global_device_ids=true, to_apply=%region_8.9 | all-reduce | flops 1 | bytes 8 | tf_op jit(solution)/shard_map/psum | solution.py:184
  1439.4 56.7 %fusion.129 = (bf16[45,2,256,256]{2,3,1,0:T(8,128)(2,1)}, f32[45,2,256,256]{2,3,1,0:T(8,128)}, f32[45,2,256,256]{2,3,1,0:T(8,128)}, f32[45,2,256,256]{2,3,1,0:T(8,128)}) fusion(f32[45,2,256,256]{2,3,1,0:T(8,128)} %copy.251, f32[]{:T(128)S(6)} %div.74, f32[45,2,256,256]{2,3,1,0:T(8,128)} %copy.247, f32[45,2,256,256]{2,3,1,0:T(8,128)} %copy.249, ...), kind=kOutput, calls=%fused_computation.169 | convolution fusion | flops 2719107584 | bytes 160249856 | tf_op jit(solution)/shard_map/cd,tpck->tpdk/dot_general | solution.py:29
  1496.1 24.1 %copy.256 = f32[45,2,256,256]{3,2,1,0:T(8,128)} copy(f32[45,2,256,256]{2,3,1,0:T(8,128)} %get-tuple-element.137) | data formatting | bytes 47185920
  1520.2 24.1 %copy.257 = f32[45,2,256,256]{3,2,1,0:T(8,128)} copy(f32[45,2,256,256]{2,3,1,0:T(8,128)} %get-tuple-element.138) | data formatting | bytes 47185920
  1544.4 24.1 %copy.258 = f32[45,2,256,256]{3,2,1,0:T(8,128)} copy(f32[45,2,256,256]{2,3,1,0:T(8,128)} %get-tuple-element.139) | data formatting | bytes 47185920
  1568.5 16.4 %copy.259 = bf16[45,2,256,256]{3,2,1,0:T(8,128)(2,1)} copy(bf16[45,2,256,256]{2,3,1,0:T(8,128)(2,1)} %get-tuple-element.136) | data formatting | bytes 23592960
  (173 shorter events, 245.2 us)
Async XLA Ops:
  7.2 216.7 %all-gather.3.cloned.1.call-start = ((), (), s32[]{:S(2)}) async-start(), calls=%async_computation.3 | async-start | bytes 8847360 | tf_op jit(solution)/shard_map/all_gather | solution.py:117
  27.5 103.5 %all-to-all-start = ((f32[8,1,64800]{2,1,0:T(1,128)}), f32[8,1,64800]{2,1,0:T(1,128)S(1)}, u32[]{:S(2)}, u32[]{:S(2)}) async-start(f32[8,1,64800]{2,1,0:T(1,128)} %reshape.199), calls=%async_computation | async-start | bytes 4153344 | tf_op jit(solution)/shard_map/all_to_all | solution.py:107
  40.9 94.5 %copy-start.25 = (f32[2,73,256]{2,0,1:T(2,128)S(1)}, f32[2,73,256]{2,0,1:T(2,128)}, u32[]{:S(2)}) copy-start(f32[2,73,256]{2,0,1:T(2,128)} %param.35) | copy-start | bytes 448516
  40.9 94.6 %copy-start.41 = (s32[360]{0:T(512)S(1)}, s32[360]{0:T(512)}, u32[]{:S(2)}) copy-start(s32[360]{0:T(512)} %param.28) | copy-start | bytes 4324
  40.9 99.1 %copy-start.30 = (f32[1097]{0:T(1024)S(1)}, f32[1097]{0:T(1024)}, u32[]{:S(2)}) copy-start(f32[1097]{0:T(1024)} %param.41) | copy-start | bytes 13168
  131.0 54.0 %all-to-all-start.1 = ((f32[8,1,64800]{2,1,0:T(1,128)}), f32[8,1,64800]{2,1,0:T(1,128)}, u32[]{:S(2)}, u32[]{:S(2)}) async-start(f32[8,1,64800]{2,1,0:T(1,128)} %reshape.201), calls=%async_computation.1 | async-start | bytes 4153344 | tf_op jit(solution)/shard_map/all_to_all | solution.py:108
  135.3 557.9 %reduce-scatter.2.cloned.1.call-start = ((), (), s32[]{:S(2)}) async-start(), calls=%async_computation.4 | async-start | bytes 26542080 | tf_op jit(solution)/shard_map/reduce_scatter | solution.py:132
  135.4 20.4 %copy-start.18 = (f32[2,73,256]{2,1,0:T(8,128)}, f32[2,73,256]{2,1,0:T(8,128)S(1)}, u32[]{:S(2)}) copy-start(f32[2,73,256]{2,1,0:T(8,128)S(1)} %copy.215) | copy-start | bytes 448516
  140.6 15.2 copy-start.27
  140.6 15.2 copy-start.22
  269.7 25.7 %slice-start = ((s8[7372800]{0:T(1024)(128)(4,1)}), s8[3178496]{0:T(1024)(128)(4,1)S(1)}, s32[]{:S(2)}) async-start(s8[7372800]{0:T(1024)(128)(4,1)} %bitcast.186), calls=%async_computation.8 | async-start | bytes 6356992
  278.4 17.0 %copy-start = (f32[45,360,74]{1,2,0:T(8,128)S(1)}, f32[45,360,74]{1,2,0:T(8,128)}, u32[]{:S(2)}) copy-start(f32[45,360,74]{1,2,0:T(8,128)} %copy.222) | copy-start | bytes 14385604
  278.5 17.0 %slice-start.1 = ((s8[7372800]{0:T(1024)(128)(4,1)}), s8[4194304]{0:T(1024)(128)(4,1)S(1)}, s32[]{:S(2)}) async-start(s8[7372800]{0:T(1024)(128)(4,1)} %bitcast.186), calls=%async_computation.9 | async-start | bytes 8388608
  459.4 233.8 %copy-start.28 = (f32[256]{0:T(256)S(1)}, f32[256]{0:T(256)}, u32[]{:S(2)}) copy-start(f32[256]{0:T(256)} %copy-done.27) | copy-start | bytes 3076
  459.4 477.0 %all-gather.5.cloned.1.call-start = ((), (), s32[]{:S(2)}) async-start(), calls=%async_computation.5 | async-start | bytes 26542080 | tf_op jit(solution)/shard_map/all_gather | solution.py:159
  703.0 8.6 copy-start.12
  711.6 10.1 copy-start.4
  730.9 515.8 %all-reduce.7.cloned.1.call-start = ((), (), s32[]{:S(2)}) async-start(), calls=%async_computation.7 | async-start | bytes 2424832 | tf_op jit(solution)/shard_map/psum | solution.py:178
  738.5 9.9 copy-start.7
  738.5 9.9 copy-start.9
  1117.7 289.3 %all-reduce.5.cloned.1.call-start = ((), (), s32[]{:S(2)}) async-start(), calls=%async_computation.6 | async-start | bytes 14745600 | tf_op jit(solution)/shard_map/psum | solution.py:181
  1172.9 24.3 %copy-start.23 = (f32[73,256]{1,0:T(8,128)S(1)}, f32[73,256]{1,0:T(8,128)}, u32[]{:S(2)}) copy-start(f32[73,256]{1,0:T(8,128)} %copy-done.22) | copy-start | bytes 224260
  1172.9 24.3 %copy-start.29 = (f32[256]{0:T(256)S(1)}, f32[256]{0:T(256)}, u32[]{:S(2)}) copy-start(f32[256]{0:T(256)} %copy-done.27) | copy-start | bytes 3076
  1172.9 24.5 %copy-start.37 = (f32[256]{0:T(256)S(1)}, f32[256]{0:T(256)}, u32[]{:S(2)}) copy-start(f32[256]{0:T(256)} %get-tuple-element.149) | copy-start | bytes 3076
  1172.9 24.5 %copy-start.39 = (f32[73]{0:T(128)S(1)}, f32[73]{0:T(128)}, u32[]{:S(2)}) copy-start(f32[73]{0:T(128)} %get-tuple-element.116) | copy-start | bytes 880
  1172.9 24.6 %copy-start.40 = (f32[512]{0:T(512)S(1)}, f32[512]{0:T(512)}, u32[]{:S(2)}) copy-start(f32[512]{0:T(512)} %get-tuple-element.151) | copy-start | bytes 6148
  1246.7 172.2 %copy-start.24 = (f32[2,73,256]{2,1,0:T(8,128)S(1)}, f32[2,73,256]{2,1,0:T(8,128)}, u32[]{:S(2)}) copy-start(f32[2,73,256]{2,1,0:T(8,128)} %get-tuple-element.122) | copy-start | bytes 448516
  1568.5 16.4 %copy-start.26 = (f32[2,73,256]{2,0,1:T(2,128)S(1)}, f32[2,73,256]{2,0,1:T(2,128)}, u32[]{:S(2)}) copy-start(f32[2,73,256]{2,0,1:T(2,128)} %param.35) | copy-start | bytes 448516
  1568.5 20.6 %copy-start.14 = (f32[2,256,512]{2,1,0:T(8,128)S(1)}, f32[2,256,512]{2,1,0:T(8,128)}, u32[]{:S(2)}) copy-start(f32[2,256,512]{2,1,0:T(8,128)} %param.38) | copy-start | bytes 3145732
  1568.5 20.6 %copy-start.15 = (f32[2,256,512]{2,1,0:T(8,128)S(1)}, f32[2,256,512]{2,1,0:T(8,128)}, u32[]{:S(2)}) copy-start(f32[2,256,512]{2,1,0:T(8,128)} %get-tuple-element.123) | copy-start | bytes 3145732
  1568.5 20.6 %copy-start.21 = (f32[2,256,512]{2,1,0:T(8,128)S(1)}, f32[2,256,512]{2,1,0:T(8,128)}, u32[]{:S(2)}) copy-start(f32[2,256,512]{2,1,0:T(8,128)} %param.39) | copy-start | bytes 3145732
  1584.9 7.9 copy-start.35
  (21 other events, 80.4 us)
Sparse Core Ops, SparseCore 0:
  11.7 124.5 all-gather.2
  459.6 233.6 reduce-scatter.1
  731.1 205.3 all-gather.4
  1117.8 128.8 all-reduce.6
  1250.4 156.4 all-reduce.4

commit v2 on v1

--- a/solution.py
+++ b/solution.py
@@ -1,9 +1,12 @@
+import functools
 import math
 
 import jax
 import jax.numpy as jnp
 import numpy as np
 from jax import lax
+from jax.experimental import pallas as pl
+from jax.experimental.pallas import tpu as pltpu
 from jax.sharding import PartitionSpec as P
 
 M = 360
@@ -33,9 +36,329 @@
     orders = np.arange(order_count, dtype=np.int64)[:, None]
     columns = np.arange(lon_count, dtype=np.int64)[None, :]
     angle = (orders * columns % lon_count) * (2.0 * math.pi / lon_count)
-    both = np.stack([np.cos(angle), -np.sin(angle)], axis=1)
-    factor = np.where(orders == 0, 1.0, 2.0)[:, :, None]
+    both = np.stack([np.cos(angle), -np.sin(angle)], axis=0)
+    factor = np.where(orders == 0, 1.0, 2.0)[None]
     return (both / lon_count).astype(np.float32), (factor * both).astype(np.float32)
+
+
+def halves(value):
+    high = value.astype(jnp.bfloat16)
+    low = (value - high.astype(jnp.float32)).astype(jnp.bfloat16)
+    return high, low
+
+
+def dot3(left, right, dims=(((1,), (0,)), ((), ()))):
+    left_high, left_low = halves(left)
+    right_high, right_low = halves(right)
+
+    def one(a, b):
+        return lax.dot_general(a, b, dims, preferred_element_type=jnp.float32)
+
+    return one(left_high, right_high) + (one(left_high, right_low) + one(left_low, right_high))
+
+
+def block_diagonal(rows):
+    count, lanes = rows.shape
+    spread = jnp.broadcast_to(rows[:, None, :], (count, 8, lanes))
+    sub = lax.broadcasted_iota(jnp.int32, (count, 8, lanes), 1)
+    lane = lax.broadcasted_iota(jnp.int32, (count, 8, lanes), 2) & 7
+    return jnp.where(sub == lane, spread, 0.0).reshape(count * 8, lanes)
+
+
+def steps(count):
+    return max(size for size in range(1, 6) if count % size == 0)
+
+
+def coefficients(spec_ref, fwd_ref, coef_ref, group):
+    rows = pl.ds(pl.multiple_of(group * 8, 8), 8)
+    spectra = spec_ref[:, rows, :]
+    lat, _, thin = spectra.shape
+    product = dot3(block_diagonal(fwd_ref[group]), spectra.reshape(lat * 8, thin))
+    coef_ref[:, rows, :] = product.reshape(product.shape[0] // 8, 8, thin)
+
+
+def forward_kernel(spec_ref, fwd_ref, inv_ref, folded_ref, grid_ref, coef_ref, mixed_ref):
+    groups = fwd_ref.shape[0]
+    degrees = folded_ref.shape[0]
+    slots = mixed_ref.shape[0]
+    for spare in range(degrees, slots):
+        mixed_ref[spare] = jnp.zeros(mixed_ref.shape[1:], jnp.float32)
+
+    def analyse(group, carry):
+        coefficients(spec_ref, fwd_ref, coef_ref, group)
+        return carry
+
+    lax.fori_loop(0, groups, analyse, 0, unroll=steps(groups))
+
+    def mix(degree, carry):
+        real = folded_ref[degree, 0]
+        imag = folded_ref[degree, 1]
+        block = jnp.concatenate(
+            [jnp.concatenate([real, imag], axis=1), jnp.concatenate([-imag, real], axis=1)], axis=0
+        )
+        mixed_ref[degree] = dot3(coef_ref[degree], block)
+        return carry
+
+    lax.fori_loop(0, degrees, mix, 0, unroll=steps(degrees))
+
+    def synthesise(group, carry):
+        rows = pl.ds(pl.multiple_of(group * 8, 8), 8)
+        mixed = mixed_ref[:, rows, :]
+        product = dot3(
+            block_diagonal(inv_ref[group]),
+            mixed.reshape(slots * 8, mixed.shape[2]),
+            (((0,), (0,)), ((), ())),
+        )
+        grid_ref[:, rows, :] = product.reshape(product.shape[0] // 8, 8, mixed.shape[2])
+        return carry
+
+    lax.fori_loop(0, groups, synthesise, 0, unroll=steps(groups))
+
+
+def backward_kernel(grid_ref, spec_ref, fwd_ref, inv_ref, thin_ref, coef_ref, out_ref):
+    groups = fwd_ref.shape[0]
+    degrees, _, channels, width = thin_ref.shape
+
+    @pl.when(pl.program_id(0) == 0)
+    def _():
+        thin_ref[...] = jnp.zeros(thin_ref.shape, jnp.float32)
+
+    def analyse(group, carry):
+        coefficients(spec_ref, fwd_ref, coef_ref, group)
+        coefficients(grid_ref, inv_ref, out_ref, group)
+        return carry
+
+    lax.fori_loop(0, groups, analyse, 0, unroll=steps(groups))
+
+    def product(degree, carry):
+        both = dot3(coef_ref[degree], out_ref[degree], (((0,), (0,)), ((), ())))
+        thin_ref[degree, 0] += both[:channels, :width] + both[channels:, width:]
+        thin_ref[degree, 1] += both[:channels, width:] - both[channels:, :width]
+        return carry
+
+    lax.fori_loop(0, degrees, product, 0, unroll=steps(degrees))
+
+
+def adam_kernel(
+    factor_ref, encoder_ref, thin_ref, weight_ref, first_ref, second_ref,
+    weight_out, first_out, second_out, low_out,
+):
+    factor = factor_ref[0]
+    encoder_high, encoder_low = halves(encoder_ref[...])
+    left = jnp.concatenate([encoder_high, encoder_high, encoder_low], axis=0)
+    for degree, part in np.ndindex(thin_ref.shape[:2]):
+        high, low = halves(thin_ref[degree, part] * factor)
+        right = jnp.concatenate([high, low, high], axis=0)
+        gradient = lax.dot_general(
+            left, right, (((0,), (0,)), ((), ())), preferred_element_type=jnp.float32
+        )
+        weight, first, second = adam_step(
+            weight_ref[degree, part], first_ref[degree, part], second_ref[degree, part], gradient, WEIGHT_DECAY
+        )
+        weight_out[degree, part] = weight
+        first_out[degree, part] = first
+        second_out[degree, part] = second
+        low_out[degree, part] = weight.astype(jnp.bfloat16)
+
+
+def table_kernel(own, me_ref, slot_ref, wire_ref, degree_ref, place_ref, *rows_refs):
+    groups, slots, lanes = rows_refs[0].shape
+    lat = lanes // 8
+    per_tile = 128 // lat
+    degree = degree_ref[...]
+    count = degree.shape[0]
+    lane = lax.broadcasted_iota(jnp.int32, (count, 128), 1) // lat
+    me = me_ref[0]
+
+    def one_group(group, carry):
+        found = ([], [])
+        for first in range(0, 8, per_tile):
+            tiles = [jnp.zeros((count, 128), jnp.float32)] * 2
+            for place in range(per_tile):
+                order = group * 8 + first + place
+                slot = slot_ref[order]
+                source = slot // own
+                at = slot - source * own
+                block = at // per_tile
+                columns = pl.ds(pl.multiple_of(block * 128, 128), 128)
+                shift = lax.rem((place - (at - block * per_tile)) * lat + 128, 128)
+                live = (degree >= order) & (order < M) & (degree < L) & (lane == place)
+                for table in range(2):
+                    both = [wire_ref[(2 * table + half) ^ me, source, :, columns] for half in range(2)]
+                    moved = pltpu.roll(jnp.concatenate(both, axis=0), shift, 1)
+                    tiles[table] = jnp.where(live, moved, tiles[table])
+            for table in range(2):
+                found[table].append(tiles[table])
+        place = place_ref[...]
+        for table in range(2):
+            high, low = halves(jnp.concatenate(found[table], axis=1))
+            rows = jnp.dot(high, place, preferred_element_type=jnp.float32)
+            rows += jnp.dot(low, place, preferred_element_type=jnp.float32)
+            rows_refs[table][group] = rows[:slots]
+        return carry
+
+    lax.fori_loop(0, groups, one_group, 0, unroll=steps(groups))
+
+
+def order_chunk(order_count, lat_total, width):
+    best = 8
+    for size in range(8, order_count + 1, 8):
+        if order_count % size == 0 and lat_total * size * width * 8 <= 8.5 * 2**20:
+            best = size
+    return best
+
+
+def vmem(mebibytes):
+    return pltpu.CompilerParams(
+        dimension_semantics=("arbitrary",), vmem_limit_bytes=mebibytes * 2**20
+    )
+
+
+def table_rows(wire, slot_of, degrees, own, lat_total, slots):
+    groups = slot_of.shape[0] // 8
+    lane = np.arange(lat_total * 8)
+    place = np.zeros((lat_total * 8, lat_total * 8), np.float32)
+    place[lane, lane % lat_total * 8 + lane // lat_total] = 1.0
+    return pl.pallas_call(
+        functools.partial(table_kernel, own),
+        in_specs=[pl.BlockSpec(memory_space=pltpu.SMEM)] * 2
+        + [pl.BlockSpec(memory_space=pltpu.VMEM)] * 3,
+        out_specs=[pl.BlockSpec(memory_space=pltpu.VMEM)] * 2,
+        out_shape=[jax.ShapeDtypeStruct((groups, slots, lat_total * 8), jnp.float32)] * 2,
+        compiler_params=pltpu.CompilerParams(vmem_limit_bytes=32 * 2**20),
+        name="table_rows",
+    )(lax.axis_index("dp")[None], slot_of, wire, degrees[:, None], jnp.asarray(place, jnp.bfloat16))
+
+
+def exchange(value, axis, count, bit):
+    return lax.ppermute(value, axis, [(i, i ^ bit) for i in range(count)])
+
+
+def tables_to_degrees(forward_table, inverse_table, wide_count, degree_slots):
+    own, lat_total, order_count = forward_table.shape
+    dp_count = lax.axis_size("dp")
+    half = -(-degree_slots // 16) * 8
+    spare = ((0, 0), (0, 2 * half - degree_slots), (0, -own * lat_total % 128))
+
+    def rows(table):
+        table = jnp.pad(table.reshape(wide_count, degree_slots, own * lat_total), spare)
+        return table.reshape(wide_count, 2, half, table.shape[2])
+
+    wire = jnp.concatenate(
+        [rows(forward_table.transpose(2, 0, 1)), rows(inverse_table.transpose(1, 0, 2))], axis=1
+    )
+    wire = lax.dynamic_index_in_dim(wire, lax.axis_index("dp"), 1, keepdims=False)
+    wire = lax.all_to_all(wire, "wide", split_axis=0, concat_axis=0, tiled=True)
+    found = []
+    for part, bits in ((wire[: wide_count // 2], (1, 2)), (wire[wide_count // 2 :], (2, 1))):
+        by_index = {0: part}
+        for bit in bits:
+            names = list(by_index)
+            passed = exchange(jnp.stack([by_index[i] for i in names]), "dp", dp_count, bit)
+            by_index.update({i ^ bit: passed[k] for k, i in enumerate(names)})
+        found.append(jnp.stack([by_index[i] for i in range(4)]))
+    return jnp.concatenate(found, axis=1)
+
+
+def all_sum(rows):
+    dp_count, wide_count = lax.axis_size("dp"), lax.axis_size("wide")
+    if dp_count != 4 or wide_count & (wide_count - 1):
+        return lax.psum(rows, ("dp", "wide"))
+    me = lax.axis_index("dp")
+    piece = rows
+    for bit in (1, 2):
+        parts = piece.reshape((2, piece.shape[0] // 2) + piece.shape[1:])
+        mine = (me & bit) // bit
+        sent = lax.dynamic_index_in_dim(parts, 1 - mine, 0, keepdims=False)
+        kept = lax.dynamic_index_in_dim(parts, mine, 0, keepdims=False)
+        piece = kept + exchange(sent, "dp", dp_count, bit)
+    bit = 1
+    while bit < wide_count:
+        piece = piece + exchange(piece, "wide", wide_count, bit)
+        bit *= 2
+    for bit in (2, 1):
+        other = exchange(piece, "dp", dp_count, bit)
+        mine = (me & bit) // bit == 0
+        piece = jnp.concatenate(
+            [jnp.where(mine, piece, other), jnp.where(mine, other, piece)], axis=0
+        )
+    return piece
+
+
+def spectral_forward(spectra, fwd_rows, inv_rows, folded):
+    lat_total, order_count, thin = spectra.shape
+    degrees, _, channels, width = folded.shape
+    slots = fwd_rows.shape[1]
+    size = order_chunk(order_count, lat_total, width)
+    groups = size // 8
+    return pl.pallas_call(
+        forward_kernel,
+        grid=(order_count // size,),
+        in_specs=[
+            pl.BlockSpec((lat_total, size, thin), lambda i: (0, i, 0)),
+            pl.BlockSpec((groups,) + fwd_rows.shape[1:], lambda i: (i, 0, 0)),
+            pl.BlockSpec((groups,) + inv_rows.shape[1:], lambda i: (i, 0, 0)),
+            pl.BlockSpec(folded.shape, lambda i: (0, 0, 0, 0)),
+        ],
+        out_specs=pl.BlockSpec((lat_total, size, 2 * width), lambda i: (0, i, 0)),
+        out_shape=jax.ShapeDtypeStruct((lat_total, order_count, 2 * width), jnp.float32),
+        scratch_shapes=[
+            pltpu.VMEM((slots, size, thin), jnp.float32),
+            pltpu.VMEM((slots, size, 2 * width), jnp.float32),
+        ],
+        compiler_params=vmem(60),
+        name="spectral_forward",
+    )(spectra, fwd_rows, inv_rows, folded)
+
+
+def spectral_backward(grid_grad, spectra, fwd_rows, inv_rows, degrees, channels):
+    lat_total, order_count, thin = spectra.shape
+    width = grid_grad.shape[2] // 2
+    slots = fwd_rows.shape[1]
+    size = order_chunk(order_count, lat_total, width)
+    groups = size // 8
+    table = pl.BlockSpec((groups,) + fwd_rows.shape[1:], lambda i: (i, 0, 0))
+    return pl.pallas_call(
+        backward_kernel,
+        grid=(order_count // size,),
+        in_specs=[
+            pl.BlockSpec((lat_total, size, 2 * width), lambda i: (0, i, 0)),
+            pl.BlockSpec((lat_total, size, thin), lambda i: (0, i, 0)),
+            table,
+            table,
+        ],
+        out_specs=pl.BlockSpec((degrees, 2, channels, width), lambda i: (0, 0, 0, 0)),
+        out_shape=jax.ShapeDtypeStruct((degrees, 2, channels, width), jnp.float32),
+        scratch_shapes=[
+            pltpu.VMEM((slots, size, thin), jnp.float32),
+            pltpu.VMEM((slots, size, 2 * width), jnp.float32),
+        ],
+        compiler_params=vmem(60),
+        name="spectral_backward",
+    )(grid_grad, spectra, fwd_rows, inv_rows)
+
+
+def spectral_adam(factor, encoder, thin, weight, first, second):
+    degrees = weight.shape[0]
+    size = steps(degrees)
+    whole = pl.BlockSpec((size,) + weight.shape[1:], lambda i: (i, 0, 0, 0))
+    wide_out = jax.ShapeDtypeStruct(weight.shape, jnp.float32)
+    return pl.pallas_call(
+        adam_kernel,
+        grid=(degrees // size,),
+        in_specs=[
+            pl.BlockSpec(memory_space=pltpu.SMEM),
+            pl.BlockSpec(encoder.shape, lambda i: (0, 0)),
+            pl.BlockSpec((size,) + thin.shape[1:], lambda i: (i, 0, 0, 0)),
+            whole,
+            whole,
+            whole,
+        ],
+        out_specs=[whole] * 4,
+        out_shape=[wide_out] * 3 + [jax.ShapeDtypeStruct(weight.shape, jnp.bfloat16)],
+        compiler_params=vmem(48),
+        name="spectral_adam",
+    )(factor, encoder, thin, weight, first, second)
 
 
 def pixel_weights(land_mask, missing_rows, first_row, lat_total, channels):
@@ -51,8 +374,8 @@
 def adam_step(weight, moment_one, moment_two, gradient, decay_rate):
     first_new = BETA_ONE * moment_one + (1.0 - BETA_ONE) * gradient
     second_new = BETA_TWO * moment_two + (1.0 - BETA_TWO) * gradient * gradient
-    first_hat = first_new / (1.0 - BETA_ONE**STEP)
-    second_hat = second_new / (1.0 - BETA_TWO**STEP)
+    first_hat = first_new * (1.0 / (1.0 - BETA_ONE**STEP))
+    second_hat = second_new * (1.0 / (1.0 - BETA_TWO**STEP))
     weight_new = weight - LEARN_RATE * (
         first_hat / (jnp.sqrt(second_hat) + EPSILON) + decay_rate * weight
     )
@@ -100,40 +423,61 @@
     hidden_bias = biases[width : width + hidden_units]
     mlp_bias = biases[width + hidden_units : 2 * width + hidden_units]
     out_bias = biases[2 * width + hidden_units :]
-    encoder = jnp.concatenate([io_weight[0], enc_bias[None]], axis=0)
+    thin_count = -(-(channels + 1) // 16) * 16
+    spare = thin_count - channels - 1
+    encoder = jnp.concatenate(
+        [io_weight[0], enc_bias[None], jnp.zeros((spare, width), jnp.float32)], axis=0
+    )
+
+    spectra = dot("caj,psj->pacs", fields, forward)
+    spectra = lax.all_gather(spectra, "wide", axis=0, tiled=False)
+    ones_row = forward.astype(np.float64).sum(axis=2).astype(np.float32)
+    spectra = jnp.concatenate(
+        [
+            spectra,
+            jnp.broadcast_to(ones_row[None, :, None, None, :], (wide_count, 2, lat_dev, 1, order_count)),
+            jnp.zeros((wide_count, 2, lat_dev, spare, order_count), jnp.float32),
+        ],
+        axis=3,
+    )
+    spectra = spectra.transpose(0, 2, 4, 1, 3).reshape(lat_total, order_count, 2 * thin_count)
 
     my_degrees = lax.dynamic_slice_in_dim(degree_map, position * degree_slots, degree_slots)
     slot_of = jnp.argsort(order_map)
-    fwd_table = lax.all_to_all(forward_table, "wide", split_axis=2, concat_axis=0, tiled=True)
-    inv_table = lax.all_to_all(inverse_table, "wide", split_axis=1, concat_axis=0, tiled=True)
-    orders = jnp.arange(order_count, dtype=jnp.int32)
-    live = (
-        (my_degrees[None, :] >= orders[:, None]) & (orders[:, None] < M) & (my_degrees[None, :] < L)
-    ).astype(jnp.float32)
-    fwd_masked = fwd_table[slot_of] * live[:, None, :]
-    inv_masked = inv_table[slot_of] * live[:, :, None]
-
-    spectra = dot("caj,spj->aspc", fields, forward)
-    spectra = lax.all_gather(spectra, "wide", axis=0, tiled=True)
-    ones_row = jnp.asarray(forward.astype(np.float64).sum(axis=2).astype(np.float32))
-    spectra = jnp.concatenate(
-        [spectra, jnp.broadcast_to(ones_row[None, :, :, None], (lat_total, order_count, 2, 1))], axis=3
-    )
-    coeffs = dot("sat,aspc->tspc", fwd_masked, spectra)
+    slots = degree_slots + degree_slots % 2
+    if 128 % lat_total == 0 and lax.axis_size("dp") == 4 and wide_count % 2 == 0:
+        wire = tables_to_degrees(forward_table, inverse_table, wide_count, degree_slots)
+        degrees = jnp.pad(my_degrees, (0, 2 * wire.shape[2] - degree_slots), constant_values=-1)
+        own = forward_table.shape[0]
+        fwd_rows, inv_rows = table_rows(wire, slot_of, degrees, own, lat_total, slots)
+    else:
+        fwd_table = lax.all_to_all(forward_table, "wide", split_axis=2, concat_axis=0, tiled=True)
+        inv_table = lax.all_to_all(inverse_table, "wide", split_axis=1, concat_axis=0, tiled=True)
+        orders = jnp.arange(order_count, dtype=jnp.int32)
+        live = (
+            (my_degrees[None, :] >= orders[:, None])
+            & (orders[:, None] < M)
+            & (my_degrees[None, :] < L)
+        ).astype(jnp.float32)
+        even = ((0, 0), (0, degree_slots % 2), (0, 0), (0, 0))
+        fwd_masked = fwd_table[slot_of] * live[:, None, :]
+        inv_masked = inv_table[slot_of] * live[:, :, None]
+        fwd_masked = fwd_masked.reshape(order_count // 8, 8, lat_total, degree_slots)
+        inv_masked = inv_masked.reshape(order_count // 8, 8, degree_slots, lat_total)
+
+        def by_degree(table):
+            return jnp.pad(table, even).reshape(order_count // 8, slots, lat_total * 8)
+
+        fwd_rows = by_degree(fwd_masked.transpose(0, 3, 2, 1))
+        inv_rows = by_degree(inv_masked.transpose(0, 2, 3, 1))
+
     folded = dot("cd,tpdk->tpck", encoder, spectral_weight)
-    out_re = dot("tsc,tck->tsk", coeffs[:, :, 0], folded[:, 0]) - dot(
-        "tsc,tck->tsk", coeffs[:, :, 1], folded[:, 1]
-    )
-    out_im = dot("tsc,tck->tsk", coeffs[:, :, 0], folded[:, 1]) + dot(
-        "tsc,tck->tsk", coeffs[:, :, 1], folded[:, 0]
-    )
-    mixed_coef = jnp.concatenate([out_re, out_im], axis=2)
-    grid_coef = dot("sta,tsk->ask", inv_masked, mixed_coef)
+    grid_coef = spectral_forward(spectra, fwd_rows, inv_rows, folded)
     grid_coef = lax.psum_scatter(grid_coef, "wide", scatter_dimension=0, tiled=True)
     grid_coef = grid_coef.reshape(lat_dev, order_count, 2, width)
 
     encoded = dot("caj,ck->ajk", fields, io_weight[0]) + enc_bias
-    mixed_in = encoded + dot("aspc,spj->ajc", grid_coef, inverse)
+    mixed_in = encoded + dot("aspc,psj->ajc", grid_coef, inverse)
     hidden_pre = dot("ajk,kh->ajh", mixed_in, mlp_weight[0]) + hidden_bias
     hidden_act, smooth_back = jax.vjp(smooth, hidden_pre)
     latent = mixed_in + dot("ajh,kh->ajk", hidden_act, mlp_weight[1]) + mlp_bias
@@ -155,33 +499,34 @@
     up_grad = dot("ajk,ajh->kh", mixed_in, pre_grad)
     mixed_grad = latent_grad + dot("ajh,kh->ajk", pre_grad, mlp_weight[0])
 
-    grid_grad = dot("ajc,spj->aspc", mixed_grad, inverse).reshape(lat_dev, order_count, 2 * width)
+    grid_grad = dot("ajc,psj->aspc", mixed_grad, inverse).reshape(lat_dev, order_count, 2 * width)
     grid_grad = lax.all_gather(grid_grad, "wide", axis=0, tiled=True)
-    out_grad = dot("sta,ask->tsk", inv_masked, grid_grad)
-    out_re_grad, out_im_grad = out_grad[:, :, :width], out_grad[:, :, width:]
-    real_part = dot("tsc,tsk->tck", coeffs[:, :, 0], out_re_grad) + dot(
-        "tsc,tsk->tck", coeffs[:, :, 1], out_im_grad
-    )
-    imag_part = dot("tsc,tsk->tck", coeffs[:, :, 0], out_im_grad) - dot(
-        "tsc,tsk->tck", coeffs[:, :, 1], out_re_grad
-    )
-    thin = jnp.stack([real_part, imag_part], axis=1)
-    encoder_grad = dot("tpck,tpdk->cd", thin, spectral_weight)
     direct = dot("caj,ajk->ck", fields, mixed_grad)
     direct_bias = jnp.sum(mixed_grad, axis=(0, 1))
-    encoder_grad = encoder_grad + jnp.concatenate([direct, direct_bias[None]], axis=0)
-    io_grad = jnp.stack([encoder_grad[:channels], decoder_grad])
-    mlp_grad = jnp.stack([up_grad, down_grad])
-    bias_grad = jnp.concatenate(
-        [encoder_grad[channels], hidden_bias_grad, mlp_bias_grad, out_bias_grad]
-    )
-    io_grad, mlp_grad, bias_grad, loss_sum, valid_weight = lax.psum(
-        (io_grad, mlp_grad, bias_grad, loss_local, count_local), ("dp", "wide")
-    )
+    small = [direct_bias, hidden_bias_grad, mlp_bias_grad, out_bias_grad, loss_local[None], count_local[None]]
+    small = jnp.concatenate(small)
+    small_count = small.shape[0]
+    flat = [up_grad.reshape(-1, width), down_grad.reshape(-1, width), decoder_grad, direct]
+    flat.append(jnp.pad(small, (0, -small_count % width)).reshape(-1, width))
+    flat = jnp.concatenate(flat, axis=0)
+    flat = all_sum(jnp.pad(flat, ((0, -flat.shape[0] % 32), (0, 0))))
+    grid_grad, flat = lax.optimization_barrier((grid_grad, flat))
+    thin = spectral_backward(grid_grad, spectra, fwd_rows, inv_rows, degree_slots, thin_count)
+    at = 2 * hidden_units
+    mlp_grad = flat[:at].reshape(2, width, hidden_units)
+    decoder_grad = flat[at : at + channels]
+    direct = flat[at + channels : at + 2 * channels]
+    small = flat[at + 2 * channels :].reshape(-1)[:small_count]
+    encoder_grad = all_sum(dot("tpck,tpdk->cd", thin, spectral_weight))
     thin = lax.psum(thin, "dp")
     gram = jnp.einsum("ck,dk->cd", encoder, encoder, precision=lax.Precision.HIGHEST)
-    spectral_squares = jnp.sum(thin * jnp.einsum("cd,tpdk->tpck", gram, thin, precision=lax.Precision.HIGHEST))
+    spectral_squares = jnp.sum(
+        thin * jnp.einsum("cd,tpdk->tpck", gram, thin, precision=lax.Precision.HIGHEST)
+    )
     spectral_squares = lax.psum(spectral_squares, "wide")
+    io_grad = jnp.stack([direct + encoder_grad[:channels], decoder_grad])
+    bias_grad = jnp.concatenate([small[:width] + encoder_grad[channels], small[width:-2]])
+    loss_sum, valid_weight = small[-2], small[-1]
     rescale = entries / valid_weight
     squares = (
         spectral_squares
@@ -191,9 +536,8 @@
     )
     grad_norm = jnp.sqrt(squares) * rescale
     factor = rescale * CLIP_LIMIT / jnp.maximum(grad_norm, CLIP_LIMIT)
-    spectral_total = dot("cd,tpck->tpdk", encoder, thin)
-    spectral_new, spectral_first_new, spectral_second_new = adam_step(
-        spectral_weight, spectral_first, spectral_second, spectral_total * factor, WEIGHT_DECAY
+    spectral_new, spectral_first_new, spectral_second_new, spectral_low = spectral_adam(
+        factor[None], encoder, thin, spectral_weight, spectral_first, spectral_second
     )
     io_new, io_first_new, io_second_new = adam_step(
         io_weight, io_first, io_second, io_grad * factor, WEIGHT_DECAY
@@ -211,7 +555,7 @@
         spectral_new,
         spectral_first_new,
         spectral_second_new,
-        spectral_new.astype(jnp.bfloat16),
+        spectral_low,
         io_new,
         io_first_new,
         io_second_new,

time: 1610 us -> 1080 us (0.67)
  matrix products: 438 us -> 109 us
  local copies, waits for them, and re-layouts: 345 us -> 67.3 us
  Pallas kernels: 0 us -> 180 us
  waiting for transfers between devices: 663 us -> 558 us
  other arithmetic: 69.5 us -> 25.8 us
  blocking collectives: 55.9 us -> 85 us
  starting transfers between devices: 10.9 us -> 29.7 us
    dot_general x28 -> x16, matrix products: 426 us -> 97.2 us  [dot(): return jnp.einsum(spec, left, right, precision=HIGH)]
    unnamed x108 -> x67, local copies, waits for them, and re-layouts: 222 us -> 18.7 us
    pallas_call x0 -> x4, Pallas kernels: none -> 180 us  [the longest x1 57.4 us: spectral_adam(): pl.pallas_call(adam_kernel, grid=(degrees // size,), in_specs=[pl.BlockSp...]
    ppermute x0 -> x18, waiting for transfers between devices: none -> 141 us  [exchange(): return lax.ppermute(value, axis, [(i, i ^ bit) for i in range(count)])]
    all_gather x1, waiting for transfers between devices: 185 us -> 59.7 us  [body(): grid_grad = lax.all_gather(grid_grad, 'wide', axis=0, tiled=True)]
    all_to_all x2 -> x0, waiting for transfers between devices: 80.4 us -> none  [the longest x1 80.4 us: body(): lax.all_to_all(forward_table, 'wide', split_axis=2, concat_axis=0, tiled=...]
    all_to_all x0 -> x1, blocking collectives: none -> 67.8 us  [tables_to_degrees(): wire = lax.all_to_all(wire, 'wide', split_axis=0, concat_axis=0, tiled=True)]
    psum x1 -> x0, blocking collectives: 38.7 us -> none  [body(): lax.psum((io_grad, mlp_grad, bias_grad, loss_local, count_local), ('dp',...]
  transfers between devices with their start and end apart: 7 -> 22, of which waited for: 5 -> 20; matrix products, arithmetic and copies ran while one was open for 14% -> 8% of each run, Pallas kernels for 0% -> 1%
where the time goes in v2:
time: 1080 us; the launch traced here: 1070 us
  waiting for transfers between devices  558 us (52%)
  Pallas kernels  180 us (17%)
  matrix products  109 us (10%)
  blocking collectives  85 us (8%)
  local copies, waits for them, and re-layouts  67.3 us (6%)
  starting transfers between devices  29.7 us (3%)
  other arithmetic  25.8 us (2%)
  between operations  19.3 us (2%)
    reduce_scatter x1, waiting for transfers between devices, body(): lax.psum_scatter(grid_coef, 'wide', scatter_dimension=0, tiled=True)  226 us
    ppermute x18, waiting for transfers between devices, exchange(): return lax.ppermute(value, axis, [(i, i ^ bit) for i in range(count)])  141 us
    psum x1, waiting for transfers between devices, body(): thin = lax.psum(thin, 'dp')  132 us
    dot_general x16, matrix products, dot(): return jnp.einsum(spec, left, right, precision=HIGH)  97.2 us
    all_to_all x1, blocking collectives, tables_to_degrees(): wire = lax.all_to_all(wire, 'wide', split_axis=0, concat_axis=0, tiled=True)  67.8 us
    all_gather x1, waiting for transfers between devices, body(): grid_grad = lax.all_gather(grid_grad, 'wide', axis=0, tiled=True)  59.7 us
    pallas_call x1, Pallas kernels, spectral_adam(): pl.pallas_call(adam_kernel, grid=(degrees // size,), in_specs=[pl.BlockSp...  57.4 us
    pallas_call x1, Pallas kernels, spectral_forward(): pl.pallas_call(forward_kernel, grid=(order_count // size,), in_specs=[pl....  56.5 us
  transfers between devices with their start and end apart: 22, of which 20 were waited for; matrix products, arithmetic and copies ran while one was open for 8% of the time, Pallas kernels for 1%

profile of v2, /device:TPU:0, one launch (start us, length us, event | category | flops | bytes accessed | tf_op | source)
XLA Modules:
  0.0 1073.9 jit_solution(960163134104953357)
XLA Ops:
  16.1 5.9 copy.141
  26.1 5.7 copy.142
  36.1 67.8 %all_to_all.5 = f32[8,24,1536]{2,1,0:T(8,128)S(1)} all-to-all(f32[8,24,1536]{2,1,0:T(8,128)S(1)} %fusion.26), channel_id=1, replica_groups=mesh['dp'=4,'wide'=8] {'wide'}, dimensions={0} | all-to-all | bytes 2359296 | tf_op jit(solution)/shard_map/all_to_all | solution.py:251
  112.1 7.4 collective-permute-done.2
  124.8 14.9 %convolution_bitcast_fusion.folded_ref = f32[45,2,80,256]{3,2,1,0:T(8,128)} fusion(f32[45,2,256,256]{3,2,1,0:T(8,128)} %weight_ref.1, f32[80,256]{1,0:T(8,128)S(1)} %maximum_maximum_fusion.1.encoder_ref), kind=kOutput, calls=%fused_computation.25 | convolution fusion | flops 2831155200 | bytes 31047680 | tf_op jit(solution)/shard_map/cd,tpdk->tpck/dot_general | solution.py:32
  139.7 8.4 collective-permute-done.3
  152.1 11.4 %table_rows.1 = (f32[45,46,256]{2,1,0:T(8,128)S(1)}, f32[45,46,256]{2,1,0:T(8,128)S(1)}) custom-call(s32[1]{0:T(128)} %bitcast.11.me_ref, s32[360]{0:T(512)S(1)} %get-tuple-element.28.slot_ref, f32[4,8,24,1536]{3,2,1,0:T(8,128)S(1)} %maximum_maximum_fusion.wire_ref, s32[48,1]{1,0:T(8,128)S(1)} %copy.114.degree_ref, bf16[256,256]{1,0:T(8,128)(2,1)S(1)} %copy-done.2), custom_call_target="tpu_custom_call" | custom-call | tf_op jit(solution)/shard_map/table_rows/pallas_call | solution.py:222
  166.2 8.4 maximum_bitcast_fusion
  174.6 7.4 copy.111
  182.0 10.3 copy.115.spec_ref
  192.4 56.5 %spectral_forward.1 = f32[32,360,512]{2,1,0:T(8,128)} custom-call(f32[32,360,160]{2,1,0:T(8,128)} %copy.115.spec_ref, f32[45,46,256]{2,1,0:T(8,128)} %copy-done, f32[45,46,256]{2,1,0:T(8,128)} %copy-done.1, f32[45,2,80,256]{3,2,1,0:T(8,128)} %convolution_bitcast_fusion.folded_ref), custom_call_target="tpu_custom_call" | custom-call | tf_op jit(solution)/shard_map/spectral_forward/pallas_call | solution.py:294
  253.3 225.6 %reduce-scatter.2.cloned.1.call-done = f32[4,360,512]{2,1,0:T(8,128)} async-done(((f32[32,360,512]{2,1,0:T(8,128)}), f32[4,360,512]{2,1,0:T(8,128)}) %reduce-scatter.2.cloned.1.call-update) | async-done | bytes 2949136 | tf_op jit(solution)/shard_map/reduce_scatter | solution.py:476
  478.9 7.3 bitcast_add_fusion
  488.7 4.5 add_add_fusion
  497.5 10.1 fusion.93
  516.9 6.1 convolution_bitcast_fusion.2
  524.2 10.4 fusion.24
  553.9 11.8 %collective-permute-done.4 = f32[592,256]{1,0:T(8,128)S(1)} collective-permute-done((f32[592,256]{1,0:T(8,128)S(1)}, f32[592,256]{1,0:T(8,128)S(1)}, u32[]{:S(2)}, u32[]{:S(2)}) %collective-permute-start.4) | collective-permute-done | bytes 606240 | tf_op jit(solution)/shard_map/ppermute | solution.py:234
  567.3 5.4 collective-permute-done.5
  574.5 4.4 collective-permute-start.7
  578.8 28.8 %collective-permute-done.7 = f32[296,256]{1,0:T(8,128)S(1)} collective-permute-done((f32[296,256]{1,0:T(8,128)S(1)}, f32[296,256]{1,0:T(8,128)S(1)}, u32[]{:S(2)}, u32[]{:S(2)}) %collective-permute-start.7) | collective-permute-done | bytes 303136 | tf_op jit(solution)/shard_map/ppermute | solution.py:234
  607.7 8.4 collective-permute-start.8
  616.0 35.4 %collective-permute-done.8 = f32[296,256]{1,0:T(8,128)S(1)} collective-permute-done((f32[296,256]{1,0:T(8,128)S(1)}, f32[296,256]{1,0:T(8,128)S(1)}, u32[]{:S(2)}, u32[]{:S(2)}) %collective-permute-start.8) | collective-permute-done | bytes 303136 | tf_op jit(solution)/shard_map/ppermute | solution.py:234
  651.5 9.0 collective-permute-done.9
  660.7 14.7 %collective-permute-done.10 = f32[592,256]{1,0:T(8,128)S(1)} collective-permute-done((f32[592,256]{1,0:T(8,128)S(1)}, f32[592,256]{1,0:T(8,128)S(1)}, u32[]{:S(2)}, u32[]{:S(2)}) %collective-permute-start.10) | collective-permute-done | bytes 606240 | tf_op jit(solution)/shard_map/ppermute | solution.py:234
  675.6 59.7 %all-gather.4.cloned.1.call-done.grid_ref = f32[32,360,512]{2,1,0:T(8,128)} async-done(((f32[4,360,512]{2,1,0:T(8,128)}), f32[32,360,512]{2,1,0:T(8,128)}) %all-gather.4.cloned.1.call-update) | async-done | bytes 23592976 | tf_op jit(solution)/shard_map/all_gather | solution.py:503
  735.3 54.2 %spectral_backward.1 = f32[45,2,80,256]{3,2,1,0:T(8,128)} custom-call(f32[32,360,512]{2,1,0:T(8,128)} %all-gather.4.cloned.1.call-done.grid_ref, f32[32,360,160]{2,1,0:T(8,128)} %copy.115.spec_ref, f32[45,46,256]{2,1,0:T(8,128)} %copy-done, f32[45,46,256]{2,1,0:T(8,128)} %copy-done.1), custom_call_target="tpu_custom_call" | custom-call | tf_op jit(solution)/shard_map/spectral_backward/pallas_call | solution.py:321
  789.5 16.8 %fusion = f32[80,256,1,1]{1,0,3,2:T(8,128)S(1)} fusion(f32[45,2,256,256]{3,2,1,0:T(8,128)} %weight_ref.1, f32[45,2,80,256]{3,2,1,0:T(8,128)} %spectral_backward.1), kind=kOutput, calls=%fused_computation | convolution fusion | flops 2831155200 | bytes 31047680 | tf_op jit(solution)/shard_map/tpck,tpdk->cd/dot_general | solution.py:32
  834.6 131.6 %all-reduce.7.cloned.1.call-done.thin_ref = f32[45,2,80,256]{3,2,1,0:T(8,128)} async-done(((f32[45,2,80,256]{3,2,1,0:T(8,128)}), f32[45,2,80,256]{3,2,1,0:T(8,128)}) %all-reduce.7.cloned.1.call-update) | async-done | bytes 7372816 | tf_op jit(solution)/shard_map/psum | solution.py:521
  966.2 11.5 %fusion.2 = f32[]{:T(128)} fusion(f32[45,2,80,256]{3,2,1,0:T(8,128)} %all-reduce.7.cloned.1.call-done.thin_ref, f32[80,80,1,1]{1,0,3,2:T(8,128)S(1)} %convolution_bitcast_fusion.5), kind=kOutput, calls=%fused_computation.6 | convolution fusion | flops 1773158400 | bytes 7398404 | tf_op jit(solution)/shard_map/cd,tpdk->tpck/dot_general | solution.py:524
  978.4 17.2 %psum.15 = f32[]{:T(128)} all-reduce(f32[]{:T(128)} %fusion.2), channel_id=1, replica_groups=mesh['dp'=4,'wide'=8] {'wide'}, use_global_device_ids=true, to_apply=%region_10.11 | all-reduce | flops 1 | bytes 8 | tf_op jit(solution)/shard_map/psum | solution.py:526
  1008.3 57.4 %spectral_adam.1 = (f32[45,2,256,256]{3,2,1,0:T(8,128)}, f32[45,2,256,256]{3,2,1,0:T(8,128)}, f32[45,2,256,256]{3,2,1,0:T(8,128)}, bf16[45,2,256,256]{3,2,1,0:T(8,128)(2,1)}) custom-call(f32[1]{0:T(128)} %bitcast.70.factor_ref, f32[80,256]{1,0:T(8,128)S(1)} %maximum_maximum_fusion.1.encoder_ref, f32[45,2,80,256]{3,2,1,0:T(8,128)} %all-reduce.7.cloned.1.call-done.thin_ref, ...), custom_call_target="tpu_custom_call" | custom-call | tf_op jit(solution)/shard_map/spectral_adam/pallas_call | solution.py:346
  (183 shorter events, 120.3 us)
Async XLA Ops:
  7.2 159.0 %all-gather.6.cloned.1.call-start = ((), (), s32[]{:S(2)}) async-start(), calls=%async_computation.5 | async-start | bytes 8073216 | tf_op jit(solution)/shard_map/all_gather | solution.py:433
  12.0 466.9 %reduce-scatter.2.cloned.1.call-start = ((), (), s32[]{:S(2)}) async-start(), calls=%async_computation.2 | async-start | bytes 26542080 | tf_op jit(solution)/shard_map/reduce_scatter | solution.py:476
  35.9 69.8 %copy-start.22 = (f32[1097]{0:T(1024)S(1)}, f32[1097]{0:T(1024)}, u32[]{:S(2)}) copy-start(f32[1097]{0:T(1024)} %param.42) | copy-start | bytes 13168
  35.9 69.8 %copy-start.18 = (f32[2,73,256]{2,0,1:T(2,128)S(1)}, f32[2,73,256]{2,0,1:T(2,128)}, u32[]{:S(2)}) copy-start(f32[2,73,256]{2,0,1:T(2,128)} %param.36) | copy-start | bytes 448516
  35.9 72.3 %copy-start.28 = (s32[360]{0:T(512)S(1)}, s32[360]{0:T(512)}, u32[]{:S(2)}) copy-start(s32[360]{0:T(512)} %param.29) | copy-start | bytes 4324
  104.0 15.5 %collective-permute-start.2 = (f32[1,4,24,1536]{3,2,1,0:T(8,128)S(1)}, f32[1,4,24,1536]{3,2,1,0:T(8,128)S(1)}, u32[]{:S(2)}, u32[]{:S(2)}) collective-permute-start(f32[1,4,24,1536]{3,2,1,0:T(8,128)S(1)} %get-tuple-element.114), channel_id=1, source_target_pairs={{0,16},{8,24},{16,0},{24,8},{1,17},{9,25},{17,1},{25,9},{2,18},{10... | collective-permute-start | bytes 1769480 | tf_op jit(solution)/shard_map/ppermute | solution.py:234
  106.5 15.5 %collective-permute-start = (f32[1,4,24,1536]{3,2,1,0:T(8,128)S(1)}, f32[1,4,24,1536]{3,2,1,0:T(8,128)S(1)}, u32[]{:S(2)}, u32[]{:S(2)}) collective-permute-start(f32[1,4,24,1536]{3,2,1,0:T(8,128)S(1)} %get-tuple-element.113), channel_id=1, source_target_pairs={{0,8},{8,0},{16,24},{24,16},{1,9},{9,1},{17,25},{25,17},{2,10},{10... | collective-permute-start | bytes 1769480 | tf_op jit(solution)/shard_map/ppermute | solution.py:234
  120.5 27.5 %collective-permute-start.3 = (f32[2,4,24,1536]{3,2,1,0:T(8,128)}, f32[2,4,24,1536]{3,2,1,0:T(8,128)}, u32[]{:S(2)}, u32[]{:S(2)}) collective-permute-start(f32[2,4,24,1536]{3,2,1,0:T(8,128)} %pad_maximum_fusion.2), channel_id=1, source_target_pairs={{0,8},{8,0},{16,24},{24,16},{1,9},{9,1},{17,25},{25,17},{2,10},{10... | collective-permute-start | bytes 3538952 | tf_op jit(solution)/shard_map/ppermute | solution.py:234
  123.1 27.3 %collective-permute-start.1 = (f32[2,4,24,1536]{3,2,1,0:T(8,128)}, f32[2,4,24,1536]{3,2,1,0:T(8,128)}, u32[]{:S(2)}, u32[]{:S(2)}) collective-permute-start(f32[2,4,24,1536]{3,2,1,0:T(8,128)} %pad_maximum_fusion.1), channel_id=1, source_target_pairs={{0,16},{8,24},{16,0},{24,8},{1,17},{9,25},{17,1},{25,9},{2,18},{10... | collective-permute-start | bytes 3538952 | tf_op jit(solution)/shard_map/ppermute | solution.py:234
  248.9 486.4 %all-gather.4.cloned.1.call-start = ((), (), s32[]{:S(2)}) async-start(), calls=%async_computation.3 | async-start | bytes 26542080 | tf_op jit(solution)/shard_map/all_gather | solution.py:503
  249.1 248.4 %copy-start.29 = (f32[512]{0:T(512)}, f32[512]{0:T(512)S(1)}, u32[]{:S(2)}) copy-start(f32[512]{0:T(512)S(1)} %slice.87) | copy-start | bytes 6148
  249.2 246.3 %copy-start.26 = (pred[73]{0:T(512)(128)(4,1)}, pred[73]{0:T(512)(128)(4,1)S(1)}, u32[]{:S(2)}) copy-start(pred[73]{0:T(512)(128)(4,1)S(1)} %iota_compare_fusion) | copy-start | bytes 223
  249.5 245.9 %copy-start.19 = (f32[4,720]{1,0:T(4,128)}, f32[4,720]{1,0:T(4,128)S(1)}, u32[]{:S(2)}) copy-start(f32[4,720]{1,0:T(4,128)S(1)} %subtract_convert_fusion) | copy-start | bytes 34564
  250.0 245.5 %copy-start.20 = (f32[4,720]{1,0:T(4,128)}, f32[4,720]{1,0:T(4,128)S(1)}, u32[]{:S(2)}) copy-start(f32[4,720]{1,0:T(4,128)S(1)} %multiply_bitcast_fusion) | copy-start | bytes 34564
  552.5 13.2 %collective-permute-start.4 = (f32[592,256]{1,0:T(8,128)S(1)}, f32[592,256]{1,0:T(8,128)S(1)}, u32[]{:S(2)}, u32[]{:S(2)}) collective-permute-start(f32[592,256]{1,0:T(8,128)S(1)} %dynamic-slice_bitcast_fusion), channel_id=1, source_target_pairs={{0,8},{8,0},{16,24},{24,16},{1,9},{9,1},{17,25},{25,17},{2,10},{10... | collective-permute-start | bytes 1818632 | tf_op jit(solution)/shard_map/ppermute | solution.py:234
  565.8 6.9 collective-permute-start.5
  572.7 1.7 collective-permute-start.6
  574.5 33.2 %collective-permute-start.7 = (f32[296,256]{1,0:T(8,128)S(1)}, f32[296,256]{1,0:T(8,128)S(1)}, u32[]{:S(2)}, u32[]{:S(2)}) collective-permute-start(f32[296,256]{1,0:T(8,128)S(1)} %add.233), channel_id=1, source_target_pairs={{0,2},{1,3},{2,0},{3,1},{4,6},{5,7},{6,4},{7,5},{8,10},{9,11},{10,... | collective-permute-start | bytes 909320 | tf_op jit(solution)/shard_map/ppermute | solution.py:234
  607.7 43.7 %collective-permute-start.8 = (f32[296,256]{1,0:T(8,128)S(1)}, f32[296,256]{1,0:T(8,128)S(1)}, u32[]{:S(2)}, u32[]{:S(2)}) collective-permute-start(f32[296,256]{1,0:T(8,128)S(1)} %add.234), channel_id=1, source_target_pairs={{0,4},{1,5},{2,6},{3,7},{4,0},{5,1},{6,2},{7,3},{8,12},{9,13},{10,... | collective-permute-start | bytes 909320 | tf_op jit(solution)/shard_map/ppermute | solution.py:234
  651.5 9.1 collective-permute-start.9
  660.6 14.8 %collective-permute-start.10 = (f32[592,256]{1,0:T(8,128)S(1)}, f32[592,256]{1,0:T(8,128)S(1)}, u32[]{:S(2)}, u32[]{:S(2)}) collective-permute-start(f32[592,256]{1,0:T(8,128)S(1)} %pad_maximum_fusion.3), channel_id=1, source_target_pairs={{0,8},{8,0},{16,24},{24,16},{1,9},{9,1},{17,25},{25,17},{2,10},{10... | collective-permute-start | bytes 1818632 | tf_op jit(solution)/shard_map/ppermute | solution.py:234
  806.3 159.9 %all-reduce.7.cloned.1.call-start = ((), (), s32[]{:S(2)}) async-start(), calls=%async_computation.4 | async-start | bytes 14745600 | tf_op jit(solution)/shard_map/psum | solution.py:521
  806.9 4.1 collective-permute-start.11
  811.0 3.9 collective-permute-start.12
  814.9 1.2 collective-permute-start.13
  816.1 3.8 collective-permute-start.14
  820.0 4.7 collective-permute-start.15
  824.7 4.3 collective-permute-start.16
  829.0 4.9 collective-permute-start.17
  831.2 167.1 %copy-start.21 = (f32[841]{0:T(1024)}, f32[841]{0:T(1024)S(1)}, u32[]{:S(2)}) copy-start(f32[841]{0:T(1024)S(1)} %slice.111) | copy-start | bytes 10096
  834.6 163.6 %copy-start.25 = (f32[1,256]{1,0:T(1,128)}, f32[1,256]{1,0:T(1,128)S(1)}, u32[]{:S(2)}) copy-start(f32[1,256]{1,0:T(1,128)S(1)} %slice_add_fusion) | copy-start | bytes 3076
  977.8 26.6 %copy-start.13 = (f32[2,256,512]{2,1,0:T(8,128)S(1)}, f32[2,256,512]{2,1,0:T(8,128)}, u32[]{:S(2)}) copy-start(f32[2,256,512]{2,1,0:T(8,128)} %param.39) | copy-start | bytes 3145732
  (21 other events, 97.5 us)
Sparse Core Ops, SparseCore 0:
  12.1 100.1 all-gather.5
  249.0 229.8 reduce-scatter.1
  517.0 218.2 all-gather.3
  810.7 155.4 all-reduce.6

commit v3 on v2

--- a/solution.py
+++ b/solution.py
@@ -69,23 +69,48 @@
     return max(size for size in range(1, 6) if count % size == 0)
 
 
-def coefficients(spec_ref, fwd_ref, coef_ref, group):
-    rows = pl.ds(pl.multiple_of(group * 8, 8), 8)
-    spectra = spec_ref[:, rows, :]
-    lat, _, thin = spectra.shape
-    product = dot3(block_diagonal(fwd_ref[group]), spectra.reshape(lat * 8, thin))
-    coef_ref[:, rows, :] = product.reshape(product.shape[0] // 8, 8, thin)
-
-
-def forward_kernel(spec_ref, fwd_ref, inv_ref, folded_ref, grid_ref, coef_ref, mixed_ref):
+def group_rows(group):
+    return pl.ds(pl.multiple_of(group * 8, 8), 8)
+
+
+def legendre(values, table, out_ref, group):
+    lat, _, lanes = values.shape
+    product = dot3(block_diagonal(table), values.reshape(lat * 8, lanes))
+    out_ref[:, group_rows(group), :] = product.reshape(product.shape[0] // 8, 8, lanes)
+
+
+def channel_spectra(spec_ref, lat_dev, channels, thin, group):
+    devices, _, size, lanes = spec_ref.shape
+    real = spec_ref[:, 0, group_rows(group), :].reshape(devices * 8, lanes)
+    imag = spec_ref[:, 1, group_rows(group), :].reshape(devices * 8, lanes)
+    lane = lax.broadcasted_iota(jnp.int32, (devices * 8, lanes), 1)
+    order = lax.broadcasted_iota(jnp.int32, (devices * 8, lanes), 0) & 7
+    order += pl.program_id(0) * size + group * 8
+    ones = jnp.where((order == 0) & (lane == channels), 1.0, 0.0)
+    half = thin // 2
+    rows = []
+    for row in range(lat_dev):
+        base = row * channels
+        left = pltpu.roll(real, (lanes - base) % lanes, 1) if base else real
+        right = pltpu.roll(imag, (half - base) % lanes, 1)
+        value = jnp.where((lane >= half) & (lane < half + channels), right, ones)
+        value = jnp.where(lane < channels, left, value)
+        rows.append(value[:, :thin].reshape(devices, 8, thin))
+    return jnp.stack(rows, axis=1).reshape(devices * lat_dev, 8, thin)
+
+
+def forward_kernel(lat_dev, channels, spec_ref, fwd_ref, inv_ref, folded_ref, grid_ref, coef_ref, mixed_ref):
     groups = fwd_ref.shape[0]
     degrees = folded_ref.shape[0]
     slots = mixed_ref.shape[0]
     for spare in range(degrees, slots):
         mixed_ref[spare] = jnp.zeros(mixed_ref.shape[1:], jnp.float32)
 
+    thin = coef_ref.shape[2]
+
     def analyse(group, carry):
-        coefficients(spec_ref, fwd_ref, coef_ref, group)
+        spectra = channel_spectra(spec_ref, lat_dev, channels, thin, group)
+        legendre(spectra, fwd_ref[group], coef_ref, group)
         return carry
 
     lax.fori_loop(0, groups, analyse, 0, unroll=steps(groups))
@@ -115,17 +140,18 @@
     lax.fori_loop(0, groups, synthesise, 0, unroll=steps(groups))
 
 
-def backward_kernel(grid_ref, spec_ref, fwd_ref, inv_ref, thin_ref, coef_ref, out_ref):
+def backward_kernel(degrees, lat_dev, fields, grid_ref, spec_ref, fwd_ref, inv_ref, thin_ref, coef_ref, out_ref):
     groups = fwd_ref.shape[0]
-    degrees, _, channels, width = thin_ref.shape
+    _, _, channels, width = thin_ref.shape
 
     @pl.when(pl.program_id(0) == 0)
     def _():
         thin_ref[...] = jnp.zeros(thin_ref.shape, jnp.float32)
 
     def analyse(group, carry):
-        coefficients(spec_ref, fwd_ref, coef_ref, group)
-        coefficients(grid_ref, inv_ref, out_ref, group)
+        spectra = channel_spectra(spec_ref, lat_dev, fields, 2 * channels, group)
+        legendre(spectra, fwd_ref[group], coef_ref, group)
+        legendre(grid_ref[:, group_rows(group), :], inv_ref[group], out_ref, group)
         return carry
 
     lax.fori_loop(0, groups, analyse, 0, unroll=steps(groups))
@@ -169,6 +195,7 @@
     count = degree.shape[0]
     lane = lax.broadcasted_iota(jnp.int32, (count, 128), 1) // lat
     me = me_ref[0]
+    me_wide = me_ref[1]
 
     def one_group(group, carry):
         found = ([], [])
@@ -184,7 +211,7 @@
                 shift = lax.rem((place - (at - block * per_tile)) * lat + 128, 128)
                 live = (degree >= order) & (order < M) & (degree < L) & (lane == place)
                 for table in range(2):
-                    both = [wire_ref[(2 * table + half) ^ me, source, :, columns] for half in range(2)]
+                    both = [wire_ref[(2 * table + half) ^ me, source ^ me_wide, :, columns] for half in range(2)]
                     moved = pltpu.roll(jnp.concatenate(both, axis=0), shift, 1)
                     tiles[table] = jnp.where(live, moved, tiles[table])
             for table in range(2):
@@ -227,28 +254,76 @@
         out_shape=[jax.ShapeDtypeStruct((groups, slots, lat_total * 8), jnp.float32)] * 2,
         compiler_params=pltpu.CompilerParams(vmem_limit_bytes=32 * 2**20),
         name="table_rows",
-    )(lax.axis_index("dp")[None], slot_of, wire, degrees[:, None], jnp.asarray(place, jnp.bfloat16))
+    )(jnp.stack([lax.axis_index("dp"), lax.axis_index("wide")]), slot_of, wire, degrees[:, None], jnp.asarray(place, jnp.bfloat16))
 
 
 def exchange(value, axis, count, bit):
     return lax.ppermute(value, axis, [(i, i ^ bit) for i in range(count)])
 
 
-def tables_to_degrees(forward_table, inverse_table, wide_count, degree_slots):
+def wire_kernel(degrees, me_ref, forward_ref, inverse_ref, wire_ref, turned_ref):
+    own, lat, order_count = forward_ref.shape
+    owners, half, lanes = wire_ref.shape
+    per_tile = 128 // lat
+    me = me_ref[0]
+
+    @pl.when(me < 2)
+    def _():
+        turned_ref[order_count:] = jnp.zeros((turned_ref.shape[0] - order_count, lanes), jnp.float32)
+        turned_ref[:order_count, : own * lat] = forward_ref[...].reshape(own * lat, order_count).T
+        if lanes > own * lat:
+            turned_ref[:order_count, own * lat :] = jnp.zeros(
+                (order_count, lanes - own * lat), jnp.float32
+            )
+
+    def forward_part(part):
+        for owner in range(owners):
+            first = owner * degrees + part * half
+            wire_ref[owner] = turned_ref[first : first + half, :]
+
+    def inverse_part(part):
+        lane = lax.broadcasted_iota(jnp.int32, (half, 128), 1) // lat
+        for owner in range(owners):
+            first = owner * degrees + part * half
+            rows = min(half, order_count - first)
+            for tile in range(lanes // 128):
+                value = jnp.zeros((rows, 128), jnp.float32)
+                for place in range(per_tile):
+                    slot = tile * per_tile + place
+                    if slot < own:
+                        found = inverse_ref[slot, first : first + rows, :]
+                        found = jnp.concatenate([found] * per_tile, axis=1)
+                        value = jnp.where(lane[:rows] == place, found, value)
+                columns = slice(tile * 128, tile * 128 + 128)
+                wire_ref[owner, :rows, columns] = value
+                if rows < half:
+                    wire_ref[owner, rows:, columns] = jnp.zeros((half - rows, 128), jnp.float32)
+
+    pl.when(me == 0)(functools.partial(forward_part, 0))
+    pl.when(me == 1)(functools.partial(forward_part, 1))
+    pl.when(me == 2)(functools.partial(inverse_part, 0))
+    pl.when(me == 3)(functools.partial(inverse_part, 1))
+
+
+def tables_to_degrees(forward_table, inverse_table, wide_count, degree_slots, beside):
     own, lat_total, order_count = forward_table.shape
     dp_count = lax.axis_size("dp")
     half = -(-degree_slots // 16) * 8
-    spare = ((0, 0), (0, 2 * half - degree_slots), (0, -own * lat_total % 128))
-
-    def rows(table):
-        table = jnp.pad(table.reshape(wide_count, degree_slots, own * lat_total), spare)
-        return table.reshape(wide_count, 2, half, table.shape[2])
-
-    wire = jnp.concatenate(
-        [rows(forward_table.transpose(2, 0, 1)), rows(inverse_table.transpose(1, 0, 2))], axis=1
-    )
-    wire = lax.dynamic_index_in_dim(wire, lax.axis_index("dp"), 1, keepdims=False)
-    wire = lax.all_to_all(wire, "wide", split_axis=0, concat_axis=0, tiled=True)
+    lanes = -(-own * lat_total // 128) * 128
+    wire = pl.pallas_call(
+        functools.partial(wire_kernel, degree_slots),
+        in_specs=[pl.BlockSpec(memory_space=pltpu.SMEM)]
+        + [pl.BlockSpec(memory_space=pltpu.VMEM)] * 2,
+        out_specs=pl.BlockSpec(memory_space=pltpu.VMEM),
+        out_shape=jax.ShapeDtypeStruct((wide_count, half, lanes), jnp.float32),
+        scratch_shapes=[pltpu.VMEM((order_count + 2 * half - degree_slots + 8, lanes), jnp.float32)],
+        compiler_params=pltpu.CompilerParams(vmem_limit_bytes=32 * 2**20),
+        name="table_wire",
+    )(lax.axis_index("dp")[None], forward_table, inverse_table)
+    me = lax.axis_index("wide")
+    pieces = [lax.dynamic_index_in_dim(wire, me ^ k, 0, keepdims=False) for k in range(wide_count)]
+    pieces = [pieces[0]] + [exchange(pieces[k], "wide", wide_count, k) for k in range(1, wide_count)]
+    wire, beside = lax.optimization_barrier((jnp.stack(pieces), beside))
     found = []
     for part, bits in ((wire[: wide_count // 2], (1, 2)), (wire[wide_count // 2 :], (2, 1))):
         by_index = {0: part}
@@ -257,45 +332,80 @@
             passed = exchange(jnp.stack([by_index[i] for i in names]), "dp", dp_count, bit)
             by_index.update({i ^ bit: passed[k] for k, i in enumerate(names)})
         found.append(jnp.stack([by_index[i] for i in range(4)]))
-    return jnp.concatenate(found, axis=1)
-
-
-def all_sum(rows):
-    dp_count, wide_count = lax.axis_size("dp"), lax.axis_size("wide")
-    if dp_count != 4 or wide_count & (wide_count - 1):
-        return lax.psum(rows, ("dp", "wide"))
+    return jnp.concatenate(found, axis=1), beside
+
+
+def reduce_halves(piece, bits):
     me = lax.axis_index("dp")
-    piece = rows
-    for bit in (1, 2):
+    for bit in bits:
         parts = piece.reshape((2, piece.shape[0] // 2) + piece.shape[1:])
         mine = (me & bit) // bit
         sent = lax.dynamic_index_in_dim(parts, 1 - mine, 0, keepdims=False)
         kept = lax.dynamic_index_in_dim(parts, mine, 0, keepdims=False)
-        piece = kept + exchange(sent, "dp", dp_count, bit)
+        piece = kept + exchange(sent, "dp", 4, bit)
+    return piece
+
+
+def gather_halves(piece, bits):
+    me = lax.axis_index("dp")
+    for bit in bits[::-1]:
+        other = exchange(piece, "dp", 4, bit)
+        low = me & bit == 0
+        piece = jnp.concatenate([jnp.where(low, piece, other), jnp.where(low, other, piece)], axis=0)
+    return piece
+
+
+def wide_sum(piece):
+    wide_count = lax.axis_size("wide")
     bit = 1
     while bit < wide_count:
         piece = piece + exchange(piece, "wide", wide_count, bit)
         bit *= 2
-    for bit in (2, 1):
-        other = exchange(piece, "dp", dp_count, bit)
-        mine = (me & bit) // bit == 0
-        piece = jnp.concatenate(
-            [jnp.where(mine, piece, other), jnp.where(mine, other, piece)], axis=0
-        )
     return piece
 
 
-def spectral_forward(spectra, fwd_rows, inv_rows, folded):
-    lat_total, order_count, thin = spectra.shape
+def by_bits():
+    wide_count = lax.axis_size("wide")
+    return lax.axis_size("dp") == 4 and wide_count & (wide_count - 1) == 0
+
+
+def all_sum(rows):
+    if not by_bits():
+        return lax.psum(rows, ("dp", "wide"))
+    return gather_halves(wide_sum(reduce_halves(rows, (1, 2))), (1, 2))
+
+
+def thin_sum(thin, gram):
+    def squares(piece):
+        product = jnp.einsum("cd,tdk->tck", gram, piece, precision=lax.Precision.HIGHEST)
+        return jnp.sum(piece * product)
+
+    pairs = thin.shape[0]
+    if not by_bits() or pairs % 4:
+        thin = lax.psum(thin, "dp")
+        return thin, lax.psum(squares(thin), "wide")
+    cut = pairs // 8 * 4
+    halved = [(reduce_halves(thin[:cut], (1, 2)), (1, 2)), (reduce_halves(thin[cut:], (2, 1)), (2, 1))]
+    total = jnp.broadcast_to(sum(squares(piece) for piece, _ in halved), (8, 128))
+    for bit in (1, 2):
+        total = total + exchange(total, "dp", 4, bit)
+    total = wide_sum(total)[0, 0]
+    return jnp.concatenate([gather_halves(piece, bits) for piece, bits in halved]), total
+
+
+def spectral_forward(spectra, fwd_rows, inv_rows, folded, lat_dev, fields):
+    devices, _, order_count, lanes = spectra.shape
+    lat_total = devices * lat_dev
     degrees, _, channels, width = folded.shape
+    thin = 2 * channels
     slots = fwd_rows.shape[1]
     size = order_chunk(order_count, lat_total, width)
     groups = size // 8
     return pl.pallas_call(
-        forward_kernel,
+        functools.partial(forward_kernel, lat_dev, fields),
         grid=(order_count // size,),
         in_specs=[
-            pl.BlockSpec((lat_total, size, thin), lambda i: (0, i, 0)),
+            pl.BlockSpec((devices, 2, size, lanes), lambda i: (0, 0, i, 0)),
             pl.BlockSpec((groups,) + fwd_rows.shape[1:], lambda i: (i, 0, 0)),
             pl.BlockSpec((groups,) + inv_rows.shape[1:], lambda i: (i, 0, 0)),
             pl.BlockSpec(folded.shape, lambda i: (0, 0, 0, 0)),
@@ -311,24 +421,27 @@
     )(spectra, fwd_rows, inv_rows, folded)
 
 
-def spectral_backward(grid_grad, spectra, fwd_rows, inv_rows, degrees, channels):
-    lat_total, order_count, thin = spectra.shape
+def spectral_backward(grid_grad, spectra, fwd_rows, inv_rows, degrees, channels, fields):
+    devices, _, order_count, lanes = spectra.shape
+    lat_total = grid_grad.shape[0]
+    lat_dev = lat_total // devices
+    thin = 2 * channels
     width = grid_grad.shape[2] // 2
     slots = fwd_rows.shape[1]
     size = order_chunk(order_count, lat_total, width)
     groups = size // 8
     table = pl.BlockSpec((groups,) + fwd_rows.shape[1:], lambda i: (i, 0, 0))
     return pl.pallas_call(
-        backward_kernel,
+        functools.partial(backward_kernel, degrees, lat_dev, fields),
         grid=(order_count // size,),
         in_specs=[
             pl.BlockSpec((lat_total, size, 2 * width), lambda i: (0, i, 0)),
-            pl.BlockSpec((lat_total, size, thin), lambda i: (0, i, 0)),
+            pl.BlockSpec((devices, 2, size, lanes), lambda i: (0, 0, i, 0)),
             table,
             table,
         ],
-        out_specs=pl.BlockSpec((degrees, 2, channels, width), lambda i: (0, 0, 0, 0)),
-        out_shape=jax.ShapeDtypeStruct((degrees, 2, channels, width), jnp.float32),
+        out_specs=pl.BlockSpec((slots, 2, channels, width), lambda i: (0, 0, 0, 0)),
+        out_shape=jax.ShapeDtypeStruct((slots, 2, channels, width), jnp.float32),
         scratch_shapes=[
             pltpu.VMEM((slots, size, thin), jnp.float32),
             pltpu.VMEM((slots, size, 2 * width), jnp.float32),
@@ -429,24 +542,17 @@
         [io_weight[0], enc_bias[None], jnp.zeros((spare, width), jnp.float32)], axis=0
     )
 
-    spectra = dot("caj,psj->pacs", fields, forward)
-    spectra = lax.all_gather(spectra, "wide", axis=0, tiled=False)
-    ones_row = forward.astype(np.float64).sum(axis=2).astype(np.float32)
-    spectra = jnp.concatenate(
-        [
-            spectra,
-            jnp.broadcast_to(ones_row[None, :, None, None, :], (wide_count, 2, lat_dev, 1, order_count)),
-            jnp.zeros((wide_count, 2, lat_dev, spare, order_count), jnp.float32),
-        ],
-        axis=3,
-    )
-    spectra = spectra.transpose(0, 2, 4, 1, 3).reshape(lat_total, order_count, 2 * thin_count)
+    lines = fields.transpose(1, 0, 2).reshape(lat_dev * channels, lon_count)
+    lines = jnp.pad(lines, ((0, -lines.shape[0] % 128), (0, 0)))
+    spectra = lax.all_gather(dot("rj,psj->psr", lines, forward), "wide", axis=0, tiled=False)
+
+    folded = dot("cd,tpdk->tpck", encoder, spectral_weight)
 
     my_degrees = lax.dynamic_slice_in_dim(degree_map, position * degree_slots, degree_slots)
     slot_of = jnp.argsort(order_map)
     slots = degree_slots + degree_slots % 2
-    if 128 % lat_total == 0 and lax.axis_size("dp") == 4 and wide_count % 2 == 0:
-        wire = tables_to_degrees(forward_table, inverse_table, wide_count, degree_slots)
+    if 128 % lat_total == 0 and lax.axis_size("dp") == 4 and wide_count == 8 and lat_total >= 8:
+        wire, folded = tables_to_degrees(forward_table, inverse_table, wide_count, degree_slots, folded)
         degrees = jnp.pad(my_degrees, (0, 2 * wire.shape[2] - degree_slots), constant_values=-1)
         own = forward_table.shape[0]
         fwd_rows, inv_rows = table_rows(wire, slot_of, degrees, own, lat_total, slots)
@@ -471,8 +577,7 @@
         fwd_rows = by_degree(fwd_masked.transpose(0, 3, 2, 1))
         inv_rows = by_degree(inv_masked.transpose(0, 2, 3, 1))
 
-    folded = dot("cd,tpdk->tpck", encoder, spectral_weight)
-    grid_coef = spectral_forward(spectra, fwd_rows, inv_rows, folded)
+    grid_coef = spectral_forward(spectra, fwd_rows, inv_rows, folded, lat_dev, channels)
     grid_coef = lax.psum_scatter(grid_coef, "wide", scatter_dimension=0, tiled=True)
     grid_coef = grid_coef.reshape(lat_dev, order_count, 2, width)
 
@@ -511,19 +616,18 @@
     flat = jnp.concatenate(flat, axis=0)
     flat = all_sum(jnp.pad(flat, ((0, -flat.shape[0] % 32), (0, 0))))
     grid_grad, flat = lax.optimization_barrier((grid_grad, flat))
-    thin = spectral_backward(grid_grad, spectra, fwd_rows, inv_rows, degree_slots, thin_count)
+    thin = spectral_backward(
+        grid_grad, spectra, fwd_rows, inv_rows, degree_slots, thin_count, channels
+    )
     at = 2 * hidden_units
     mlp_grad = flat[:at].reshape(2, width, hidden_units)
     decoder_grad = flat[at : at + channels]
     direct = flat[at + channels : at + 2 * channels]
     small = flat[at + 2 * channels :].reshape(-1)[:small_count]
-    encoder_grad = all_sum(dot("tpck,tpdk->cd", thin, spectral_weight))
-    thin = lax.psum(thin, "dp")
+    encoder_grad = all_sum(dot("tpck,tpdk->cd", thin[:degree_slots], spectral_weight))
     gram = jnp.einsum("ck,dk->cd", encoder, encoder, precision=lax.Precision.HIGHEST)
-    spectral_squares = jnp.sum(
-        thin * jnp.einsum("cd,tpdk->tpck", gram, thin, precision=lax.Precision.HIGHEST)
-    )
-    spectral_squares = lax.psum(spectral_squares, "wide")
+    thin, spectral_squares = thin_sum(thin.reshape(2 * slots, thin_count, width), gram)
+    thin = thin.reshape(slots, 2, thin_count, width)
     io_grad = jnp.stack([direct + encoder_grad[:channels], decoder_grad])
     bias_grad = jnp.concatenate([small[:width] + encoder_grad[channels], small[width:-2]])
     loss_sum, valid_weight = small[-2], small[-1]

time: 1080 us -> 1000 us (0.926)
  blocking collectives: 85 us -> 0 us
  starting transfers between devices: 29.7 us -> 48.9 us
  local copies, waits for them, and re-layouts: 67.3 us -> 51.2 us
    psum x1 -> x0, waiting for transfers between devices: 132 us -> none  [body(): thin = lax.psum(thin, 'dp')]
    ppermute x18 -> x38, waiting for transfers between devices: 141 us -> 230 us  [exchange(): return lax.ppermute(value, axis, [(i, i ^ bit) for i in range(count)])]
    all_to_all x1 -> x0, blocking collectives: 67.8 us -> none  [tables_to_degrees(): wire = lax.all_to_all(wire, 'wide', split_axis=0, concat_axis=0, tiled=True)]
    reduce_scatter x1, waiting for transfers between devices: 226 us -> 248 us  [body(): lax.psum_scatter(grid_coef, 'wide', scatter_dimension=0, tiled=True)]
    ppermute x18 -> x38, starting transfers between devices: 29.4 us -> 48.5 us  [exchange(): return lax.ppermute(value, axis, [(i, i ^ bit) for i in range(count)])]
    psum x1 -> x0, blocking collectives: 17.2 us -> none  [body(): spectral_squares = lax.psum(spectral_squares, 'wide')]
    reshape x4 -> x3, local copies, waits for them, and re-layouts: 18.5 us -> 2.72 us  [the longest x2 2.72 us: body(): lines = fields.transpose(1, 0, 2).reshape(lat_dev * channels, lon_count)]
    all_gather x1, waiting for transfers between devices: 59.7 us -> 74.3 us  [body(): grid_grad = lax.all_gather(grid_grad, 'wide', axis=0, tiled=True)]
  transfers between devices with their start and end apart: 22 -> 41, of which waited for: 20 -> 29; matrix products, arithmetic and copies ran while one was open for 8% -> 12% of each run, Pallas kernels for 1% -> 1%
where the time goes in v3:
time: 1000 us; the launch traced here: 992 us
  waiting for transfers between devices  552 us (55%)
  Pallas kernels  184 us (18%)
  matrix products  101 us (10%)
  local copies, waits for them, and re-layouts  51.2 us (5%)
  starting transfers between devices  48.9 us (5%)
  other arithmetic  34.6 us (3%)
  between operations  20.6 us (2%)
    reduce_scatter x1, waiting for transfers between devices, body(): lax.psum_scatter(grid_coef, 'wide', scatter_dimension=0, tiled=True)  248 us
    ppermute x38, waiting for transfers between devices, exchange(): return lax.ppermute(value, axis, [(i, i ^ bit) for i in range(count)])  230 us
    dot_general x16, matrix products, dot(): return jnp.einsum(spec, left, right, precision=HIGH)  97.1 us
    all_gather x1, waiting for transfers between devices, body(): grid_grad = lax.all_gather(grid_grad, 'wide', axis=0, tiled=True)  74.3 us
    pallas_call x1, Pallas kernels, spectral_forward(): pl.pallas_call(functools.partial(forward_kernel, lat_dev, fields), grid=(...  59.2 us
    pallas_call x1, Pallas kernels, spectral_adam(): pl.pallas_call(adam_kernel, grid=(degrees // size,), in_specs=[pl.BlockSp...  57.4 us
    pallas_call x1, Pallas kernels, spectral_backward(): pl.pallas_call(functools.partial(backward_kernel, degrees, lat_dev, field...  55.3 us
    ppermute x38, starting transfers between devices, exchange(): return lax.ppermute(value, axis, [(i, i ^ bit) for i in range(count)])  48.5 us
  transfers between devices with their start and end apart: 41, of which 29 were waited for; matrix products, arithmetic and copies ran while one was open for 12% of the time, Pallas kernels for 1%

profile of v3, /device:TPU:0, one launch (start us, length us, event | category | flops | bytes accessed | tf_op | source)
XLA Modules:
  0.0 992.4 jit_solution(971839325865965449)
XLA Ops:
  10.0 4.5 fusion.26
  14.6 6.4 copy.104.inverse_ref
  32.3 15.0 %convolution_bitcast_fusion.folded_ref = f32[45,2,80,256]{3,2,1,0:T(8,128)} fusion(f32[45,2,256,256]{3,2,1,0:T(8,128)} %weight_ref.1, f32[80,256]{1,0:T(8,128)S(1)} %maximum_maximum_fusion.1.encoder_ref), kind=kOutput, calls=%fused_computation.21 | convolution fusion | flops 2831155200 | bytes 31047680 | tf_op jit(solution)/shard_map/cd,tpdk->tpck/dot_general | solution.py:32
  58.1 6.7 collective-permute-done.5
  64.8 5.6 collective-permute-done.6
  76.4 12.4 %collective-permute-done.9 = f32[1,4,24,1536]{3,2,1,0:T(8,128)S(1)} collective-permute-done((f32[1,4,24,1536]{3,2,1,0:T(8,128)S(1)}, f32[1,4,24,1536]{3,2,1,0:T(8,128)S(1)}, u32[]{:S(2)}, u32[]{:S(2)}) %collective-permute-start.9) | collective-permute-done | bytes 589856 | tf_op jit(solution)/shard_map/ppermute | solution.py:261
  98.9 19.0 %collective-permute-done.10 = f32[2,4,24,1536]{3,2,1,0:T(8,128)} collective-permute-done((f32[2,4,24,1536]{3,2,1,0:T(8,128)}, f32[2,4,24,1536]{3,2,1,0:T(8,128)}, u32[]{:S(2)}, u32[]{:S(2)}) %collective-permute-start.10) | collective-permute-done | bytes 1179680 | tf_op jit(solution)/shard_map/ppermute | solution.py:261
  121.9 11.5 %table_rows.1 = (f32[45,46,256]{2,1,0:T(8,128)S(1)}, f32[45,46,256]{2,1,0:T(8,128)S(1)}) custom-call(s32[2]{0:T(128)S(1)} %pad_add_fusion.me_ref, s32[360]{0:T(512)S(1)} %get-tuple-element.30.slot_ref, f32[4,8,24,1536]{3,2,1,0:T(8,128)S(1)} %maximum_maximum_fusion.wire_ref, s32[48,1]{1,0:T(8,128)S(1)} %copy.105.degree_ref, bf16[256,256]{1,0:T(8,128)(2,1)S(1)} %copy-done.4), custom_call_target="tpu_custom_call" | custom-call | tf_op jit(solution)/shard_map/table_rows/pallas_call | solution.py:249
  136.1 59.2 %spectral_forward.1 = f32[32,360,512]{2,1,0:T(8,128)} custom-call(f32[8,2,360,384]{3,2,1,0:T(8,128)} %bitcast.213, f32[45,46,256]{2,1,0:T(8,128)} %copy-done.1, f32[45,46,256]{2,1,0:T(8,128)} %copy-done.2, f32[45,2,80,256]{3,2,1,0:T(8,128)} %convolution_bitcast_fusion.folded_ref), custom_call_target="tpu_custom_call" | custom-call | tf_op jit(solution)/shard_map/spectral_forward/pallas_call | solution.py:404
  199.5 247.9 %reduce-scatter.2.cloned.1.call-done = f32[4,360,512]{2,1,0:T(8,128)} async-done(((f32[32,360,512]{2,1,0:T(8,128)}), f32[4,360,512]{2,1,0:T(8,128)}) %reduce-scatter.2.cloned.1.call-update) | async-done | bytes 2949136 | tf_op jit(solution)/shard_map/reduce_scatter | solution.py:581
  447.4 7.2 bitcast_add_fusion
  457.2 4.5 add_add_fusion
  466.0 10.1 %fusion.96 = (f32[512]{0:T(512)}, f32[4,720,512]{2,1,0:T(8,128)S(1)}) fusion(f32[4,720,512]{2,1,0:T(8,128)S(1)} %fusion.41, f32[512]{0:T(512)S(1)} %slice.101, f32[4,720,256]{2,1,0:T(8,128)S(1)} %get-tuple-element.152, f32[2,256,512]{2,1,0:T(8,128)S(1)} %copy-done.26), kind=kOutput, calls=%fused_computation.188 | convolution fusion | flops 2295889408 | bytes 15273984 | tf_op jit(solution)/shard_map/ajk,kh->ajh/dot_general | solution.py:32
  485.3 6.1 convolution_bitcast_fusion.3
  492.7 10.6 %fusion.25 = f32[256,512]{1,0:T(8,128)} fusion(f32[4,720,256]{2,1,0:T(8,128)} %copy-done.12, f32[4,720,512]{2,1,0:T(8,128)} %copy-done.25, f32[512]{0:T(512)} %copy-done.45), kind=kOutput, calls=%fused_computation.41 | convolution fusion | flops 2278195200 | bytes 9373696 | tf_op jit(solution)/shard_map/ajk,ajh->kh/dot_general | solution.py:32
  521.4 11.7 %collective-permute-done.11 = f32[592,256]{1,0:T(8,128)S(1)} collective-permute-done((f32[592,256]{1,0:T(8,128)S(1)}, f32[592,256]{1,0:T(8,128)S(1)}, u32[]{:S(2)}, u32[]{:S(2)}) %collective-permute-start.11) | collective-permute-done | bytes 606240 | tf_op jit(solution)/shard_map/ppermute | solution.py:261
  534.9 5.3 collective-permute-done.12
  541.9 4.7 collective-permute-start.14
  546.7 28.8 %collective-permute-done.14 = f32[296,256]{1,0:T(8,128)S(1)} collective-permute-done((f32[296,256]{1,0:T(8,128)S(1)}, f32[296,256]{1,0:T(8,128)S(1)}, u32[]{:S(2)}, u32[]{:S(2)}) %collective-permute-start.14) | collective-permute-done | bytes 303136 | tf_op jit(solution)/shard_map/ppermute | solution.py:261
  575.5 30.9 %collective-permute-done.15 = f32[296,256]{1,0:T(8,128)S(1)} collective-permute-done((f32[296,256]{1,0:T(8,128)S(1)}, f32[296,256]{1,0:T(8,128)S(1)}, u32[]{:S(2)}, u32[]{:S(2)}) %collective-permute-start.15) | collective-permute-done | bytes 303136 | tf_op jit(solution)/shard_map/ppermute | solution.py:261
  608.2 6.8 collective-permute-done.16
  616.6 12.6 %collective-permute-done.17 = f32[592,256]{1,0:T(8,128)S(1)} collective-permute-done((f32[592,256]{1,0:T(8,128)S(1)}, f32[592,256]{1,0:T(8,128)S(1)}, u32[]{:S(2)}, u32[]{:S(2)}) %collective-permute-start.17) | collective-permute-done | bytes 606240 | tf_op jit(solution)/shard_map/ppermute | solution.py:261
  629.4 74.3 %all-gather.4.cloned.1.call-done.grid_ref = f32[32,360,512]{2,1,0:T(8,128)} async-done(((f32[4,360,512]{2,1,0:T(8,128)}), f32[32,360,512]{2,1,0:T(8,128)}) %all-gather.4.cloned.1.call-update) | async-done | bytes 23592976 | tf_op jit(solution)/shard_map/all_gather | solution.py:608
  703.7 55.3 %spectral_backward.1 = f32[46,2,80,256]{3,2,1,0:T(8,128)} custom-call(f32[32,360,512]{2,1,0:T(8,128)} %all-gather.4.cloned.1.call-done.grid_ref, f32[8,2,360,384]{3,2,1,0:T(8,128)} %bitcast.214, f32[45,46,256]{2,1,0:T(8,128)} %copy-done.1, f32[45,46,256]{2,1,0:T(8,128)} %copy-done.2), custom_call_target="tpu_custom_call" | custom-call | tf_op jit(solution)/shard_map/spectral_backward/pallas_call | solution.py:434
  770.9 16.7 %fusion = f32[80,256,1,1]{1,0,3,2:T(8,128)S(1)} fusion(f32[45,2,256,256]{3,2,1,0:T(8,128)} %weight_ref.1, f32[46,2,80,256]{3,2,1,0:T(8,128)} %spectral_backward.1), kind=kOutput, calls=%fused_computation | convolution fusion | flops 2831155200 | bytes 31047680 | tf_op jit(solution)/shard_map/tpck,tpdk->cd/dot_general | solution.py:32
  788.3 20.8 %collective-permute-done.27 = f32[40,256]{1,0:T(8,128)S(1)} collective-permute-done((f32[40,256]{1,0:T(8,128)S(1)}, f32[40,256]{1,0:T(8,128)S(1)}, u32[]{:S(2)}, u32[]{:S(2)}) %collective-permute-start.27) | collective-permute-done | bytes 40992 | tf_op jit(solution)/shard_map/ppermute | solution.py:261
  830.3 12.1 %collective-permute-done.32 = f32[20,256]{1,0:T(8,128)S(1)} collective-permute-done((f32[20,256]{1,0:T(8,128)S(1)}, f32[20,256]{1,0:T(8,128)S(1)}, u32[]{:S(2)}, u32[]{:S(2)}) %collective-permute-start.32) | collective-permute-done | bytes 20512 | tf_op jit(solution)/shard_map/ppermute | solution.py:261
  856.7 8.8 collective-permute-done.23
  868.9 9.5 collective-permute-done.36
  904.7 10.4 %collective-permute-done.35 = f32[22,80,256]{2,1,0:T(8,128)} collective-permute-done((f32[22,80,256]{2,1,0:T(8,128)}, f32[22,80,256]{2,1,0:T(8,128)}, u32[]{:S(2)}, u32[]{:S(2)}) %collective-permute-start.35) | collective-permute-done | bytes 1802272 | tf_op jit(solution)/shard_map/ppermute | solution.py:261
  916.9 5.2 collective-permute-done.37
  927.2 57.4 %spectral_adam.1 = (f32[45,2,256,256]{3,2,1,0:T(8,128)}, f32[45,2,256,256]{3,2,1,0:T(8,128)}, f32[45,2,256,256]{3,2,1,0:T(8,128)}, bf16[45,2,256,256]{3,2,1,0:T(8,128)(2,1)}) custom-call(f32[1]{0:T(128)} %bitcast.89.factor_ref, f32[80,256]{1,0:T(8,128)S(1)} %maximum_maximum_fusion.1.encoder_ref, f32[46,2,80,256]{3,2,1,0:T(8,128)} %bitcast.215, ...), custom_call_target="tpu_custom_call" | custom-call | tf_op jit(solution)/shard_map/spectral_adam/pallas_call | solution.py:459
  (276 shorter events, 173.4 us)
Async XLA Ops:
  7.2 128.9 %all-gather.6.cloned.1.call-start = ((), (), s32[]{:S(2)}) async-start(), calls=%async_computation.3 | async-start | bytes 9953280 | tf_op jit(solution)/shard_map/all_gather | solution.py:547
  14.5 432.9 %reduce-scatter.2.cloned.1.call-start = ((), (), s32[]{:S(2)}) async-start(), calls=%async_computation.1 | async-start | bytes 26542080 | tf_op jit(solution)/shard_map/reduce_scatter | solution.py:581
  25.6 21.6 %collective-permute-start = (f32[24,1536]{1,0:T(8,128)S(1)}, f32[24,1536]{1,0:T(8,128)S(1)}, u32[]{:S(2)}, u32[]{:S(2)}) collective-permute-start(f32[24,1536]{1,0:T(8,128)S(1)} %get-tuple-element.135), channel_id=1, source_target_pairs={{0,1},{1,0},{2,3},{3,2},{4,5},{5,4},{6,7},{7,6},{8,9},{9,8},{10,11... | collective-permute-start | bytes 442376 | tf_op jit(solution)/shard_map/ppermute | solution.py:261
  26.2 24.6 %collective-permute-start.1 = (f32[24,1536]{1,0:T(8,128)S(1)}, f32[24,1536]{1,0:T(8,128)S(1)}, u32[]{:S(2)}, u32[]{:S(2)}) collective-permute-start(f32[24,1536]{1,0:T(8,128)S(1)} %get-tuple-element.134), channel_id=1, source_target_pairs={{0,2},{1,3},{2,0},{3,1},{4,6},{5,7},{6,4},{7,5},{8,10},{9,11},{10,... | collective-permute-start | bytes 442376 | tf_op jit(solution)/shard_map/ppermute | solution.py:261
  29.2 26.0 %collective-permute-start.2 = (f32[24,1536]{1,0:T(8,128)S(1)}, f32[24,1536]{1,0:T(8,128)S(1)}, u32[]{:S(2)}, u32[]{:S(2)}) collective-permute-start(f32[24,1536]{1,0:T(8,128)S(1)} %get-tuple-element.133), channel_id=1, source_target_pairs={{0,3},{1,2},{2,1},{3,0},{4,7},{5,6},{6,5},{7,4},{8,11},{9,10},{10,... | collective-permute-start | bytes 442376 | tf_op jit(solution)/shard_map/ppermute | solution.py:261
  29.3 25.9 %collective-permute-start.3 = (f32[24,1536]{1,0:T(8,128)S(1)}, f32[24,1536]{1,0:T(8,128)S(1)}, u32[]{:S(2)}, u32[]{:S(2)}) collective-permute-start(f32[24,1536]{1,0:T(8,128)S(1)} %get-tuple-element.132), channel_id=1, source_target_pairs={{0,4},{1,5},{2,6},{3,7},{4,0},{5,1},{6,2},{7,3},{8,12},{9,13},{10,... | collective-permute-start | bytes 442376 | tf_op jit(solution)/shard_map/ppermute | solution.py:261
  32.1 26.1 %collective-permute-start.4 = (f32[24,1536]{1,0:T(8,128)S(1)}, f32[24,1536]{1,0:T(8,128)S(1)}, u32[]{:S(2)}, u32[]{:S(2)}) collective-permute-start(f32[24,1536]{1,0:T(8,128)S(1)} %get-tuple-element.131), channel_id=1, source_target_pairs={{0,5},{1,4},{2,7},{3,6},{4,1},{5,0},{6,3},{7,2},{8,13},{9,12},{10,... | collective-permute-start | bytes 442376 | tf_op jit(solution)/shard_map/ppermute | solution.py:261
  47.2 17.6 %collective-permute-start.5 = (f32[24,1536]{1,0:T(8,128)S(1)}, f32[24,1536]{1,0:T(8,128)S(1)}, u32[]{:S(2)}, u32[]{:S(2)}) collective-permute-start(f32[24,1536]{1,0:T(8,128)S(1)} %get-tuple-element.130), channel_id=1, source_target_pairs={{0,6},{1,7},{2,4},{3,5},{4,2},{5,3},{6,0},{7,1},{8,14},{9,15},{10,... | collective-permute-start | bytes 442376 | tf_op jit(solution)/shard_map/ppermute | solution.py:261
  50.8 19.7 %collective-permute-start.6 = (f32[24,1536]{1,0:T(8,128)S(1)}, f32[24,1536]{1,0:T(8,128)S(1)}, u32[]{:S(2)}, u32[]{:S(2)}) collective-permute-start(f32[24,1536]{1,0:T(8,128)S(1)} %get-tuple-element.129), channel_id=1, source_target_pairs={{0,7},{1,6},{2,5},{3,4},{4,3},{5,2},{6,1},{7,0},{8,15},{9,14},{10,... | collective-permute-start | bytes 442376 | tf_op jit(solution)/shard_map/ppermute | solution.py:261
  70.6 18.1 %collective-permute-start.9 = (f32[1,4,24,1536]{3,2,1,0:T(8,128)S(1)}, f32[1,4,24,1536]{3,2,1,0:T(8,128)S(1)}, u32[]{:S(2)}, u32[]{:S(2)}) collective-permute-start(f32[1,4,24,1536]{3,2,1,0:T(8,128)S(1)} %get-tuple-element.126), channel_id=1, source_target_pairs={{0,16},{8,24},{16,0},{24,8},{1,17},{9,25},{17,1},{25,9},{2,18},{10... | collective-permute-start | bytes 1769480 | tf_op jit(solution)/shard_map/ppermute | solution.py:261
  74.9 16.5 %collective-permute-start.7 = (f32[1,4,24,1536]{3,2,1,0:T(8,128)S(1)}, f32[1,4,24,1536]{3,2,1,0:T(8,128)S(1)}, u32[]{:S(2)}, u32[]{:S(2)}) collective-permute-start(f32[1,4,24,1536]{3,2,1,0:T(8,128)S(1)} %get-tuple-element.125), channel_id=1, source_target_pairs={{0,8},{8,0},{16,24},{24,16},{1,9},{9,1},{17,25},{25,17},{2,10},{10... | collective-permute-start | bytes 1769480 | tf_op jit(solution)/shard_map/ppermute | solution.py:261
  89.8 28.1 %collective-permute-start.10 = (f32[2,4,24,1536]{3,2,1,0:T(8,128)}, f32[2,4,24,1536]{3,2,1,0:T(8,128)}, u32[]{:S(2)}, u32[]{:S(2)}) collective-permute-start(f32[2,4,24,1536]{3,2,1,0:T(8,128)} %pad_maximum_fusion.5), channel_id=1, source_target_pairs={{0,8},{8,0},{16,24},{24,16},{1,9},{9,1},{17,25},{25,17},{2,10},{10... | collective-permute-start | bytes 3538952 | tf_op jit(solution)/shard_map/ppermute | solution.py:261
  92.4 27.8 %collective-permute-start.8 = (f32[2,4,24,1536]{3,2,1,0:T(8,128)}, f32[2,4,24,1536]{3,2,1,0:T(8,128)}, u32[]{:S(2)}, u32[]{:S(2)}) collective-permute-start(f32[2,4,24,1536]{3,2,1,0:T(8,128)} %pad_maximum_fusion.4), channel_id=1, source_target_pairs={{0,16},{8,24},{16,0},{24,8},{1,17},{9,25},{17,1},{25,9},{2,18},{10... | collective-permute-start | bytes 3538952 | tf_op jit(solution)/shard_map/ppermute | solution.py:261
  195.3 508.4 %all-gather.4.cloned.1.call-start = ((), (), s32[]{:S(2)}) async-start(), calls=%async_computation.2 | async-start | bytes 26542080 | tf_op jit(solution)/shard_map/all_gather | solution.py:608
  520.0 13.2 %collective-permute-start.11 = (f32[592,256]{1,0:T(8,128)S(1)}, f32[592,256]{1,0:T(8,128)S(1)}, u32[]{:S(2)}, u32[]{:S(2)}) collective-permute-start(f32[592,256]{1,0:T(8,128)S(1)} %dynamic-slice_bitcast_fusion.4), channel_id=1, source_target_pairs={{0,8},{8,0},{16,24},{24,16},{1,9},{9,1},{17,25},{25,17},{2,10},{10... | collective-permute-start | bytes 1818632 | tf_op jit(solution)/shard_map/ppermute | solution.py:261
  541.9 33.5 %collective-permute-start.14 = (f32[296,256]{1,0:T(8,128)S(1)}, f32[296,256]{1,0:T(8,128)S(1)}, u32[]{:S(2)}, u32[]{:S(2)}) collective-permute-start(f32[296,256]{1,0:T(8,128)S(1)} %add.297), channel_id=1, source_target_pairs={{0,2},{1,3},{2,0},{3,1},{4,6},{5,7},{6,4},{7,5},{8,10},{9,11},{10,... | collective-permute-start | bytes 909320 | tf_op jit(solution)/shard_map/ppermute | solution.py:261
  575.5 31.0 %collective-permute-start.15 = (f32[296,256]{1,0:T(8,128)S(1)}, f32[296,256]{1,0:T(8,128)S(1)}, u32[]{:S(2)}, u32[]{:S(2)}) collective-permute-start(f32[296,256]{1,0:T(8,128)S(1)} %add.298), channel_id=1, source_target_pairs={{0,4},{1,5},{2,6},{3,7},{4,0},{5,1},{6,2},{7,3},{8,12},{9,13},{10,... | collective-permute-start | bytes 909320 | tf_op jit(solution)/shard_map/ppermute | solution.py:261
  606.5 8.5 collective-permute-start.16
  615.1 14.1 %collective-permute-start.17 = (f32[592,256]{1,0:T(8,128)S(1)}, f32[592,256]{1,0:T(8,128)S(1)}, u32[]{:S(2)}, u32[]{:S(2)}) collective-permute-start(f32[592,256]{1,0:T(8,128)S(1)} %pad_maximum_fusion.6), channel_id=1, source_target_pairs={{0,8},{8,0},{16,24},{24,16},{1,9},{9,1},{17,25},{25,17},{2,10},{10... | collective-permute-start | bytes 1818632 | tf_op jit(solution)/shard_map/ppermute | solution.py:261
  766.5 49.6 %collective-permute-start.18 = (f32[22,80,256]{2,1,0:T(8,128)}, f32[22,80,256]{2,1,0:T(8,128)}, u32[]{:S(2)}, u32[]{:S(2)}) collective-permute-start(f32[22,80,256]{2,1,0:T(8,128)} %dynamic-slice_bitcast_fusion.1), channel_id=1, source_target_pairs={{0,8},{8,0},{16,24},{24,16},{1,9},{9,1},{17,25},{25,17},{2,10},{10... | collective-permute-start | bytes 5406728 | tf_op jit(solution)/shard_map/ppermute | solution.py:261
  769.4 51.8 %collective-permute-start.20 = (f32[24,80,256]{2,1,0:T(8,128)}, f32[24,80,256]{2,1,0:T(8,128)S(1)}, u32[]{:S(2)}, u32[]{:S(2)}) collective-permute-start(f32[24,80,256]{2,1,0:T(8,128)} %dynamic-slice_bitcast_fusion), channel_id=1, source_target_pairs={{0,16},{8,24},{16,0},{24,8},{1,17},{9,25},{17,1},{25,9},{2,18},{10... | collective-permute-start | bytes 5898248 | tf_op jit(solution)/shard_map/ppermute | solution.py:261
  787.7 21.5 %collective-permute-start.27 = (f32[40,256]{1,0:T(8,128)S(1)}, f32[40,256]{1,0:T(8,128)S(1)}, u32[]{:S(2)}, u32[]{:S(2)}) collective-permute-start(f32[40,256]{1,0:T(8,128)S(1)} %dynamic-slice_bitcast_fusion.13), channel_id=1, source_target_pairs={{0,8},{8,0},{16,24},{24,16},{1,9},{9,1},{17,25},{25,17},{2,10},{10... | collective-permute-start | bytes 122888 | tf_op jit(solution)/shard_map/ppermute | solution.py:261
  816.1 7.6 collective-permute-start.30
  819.7 22.8 %collective-permute-start.19 = (f32[11,80,256]{2,1,0:T(8,128)}, f32[11,80,256]{2,1,0:T(8,128)}, u32[]{:S(2)}, u32[]{:S(2)}) collective-permute-start(f32[11,80,256]{2,1,0:T(8,128)} %dynamic-slice_bitcast_fusion.3), channel_id=1, source_target_pairs={{0,16},{8,24},{16,0},{24,8},{1,17},{9,25},{17,1},{25,9},{2,18},{10... | collective-permute-start | bytes 2703368 | tf_op jit(solution)/shard_map/ppermute | solution.py:261
  822.8 24.4 %collective-permute-start.21 = (f32[12,80,256]{2,1,0:T(8,128)S(1)}, f32[12,80,256]{2,1,0:T(8,128)}, u32[]{:S(2)}, u32[]{:S(2)}) collective-permute-start(f32[12,80,256]{2,1,0:T(8,128)S(1)} %dynamic-slice_bitcast_fusion.2), channel_id=1, source_target_pairs={{0,8},{8,0},{16,24},{24,16},{1,9},{9,1},{17,25},{25,17},{2,10},{10... | collective-permute-start | bytes 2949128 | tf_op jit(solution)/shard_map/ppermute | solution.py:261
  828.5 14.0 %collective-permute-start.32 = (f32[20,256]{1,0:T(8,128)S(1)}, f32[20,256]{1,0:T(8,128)S(1)}, u32[]{:S(2)}, u32[]{:S(2)}) collective-permute-start(f32[20,256]{1,0:T(8,128)S(1)} %add.314), channel_id=1, source_target_pairs={{0,16},{8,24},{16,0},{24,8},{1,17},{9,25},{17,1},{25,9},{2,18},{10... | collective-permute-start | bytes 61448 | tf_op jit(solution)/shard_map/ppermute | solution.py:261
  844.0 21.5 %collective-permute-start.34 = (f32[11,80,256]{2,1,0:T(8,128)S(1)}, f32[11,80,256]{2,1,0:T(8,128)}, u32[]{:S(2)}, u32[]{:S(2)}) collective-permute-start(f32[11,80,256]{2,1,0:T(8,128)S(1)} %bitcast_add_fusion.4), channel_id=1, source_target_pairs={{0,16},{8,24},{16,0},{24,8},{1,17},{9,25},{17,1},{25,9},{2,18},{10... | collective-permute-start | bytes 2703368 | tf_op jit(solution)/shard_map/ppermute | solution.py:261
  853.7 24.7 %collective-permute-start.36 = (f32[12,80,256]{2,1,0:T(8,128)S(1)}, f32[12,80,256]{2,1,0:T(8,128)S(1)}, u32[]{:S(2)}, u32[]{:S(2)}) collective-permute-start(f32[12,80,256]{2,1,0:T(8,128)S(1)} %bitcast_add_fusion.3), channel_id=1, source_target_pairs={{0,8},{8,0},{16,24},{24,16},{1,9},{9,1},{17,25},{25,17},{2,10},{10... | collective-permute-start | bytes 2949128 | tf_op jit(solution)/shard_map/ppermute | solution.py:261
  855.2 10.3 %collective-permute-start.23 = (f32[8,128]{1,0:T(8,128)S(1)}, f32[8,128]{1,0:T(8,128)S(1)}, u32[]{:S(2)}, u32[]{:S(2)}) collective-permute-start(f32[8,128]{1,0:T(8,128)S(1)} %broadcast_add_fusion), channel_id=1, source_target_pairs={{0,16},{8,24},{16,0},{24,8},{1,17},{9,25},{17,1},{25,9},{2,18},{10... | collective-permute-start | bytes 12296 | tf_op jit(solution)/shard_map/ppermute | solution.py:261
  865.5 16.0 %collective-permute-start.24 = (f32[8,128]{1,0:T(8,128)S(1)}, f32[8,128]{1,0:T(8,128)S(1)}, u32[]{:S(2)}, u32[]{:S(2)}) collective-permute-start(f32[8,128]{1,0:T(8,128)S(1)} %fusion.117), channel_id=1, source_target_pairs={{0,1},{1,0},{2,3},{3,2},{4,5},{5,4},{6,7},{7,6},{8,9},{9,8},{10,11... | collective-permute-start | bytes 12296 | tf_op jit(solution)/shard_map/ppermute | solution.py:261
  868.3 46.8 %collective-permute-start.35 = (f32[22,80,256]{2,1,0:T(8,128)}, f32[22,80,256]{2,1,0:T(8,128)}, u32[]{:S(2)}, u32[]{:S(2)}) collective-permute-start(f32[22,80,256]{2,1,0:T(8,128)} %pad_maximum_fusion.2), channel_id=1, source_target_pairs={{0,8},{8,0},{16,24},{24,16},{1,9},{9,1},{17,25},{25,17},{2,10},{10... | collective-permute-start | bytes 5406728 | tf_op jit(solution)/shard_map/ppermute | solution.py:261
  880.9 41.1 %collective-permute-start.37 = (f32[24,80,256]{2,1,0:T(8,128)}, f32[24,80,256]{2,1,0:T(8,128)}, u32[]{:S(2)}, u32[]{:S(2)}) collective-permute-start(f32[24,80,256]{2,1,0:T(8,128)} %pad_maximum_fusion.1), channel_id=1, source_target_pairs={{0,16},{8,24},{16,0},{24,8},{1,17},{9,25},{17,1},{25,9},{2,18},{10... | collective-permute-start | bytes 5898248 | tf_op jit(solution)/shard_map/ppermute | solution.py:261
  (56 other events, 1390.5 us)
Sparse Core Ops, SparseCore 0:
  14.6 113.4 all-gather.5
  195.5 251.8 reduce-scatter.1
  485.4 218.2 all-gather.3

commit v4 on v3

--- a/solution.py
+++ b/solution.py
@@ -80,9 +80,8 @@
 
 
 def channel_spectra(spec_ref, lat_dev, channels, thin, group):
-    devices, _, size, lanes = spec_ref.shape
-    real = spec_ref[:, 0, group_rows(group), :].reshape(devices * 8, lanes)
-    imag = spec_ref[:, 1, group_rows(group), :].reshape(devices * 8, lanes)
+    devices, size, lanes = spec_ref.shape
+    spectra = spec_ref[:, group_rows(group), :].reshape(devices * 8, lanes)
     lane = lax.broadcasted_iota(jnp.int32, (devices * 8, lanes), 1)
     order = lax.broadcasted_iota(jnp.int32, (devices * 8, lanes), 0) & 7
     order += pl.program_id(0) * size + group * 8
@@ -90,9 +89,10 @@
     half = thin // 2
     rows = []
     for row in range(lat_dev):
-        base = row * channels
-        left = pltpu.roll(real, (lanes - base) % lanes, 1) if base else real
-        right = pltpu.roll(imag, (half - base) % lanes, 1)
+        real = row * channels
+        imag = (lat_dev + row) * channels
+        left = pltpu.roll(spectra, (lanes - real) % lanes, 1) if row else spectra
+        right = pltpu.roll(spectra, (half - imag) % lanes, 1)
         value = jnp.where((lane >= half) & (lane < half + channels), right, ones)
         value = jnp.where(lane < channels, left, value)
         rows.append(value[:, :thin].reshape(devices, 8, thin))
@@ -165,15 +165,16 @@
     lax.fori_loop(0, degrees, product, 0, unroll=steps(degrees))
 
 
-def adam_kernel(
-    factor_ref, encoder_ref, thin_ref, weight_ref, first_ref, second_ref,
-    weight_out, first_out, second_out, low_out,
-):
+def adam_kernel(first_steps, block_ref, thin_block_ref, factor_ref, encoder_ref, *refs):
+    one_ref, two_ref, weight_ref, first_ref, second_ref = refs[:5]
+    weight_out, first_out, second_out, low_out = refs[-4:]
     factor = factor_ref[0]
+    in_one = pl.program_id(0) < first_steps
     encoder_high, encoder_low = halves(encoder_ref[...])
     left = jnp.concatenate([encoder_high, encoder_high, encoder_low], axis=0)
-    for degree, part in np.ndindex(thin_ref.shape[:2]):
-        high, low = halves(thin_ref[degree, part] * factor)
+    for degree, part in np.ndindex(one_ref.shape[:2]):
+        thin = jnp.where(in_one, one_ref[degree, part], two_ref[degree, part])
+        high, low = halves(thin * factor)
         right = jnp.concatenate([high, low, high], axis=0)
         gradient = lax.dot_general(
             left, right, (((0,), (0,)), ((), ())), preferred_element_type=jnp.float32
@@ -346,12 +347,15 @@
     return piece
 
 
+def gather_half(piece, bit):
+    other = exchange(piece, "dp", 4, bit)
+    low = lax.axis_index("dp") & bit == 0
+    return jnp.concatenate([jnp.where(low, piece, other), jnp.where(low, other, piece)], axis=0)
+
+
 def gather_halves(piece, bits):
-    me = lax.axis_index("dp")
     for bit in bits[::-1]:
-        other = exchange(piece, "dp", 4, bit)
-        low = me & bit == 0
-        piece = jnp.concatenate([jnp.where(low, piece, other), jnp.where(low, other, piece)], axis=0)
+        piece = gather_half(piece, bit)
     return piece
 
 
@@ -375,26 +379,34 @@
     return gather_halves(wide_sum(reduce_halves(rows, (1, 2))), (1, 2))
 
 
-def thin_sum(thin, gram):
+def thin_sum(thin, gram, cut):
     def squares(piece):
         product = jnp.einsum("cd,tdk->tck", gram, piece, precision=lax.Precision.HIGHEST)
         return jnp.sum(piece * product)
 
-    pairs = thin.shape[0]
-    if not by_bits() or pairs % 4:
+    me = lax.axis_index("dp")
+    if not by_bits():
         thin = lax.psum(thin, "dp")
-        return thin, lax.psum(squares(thin), "wide")
-    cut = pairs // 8 * 4
-    halved = [(reduce_halves(thin[:cut], (1, 2)), (1, 2)), (reduce_halves(thin[cut:], (2, 1)), (2, 1))]
-    total = jnp.broadcast_to(sum(squares(piece) for piece, _ in halved), (8, 128))
+        parts = []
+        for part in (thin[:cut], thin[cut:]):
+            middle = part.shape[0] // 2
+            parts.append((part[:middle], part[middle:], True))
+        return parts, lax.psum(squares(thin), "wide")
+    one, two = reduce_halves(thin[:cut], (1, 2)), reduce_halves(thin[cut:], (2, 1))
+    total = jnp.broadcast_to(squares(one) + squares(two), (8, 128))
     for bit in (1, 2):
         total = total + exchange(total, "dp", 4, bit)
     total = wide_sum(total)[0, 0]
-    return jnp.concatenate([gather_halves(piece, bits) for piece, bits in halved]), total
+    one, two = gather_half(one, 2), gather_half(two, 1)
+    parts = [
+        (one, exchange(one, "dp", 4, 1), me & 1 == 0),
+        (two, exchange(two, "dp", 4, 2), me & 2 == 0),
+    ]
+    return parts, total
 
 
 def spectral_forward(spectra, fwd_rows, inv_rows, folded, lat_dev, fields):
-    devices, _, order_count, lanes = spectra.shape
+    devices, order_count, lanes = spectra.shape
     lat_total = devices * lat_dev
     degrees, _, channels, width = folded.shape
     thin = 2 * channels
@@ -405,7 +417,7 @@
         functools.partial(forward_kernel, lat_dev, fields),
         grid=(order_count // size,),
         in_specs=[
-            pl.BlockSpec((devices, 2, size, lanes), lambda i: (0, 0, i, 0)),
+            pl.BlockSpec((devices, size, lanes), lambda i: (0, i, 0)),
             pl.BlockSpec((groups,) + fwd_rows.shape[1:], lambda i: (i, 0, 0)),
             pl.BlockSpec((groups,) + inv_rows.shape[1:], lambda i: (i, 0, 0)),
             pl.BlockSpec(folded.shape, lambda i: (0, 0, 0, 0)),
@@ -422,10 +434,12 @@
 
 
 def spectral_backward(grid_grad, spectra, fwd_rows, inv_rows, degrees, channels, fields):
-    devices, _, order_count, lanes = spectra.shape
+    devices, order_count, lanes = spectra.shape
     lat_total = grid_grad.shape[0]
     lat_dev = lat_total // devices
     thin = 2 * channels
+    block, first_steps, second_steps = adam_split(degrees)
+    thin_slots = 2 * block * (first_steps + second_steps)
     width = grid_grad.shape[2] // 2
     slots = fwd_rows.shape[1]
     size = order_chunk(order_count, lat_total, width)
@@ -436,12 +450,12 @@
         grid=(order_count // size,),
         in_specs=[
             pl.BlockSpec((lat_total, size, 2 * width), lambda i: (0, i, 0)),
-            pl.BlockSpec((devices, 2, size, lanes), lambda i: (0, 0, i, 0)),
+            pl.BlockSpec((devices, size, lanes), lambda i: (0, i, 0)),
             table,
             table,
         ],
-        out_specs=pl.BlockSpec((slots, 2, channels, width), lambda i: (0, 0, 0, 0)),
-        out_shape=jax.ShapeDtypeStruct((slots, 2, channels, width), jnp.float32),
+        out_specs=pl.BlockSpec((thin_slots, 2, channels, width), lambda i: (0, 0, 0, 0)),
+        out_shape=jax.ShapeDtypeStruct((thin_slots, 2, channels, width), jnp.float32),
         scratch_shapes=[
             pltpu.VMEM((slots, size, thin), jnp.float32),
             pltpu.VMEM((slots, size, 2 * width), jnp.float32),
@@ -451,27 +465,49 @@
     )(grid_grad, spectra, fwd_rows, inv_rows)
 
 
-def spectral_adam(factor, encoder, thin, weight, first, second):
+def adam_split(degrees):
+    size = 3 if degrees % 3 == 0 and degrees >= 12 else 1
+    steps_all = -(-degrees // (2 * size))
+    return size, steps_all // 2, steps_all - steps_all // 2
+
+
+def spectral_adam(factor, encoder, one, two, low_one, low_two, weights, done):
+    weight = weights[0]
     degrees = weight.shape[0]
-    size = steps(degrees)
-    whole = pl.BlockSpec((size,) + weight.shape[1:], lambda i: (i, 0, 0, 0))
-    wide_out = jax.ShapeDtypeStruct(weight.shape, jnp.float32)
+    size, first_steps, second_steps = adam_split(degrees)
+    step = jnp.arange(first_steps + second_steps, dtype=jnp.int32)
+    start_two = 2 * first_steps + jnp.where(low_two, 0, second_steps)
+    block = jnp.where(
+        step < first_steps, step + jnp.where(low_one, 0, first_steps), step - first_steps + start_two
+    )
+    block = jnp.minimum(block, degrees // size - 1)
+    thin_block = jnp.where(step < first_steps, 0, block - start_two)
+    whole = pl.BlockSpec((size,) + weight.shape[1:], lambda i, b, t: (b[i], 0, 0, 0))
+    thin = (size,) + one.shape[1:]
+    outs = [jax.ShapeDtypeStruct(weight.shape, jnp.float32)] * 3
+    outs.append(jax.ShapeDtypeStruct(weight.shape, jnp.bfloat16))
     return pl.pallas_call(
-        adam_kernel,
-        grid=(degrees // size,),
-        in_specs=[
-            pl.BlockSpec(memory_space=pltpu.SMEM),
-            pl.BlockSpec(encoder.shape, lambda i: (0, 0)),
-            pl.BlockSpec((size,) + thin.shape[1:], lambda i: (i, 0, 0, 0)),
-            whole,
-            whole,
-            whole,
-        ],
-        out_specs=[whole] * 4,
-        out_shape=[wide_out] * 3 + [jax.ShapeDtypeStruct(weight.shape, jnp.bfloat16)],
+        functools.partial(adam_kernel, first_steps),
+        grid_spec=pltpu.PrefetchScalarGridSpec(
+            num_scalar_prefetch=2,
+            grid=(first_steps + second_steps,),
+            in_specs=[
+                pl.BlockSpec(memory_space=pltpu.SMEM),
+                pl.BlockSpec(encoder.shape, lambda i, b, t: (0, 0)),
+                pl.BlockSpec(thin, lambda i, b, t: (jnp.minimum(i, first_steps - 1), 0, 0, 0)),
+                pl.BlockSpec(thin, lambda i, b, t: (t[i], 0, 0, 0)),
+                whole,
+                whole,
+                whole,
+            ]
+            + [pl.BlockSpec(memory_space=pl.ANY)] * len(done),
+            out_specs=[whole] * 4,
+        ),
+        out_shape=outs,
+        input_output_aliases={9 + k: k for k in range(len(done))},
         compiler_params=vmem(48),
         name="spectral_adam",
-    )(factor, encoder, thin, weight, first, second)
+    )(block, thin_block, factor, encoder, one, two, *weights, *done)
 
 
 def pixel_weights(land_mask, missing_rows, first_row, lat_total, channels):
@@ -543,8 +579,9 @@
     )
 
     lines = fields.transpose(1, 0, 2).reshape(lat_dev * channels, lon_count)
-    lines = jnp.pad(lines, ((0, -lines.shape[0] % 128), (0, 0)))
-    spectra = lax.all_gather(dot("rj,psj->psr", lines, forward), "wide", axis=0, tiled=False)
+    spectra = [dot("rj,sj->sr", lines, table) for table in forward]
+    spare = -2 * lat_dev * channels % 128
+    spectra = jnp.concatenate(spectra + [jnp.zeros((order_count, spare), jnp.float32)], axis=1)
 
     folded = dot("cd,tpdk->tpck", encoder, spectral_weight)
 
@@ -552,7 +589,9 @@
     slot_of = jnp.argsort(order_map)
     slots = degree_slots + degree_slots % 2
     if 128 % lat_total == 0 and lax.axis_size("dp") == 4 and wide_count == 8 and lat_total >= 8:
-        wire, folded = tables_to_degrees(forward_table, inverse_table, wide_count, degree_slots, folded)
+        wire, (folded, spectra) = tables_to_degrees(
+            forward_table, inverse_table, wide_count, degree_slots, (folded, spectra)
+        )
         degrees = jnp.pad(my_degrees, (0, 2 * wire.shape[2] - degree_slots), constant_values=-1)
         own = forward_table.shape[0]
         fwd_rows, inv_rows = table_rows(wire, slot_of, degrees, own, lat_total, slots)
@@ -577,6 +616,7 @@
         fwd_rows = by_degree(fwd_masked.transpose(0, 3, 2, 1))
         inv_rows = by_degree(inv_masked.transpose(0, 2, 3, 1))
 
+    spectra = lax.all_gather(spectra, "wide", axis=0, tiled=False)
     grid_coef = spectral_forward(spectra, fwd_rows, inv_rows, folded, lat_dev, channels)
     grid_coef = lax.psum_scatter(grid_coef, "wide", scatter_dimension=0, tiled=True)
     grid_coef = grid_coef.reshape(lat_dev, order_count, 2, width)
@@ -626,8 +666,9 @@
     small = flat[at + 2 * channels :].reshape(-1)[:small_count]
     encoder_grad = all_sum(dot("tpck,tpdk->cd", thin[:degree_slots], spectral_weight))
     gram = jnp.einsum("ck,dk->cd", encoder, encoder, precision=lax.Precision.HIGHEST)
-    thin, spectral_squares = thin_sum(thin.reshape(2 * slots, thin_count, width), gram)
-    thin = thin.reshape(slots, 2, thin_count, width)
+    size, first_steps, _ = adam_split(degree_slots)
+    pairs = thin.reshape((-1,) + thin.shape[2:])
+    parts, spectral_squares = thin_sum(pairs, gram, 4 * size * first_steps)
     io_grad = jnp.stack([direct + encoder_grad[:channels], decoder_grad])
     bias_grad = jnp.concatenate([small[:width] + encoder_grad[channels], small[width:-2]])
     loss_sum, valid_weight = small[-2], small[-1]
@@ -640,9 +681,13 @@
     )
     grad_norm = jnp.sqrt(squares) * rescale
     factor = rescale * CLIP_LIMIT / jnp.maximum(grad_norm, CLIP_LIMIT)
-    spectral_new, spectral_first_new, spectral_second_new, spectral_low = spectral_adam(
-        factor[None], encoder, thin, spectral_weight, spectral_first, spectral_second
-    )
+    spectral = ()
+    weights = (spectral_weight, spectral_first, spectral_second)
+    for half in range(2):
+        one, two = (part[half].reshape((-1, 2) + thin.shape[2:]) for part in parts)
+        low_one, low_two = ((part[2] if half == 0 else jnp.logical_not(part[2])) for part in parts)
+        spectral = spectral_adam(factor[None], encoder, one, two, low_one, low_two, weights, spectral)
+    spectral_new, spectral_first_new, spectral_second_new, spectral_low = spectral
     io_new, io_first_new, io_second_new = adam_step(
         io_weight, io_first, io_second, io_grad * factor, WEIGHT_DECAY
     )

time: 1000 us -> 954 us (0.954)
  waiting for transfers between devices: 552 us -> 503 us
    ppermute x38, waiting for transfers between devices: 230 us -> 187 us  [exchange(): return lax.ppermute(value, axis, [(i, i ^ bit) for i in range(count)])]
    reduce_scatter x1, waiting for transfers between devices: 248 us -> 227 us  [body(): lax.psum_scatter(grid_coef, 'wide', scatter_dimension=0, tiled=True)]
    all_gather x1, waiting for transfers between devices: 0.01 us -> 13.6 us  [body(): spectra = lax.all_gather(spectra, 'wide', axis=0, tiled=False)]
    unnamed x104 -> x92, local copies, waits for them, and re-layouts: 19 us -> 25 us
    pallas_call x1 -> x2, Pallas kernels: 57.4 us -> 62.3 us  [spectral_adam(): pl.pallas_call(functools.partial(adam_kernel, first_steps), grid_spec=plt...]
    dot_general x16 -> x17, matrix products: 97.1 us -> 95.7 us  [dot(): return jnp.einsum(spec, left, right, precision=HIGH)]
  transfers between devices with their start and end apart: 41 -> 41, of which waited for: 29 -> 24; matrix products, arithmetic and copies ran while one was open for 12% -> 14% of each run, Pallas kernels for 1% -> 4%
where the time goes in v4:
time: 954 us; the launch traced here: 948 us
  waiting for transfers between devices  503 us (53%)
  Pallas kernels  189 us (20%)
  matrix products  101 us (11%)
  local copies, waits for them, and re-layouts  55.8 us (6%)
  starting transfers between devices  49.1 us (5%)
  other arithmetic  29.6 us (3%)
  between operations  20.6 us (2%)
    reduce_scatter x1, waiting for transfers between devices, body(): lax.psum_scatter(grid_coef, 'wide', scatter_dimension=0, tiled=True)  227 us
    ppermute x38, waiting for transfers between devices, exchange(): return lax.ppermute(value, axis, [(i, i ^ bit) for i in range(count)])  187 us
    dot_general x17, matrix products, dot(): return jnp.einsum(spec, left, right, precision=HIGH)  95.7 us
    all_gather x1, waiting for transfers between devices, body(): grid_grad = lax.all_gather(grid_grad, 'wide', axis=0, tiled=True)  74.6 us
    pallas_call x2, Pallas kernels, spectral_adam(): pl.pallas_call(functools.partial(adam_kernel, first_steps), grid_spec=plt...  62.3 us
    pallas_call x1, Pallas kernels, spectral_forward(): pl.pallas_call(functools.partial(forward_kernel, lat_dev, fields), grid=(...  59.2 us
    pallas_call x1, Pallas kernels, spectral_backward(): pl.pallas_call(functools.partial(backward_kernel, degrees, lat_dev, field...  55.1 us
    ppermute x38, starting transfers between devices, exchange(): return lax.ppermute(value, axis, [(i, i ^ bit) for i in range(count)])  48.5 us
  transfers between devices with their start and end apart: 41, of which 24 were waited for; matrix products, arithmetic and copies ran while one was open for 14% of the time, Pallas kernels for 4%

profile of v4, /device:TPU:0, one launch (start us, length us, event | category | flops | bytes accessed | tf_op | source)
XLA Modules:
  0.0 947.9 jit_solution(8513077807179305020)
XLA Ops:
  7.3 6.4 copy.107.inverse_ref
  28.7 14.9 %convolution_bitcast_fusion.folded_ref = f32[45,2,80,256]{3,2,1,0:T(8,128)} fusion(f32[45,2,256,256]{3,2,1,0:T(8,128)} %refs_2_.3, f32[80,256]{1,0:T(8,128)S(1)} %maximum_maximum_fusion.2.encoder_ref), kind=kOutput, calls=%fused_computation.20 | convolution fusion | flops 2831155200 | bytes 31047680 | tf_op jit(solution)/shard_map/cd,tpdk->tpck/dot_general | solution.py:32
  59.0 4.2 collective-permute-start.9
  64.7 12.2 %collective-permute-done.9 = f32[1,4,24,1536]{3,2,1,0:T(8,128)S(1)} collective-permute-done((f32[1,4,24,1536]{3,2,1,0:T(8,128)S(1)}, f32[1,4,24,1536]{3,2,1,0:T(8,128)S(1)}, u32[]{:S(2)}, u32[]{:S(2)}) %collective-permute-start.9) | collective-permute-done | bytes 589856 | tf_op jit(solution)/shard_map/ppermute | solution.py:262
  87.0 18.9 %collective-permute-done.10 = f32[2,4,24,1536]{3,2,1,0:T(8,128)} collective-permute-done((f32[2,4,24,1536]{3,2,1,0:T(8,128)}, f32[2,4,24,1536]{3,2,1,0:T(8,128)}, u32[]{:S(2)}, u32[]{:S(2)}) %collective-permute-start.10) | collective-permute-done | bytes 1179680 | tf_op jit(solution)/shard_map/ppermute | solution.py:262
  109.9 11.5 %table_rows.1 = (f32[45,46,256]{2,1,0:T(8,128)S(1)}, f32[45,46,256]{2,1,0:T(8,128)S(1)}) custom-call(s32[2]{0:T(128)S(1)} %pad_add_fusion.me_ref, s32[360]{0:T(512)S(1)} %get-tuple-element.36.slot_ref, f32[4,8,24,1536]{3,2,1,0:T(8,128)S(1)} %maximum_maximum_fusion.wire_ref, s32[48,1]{1,0:T(8,128)S(1)} %copy.110.degree_ref, bf16[256,256]{1,0:T(8,128)(2,1)S(1)} %copy-done.4), custom_call_target="tpu_custom_call" | custom-call | tf_op jit(solution)/shard_map/table_rows/pallas_call | solution.py:250
  124.2 13.6 %all-gather.6.cloned.1.call-done = f32[2880,640]{1,0:T(8,128)} async-done(((f32[360,640]{1,0:T(8,128)}), f32[2880,640]{1,0:T(8,128)}) %all-gather.6.cloned.1.call-update) | async-done | bytes 7372816 | tf_op jit(solution)/shard_map/all_gather | solution.py:619
  137.8 59.2 %spectral_forward.1 = f32[32,360,512]{2,1,0:T(8,128)} custom-call(f32[8,360,640]{2,1,0:T(8,128)} %bitcast.215, f32[45,46,256]{2,1,0:T(8,128)} %copy-done.1, f32[45,46,256]{2,1,0:T(8,128)} %copy-done.2, f32[45,2,80,256]{3,2,1,0:T(8,128)} %convolution_bitcast_fusion.folded_ref), custom_call_target="tpu_custom_call" | custom-call | tf_op jit(solution)/shard_map/spectral_forward/pallas_call | solution.py:416
  200.7 227.4 %reduce-scatter.2.cloned.1.call-done = f32[4,360,512]{2,1,0:T(8,128)} async-done(((f32[32,360,512]{2,1,0:T(8,128)}), f32[4,360,512]{2,1,0:T(8,128)}) %reduce-scatter.2.cloned.1.call-update) | async-done | bytes 2949136 | tf_op jit(solution)/shard_map/reduce_scatter | solution.py:621
  428.1 7.2 bitcast_add_fusion
  437.9 4.6 add_add_fusion
  446.8 10.1 %fusion.93 = (f32[512]{0:T(512)}, f32[4,720,512]{2,1,0:T(8,128)S(1)}) fusion(f32[4,720,512]{2,1,0:T(8,128)S(1)} %fusion.38, f32[512]{0:T(512)S(1)} %slice.101, f32[4,720,256]{2,1,0:T(8,128)S(1)} %get-tuple-element.160, f32[2,256,512]{2,1,0:T(8,128)S(1)} %copy-done.20), kind=kOutput, calls=%fused_computation.187 | convolution fusion | flops 2295889408 | bytes 15273984 | tf_op jit(solution)/shard_map/ajk,kh->ajh/dot_general | solution.py:32
  460.2 3.9 fusion.16
  466.2 6.1 convolution_bitcast_fusion.3
  473.5 10.6 %fusion.25 = f32[256,512]{1,0:T(8,128)} fusion(f32[4,720,256]{2,1,0:T(8,128)} %copy-done.12, f32[4,720,512]{2,1,0:T(8,128)} %copy-done.19, f32[512]{0:T(512)} %copy-done.39), kind=kOutput, calls=%fused_computation.40 | convolution fusion | flops 2278195200 | bytes 9373696 | tf_op jit(solution)/shard_map/ajk,ajh->kh/dot_general | solution.py:32
  502.3 11.8 %collective-permute-done.11 = f32[592,256]{1,0:T(8,128)S(1)} collective-permute-done((f32[592,256]{1,0:T(8,128)S(1)}, f32[592,256]{1,0:T(8,128)S(1)}, u32[]{:S(2)}, u32[]{:S(2)}) %collective-permute-start.11) | collective-permute-done | bytes 606240 | tf_op jit(solution)/shard_map/ppermute | solution.py:262
  515.7 5.4 collective-permute-done.12
  522.8 4.4 collective-permute-start.14
  527.2 28.8 %collective-permute-done.14 = f32[296,256]{1,0:T(8,128)S(1)} collective-permute-done((f32[296,256]{1,0:T(8,128)S(1)}, f32[296,256]{1,0:T(8,128)S(1)}, u32[]{:S(2)}, u32[]{:S(2)}) %collective-permute-start.14) | collective-permute-done | bytes 303136 | tf_op jit(solution)/shard_map/ppermute | solution.py:262
  556.1 30.9 %collective-permute-done.15 = f32[296,256]{1,0:T(8,128)S(1)} collective-permute-done((f32[296,256]{1,0:T(8,128)S(1)}, f32[296,256]{1,0:T(8,128)S(1)}, u32[]{:S(2)}, u32[]{:S(2)}) %collective-permute-start.15) | collective-permute-done | bytes 303136 | tf_op jit(solution)/shard_map/ppermute | solution.py:262
  588.9 6.7 collective-permute-done.16
  597.6 12.2 %collective-permute-done.17 = f32[592,256]{1,0:T(8,128)S(1)} collective-permute-done((f32[592,256]{1,0:T(8,128)S(1)}, f32[592,256]{1,0:T(8,128)S(1)}, u32[]{:S(2)}, u32[]{:S(2)}) %collective-permute-start.17) | collective-permute-done | bytes 606240 | tf_op jit(solution)/shard_map/ppermute | solution.py:262
  610.0 74.6 %all-gather.4.cloned.1.call-done.grid_ref = f32[32,360,512]{2,1,0:T(8,128)} async-done(((f32[4,360,512]{2,1,0:T(8,128)}), f32[32,360,512]{2,1,0:T(8,128)}) %all-gather.4.cloned.1.call-update) | async-done | bytes 23592976 | tf_op jit(solution)/shard_map/all_gather | solution.py:648
  684.6 55.1 %spectral_backward.1 = f32[48,2,80,256]{3,2,1,0:T(8,128)} custom-call(f32[32,360,512]{2,1,0:T(8,128)} %all-gather.4.cloned.1.call-done.grid_ref, f32[8,360,640]{2,1,0:T(8,128)} %bitcast.216, f32[45,46,256]{2,1,0:T(8,128)} %copy-done.1, f32[45,46,256]{2,1,0:T(8,128)} %copy-done.2), custom_call_target="tpu_custom_call" | custom-call | tf_op jit(solution)/shard_map/spectral_backward/pallas_call | solution.py:448
  739.7 3.9 fusion.88
  748.9 16.7 %fusion = f32[80,256,1,1]{1,0,3,2:T(8,128)S(1)} fusion(f32[45,2,256,256]{3,2,1,0:T(8,128)} %refs_2_.3, f32[48,2,80,256]{3,2,1,0:T(8,128)} %spectral_backward.1), kind=kOutput, calls=%fused_computation | convolution fusion | flops 2831155200 | bytes 31047680 | tf_op jit(solution)/shard_map/tpck,tpdk->cd/dot_general | solution.py:32
  767.2 22.5 %collective-permute-done.27 = f32[40,256]{1,0:T(8,128)S(1)} collective-permute-done((f32[40,256]{1,0:T(8,128)S(1)}, f32[40,256]{1,0:T(8,128)S(1)}, u32[]{:S(2)}, u32[]{:S(2)}) %collective-permute-start.27) | collective-permute-done | bytes 40992 | tf_op jit(solution)/shard_map/ppermute | solution.py:262
  811.2 7.1 collective-permute-done.19
  833.8 12.5 %collective-permute-done.22 = f32[8,128]{1,0:T(8,128)S(1)} collective-permute-done((f32[8,128]{1,0:T(8,128)S(1)}, f32[8,128]{1,0:T(8,128)S(1)}, u32[]{:S(2)}, u32[]{:S(2)}) %collective-permute-start.22) | collective-permute-done | bytes 4128 | tf_op jit(solution)/shard_map/ppermute | solution.py:262
  873.4 4.3 fusion.83
  877.7 30.9 %spectral_adam.2 = (f32[45,2,256,256]{3,2,1,0:T(8,128)}, f32[45,2,256,256]{3,2,1,0:T(8,128)}, f32[45,2,256,256]{3,2,1,0:T(8,128)}, bf16[45,2,256,256]{3,2,1,0:T(8,128)(2,1)}) custom-call(s32[8]{0:T(128)S(1)} %get-tuple-element.165.block_ref, s32[8]{0:T(128)S(1)} %get-tuple-element.164.thin_block_ref, f32[1]{0:T(128)} %bitcast.88.factor_ref, ...), custom_call_target="tpu_custom_call" | custom-call | tf_op jit(solution)/shard_map/spectral_adam/pallas_call | solution.py:489
  908.6 31.4 %spectral_adam.3 = (f32[45,2,256,256]{3,2,1,0:T(8,128)}, f32[45,2,256,256]{3,2,1,0:T(8,128)}, f32[45,2,256,256]{3,2,1,0:T(8,128)}, bf16[45,2,256,256]{3,2,1,0:T(8,128)(2,1)}) custom-call(s32[8]{0:T(128)S(1)} %get-tuple-element.163.block_ref, ...), custom_call_target="tpu_custom_call", output_to_operand_aliasing={{0}: (9, {}), {1}: (10, {}), {2}: (11, {}), {3}: (12, {})} | custom-call | tf_op jit(solution)/shard_map/spectral_adam/pallas_call | solution.py:489
  (268 shorter events, 157.3 us)
Async XLA Ops:
  7.2 130.6 %all-gather.6.cloned.1.call-start = ((), (), s32[]{:S(2)}) async-start(), calls=%async_computation.3 | async-start | bytes 8294400 | tf_op jit(solution)/shard_map/all_gather | solution.py:619
  19.0 24.8 %collective-permute-start = (f32[24,1536]{1,0:T(8,128)}, f32[24,1536]{1,0:T(8,128)}, u32[]{:S(2)}, u32[]{:S(2)}) collective-permute-start(f32[24,1536]{1,0:T(8,128)} %get-tuple-element.143), channel_id=1, source_target_pairs={{0,1},{1,0},{2,3},{3,2},{4,5},{5,4},{6,7},{7,6},{8,9},{9,8},{10,11... | collective-permute-start | bytes 442376 | tf_op jit(solution)/shard_map/ppermute | solution.py:262
  19.4 29.5 %collective-permute-start.1 = (f32[24,1536]{1,0:T(8,128)}, f32[24,1536]{1,0:T(8,128)}, u32[]{:S(2)}, u32[]{:S(2)}) collective-permute-start(f32[24,1536]{1,0:T(8,128)} %get-tuple-element.142), channel_id=1, source_target_pairs={{0,2},{1,3},{2,0},{3,1},{4,6},{5,7},{6,4},{7,5},{8,10},{9,11},{10,... | collective-permute-start | bytes 442376 | tf_op jit(solution)/shard_map/ppermute | solution.py:262
  22.0 28.6 %collective-permute-start.2 = (f32[24,1536]{1,0:T(8,128)}, f32[24,1536]{1,0:T(8,128)}, u32[]{:S(2)}, u32[]{:S(2)}) collective-permute-start(f32[24,1536]{1,0:T(8,128)} %get-tuple-element.141), channel_id=1, source_target_pairs={{0,3},{1,2},{2,1},{3,0},{4,7},{5,6},{6,5},{7,4},{8,11},{9,10},{10,... | collective-permute-start | bytes 442376 | tf_op jit(solution)/shard_map/ppermute | solution.py:262
  22.1 30.1 %collective-permute-start.3 = (f32[24,1536]{1,0:T(8,128)}, f32[24,1536]{1,0:T(8,128)}, u32[]{:S(2)}, u32[]{:S(2)}) collective-permute-start(f32[24,1536]{1,0:T(8,128)} %get-tuple-element.140), channel_id=1, source_target_pairs={{0,4},{1,5},{2,6},{3,7},{4,0},{5,1},{6,2},{7,3},{8,12},{9,13},{10,... | collective-permute-start | bytes 442376 | tf_op jit(solution)/shard_map/ppermute | solution.py:262
  24.9 28.9 %collective-permute-start.4 = (f32[24,1536]{1,0:T(8,128)}, f32[24,1536]{1,0:T(8,128)}, u32[]{:S(2)}, u32[]{:S(2)}) collective-permute-start(f32[24,1536]{1,0:T(8,128)} %get-tuple-element.139), channel_id=1, source_target_pairs={{0,5},{1,4},{2,7},{3,6},{4,1},{5,0},{6,3},{7,2},{8,13},{9,12},{10,... | collective-permute-start | bytes 442376 | tf_op jit(solution)/shard_map/ppermute | solution.py:262
  43.7 11.7 %collective-permute-start.5 = (f32[24,1536]{1,0:T(8,128)S(1)}, f32[24,1536]{1,0:T(8,128)S(1)}, u32[]{:S(2)}, u32[]{:S(2)}) collective-permute-start(f32[24,1536]{1,0:T(8,128)S(1)} %get-tuple-element.138), channel_id=1, source_target_pairs={{0,6},{1,7},{2,4},{3,5},{4,2},{5,3},{6,0},{7,1},{8,14},{9,15},{10,... | collective-permute-start | bytes 442376 | tf_op jit(solution)/shard_map/ppermute | solution.py:262
  48.9 7.7 collective-permute-start.6
  58.6 369.5 %reduce-scatter.2.cloned.1.call-start = ((), (), s32[]{:S(2)}) async-start(), calls=%async_computation.1 | async-start | bytes 26542080 | tf_op jit(solution)/shard_map/reduce_scatter | solution.py:621
  59.0 17.9 %collective-permute-start.9 = (f32[1,4,24,1536]{3,2,1,0:T(8,128)S(1)}, f32[1,4,24,1536]{3,2,1,0:T(8,128)S(1)}, u32[]{:S(2)}, u32[]{:S(2)}) collective-permute-start(f32[1,4,24,1536]{3,2,1,0:T(8,128)S(1)} %get-tuple-element.134), channel_id=1, source_target_pairs={{0,16},{8,24},{16,0},{24,8},{1,17},{9,25},{17,1},{25,9},{2,18},{10... | collective-permute-start | bytes 1769480 | tf_op jit(solution)/shard_map/ppermute | solution.py:262
  63.2 16.2 %collective-permute-start.7 = (f32[1,4,24,1536]{3,2,1,0:T(8,128)S(1)}, f32[1,4,24,1536]{3,2,1,0:T(8,128)S(1)}, u32[]{:S(2)}, u32[]{:S(2)}) collective-permute-start(f32[1,4,24,1536]{3,2,1,0:T(8,128)S(1)} %get-tuple-element.133), channel_id=1, source_target_pairs={{0,8},{8,0},{16,24},{24,16},{1,9},{9,1},{17,25},{25,17},{2,10},{10... | collective-permute-start | bytes 1769480 | tf_op jit(solution)/shard_map/ppermute | solution.py:262
  78.0 27.9 %collective-permute-start.10 = (f32[2,4,24,1536]{3,2,1,0:T(8,128)}, f32[2,4,24,1536]{3,2,1,0:T(8,128)}, u32[]{:S(2)}, u32[]{:S(2)}) collective-permute-start(f32[2,4,24,1536]{3,2,1,0:T(8,128)} %pad_maximum_fusion.4), channel_id=1, source_target_pairs={{0,8},{8,0},{16,24},{24,16},{1,9},{9,1},{17,25},{25,17},{2,10},{10... | collective-permute-start | bytes 3538952 | tf_op jit(solution)/shard_map/ppermute | solution.py:262
  80.6 27.7 %collective-permute-start.8 = (f32[2,4,24,1536]{3,2,1,0:T(8,128)}, f32[2,4,24,1536]{3,2,1,0:T(8,128)}, u32[]{:S(2)}, u32[]{:S(2)}) collective-permute-start(f32[2,4,24,1536]{3,2,1,0:T(8,128)} %pad_maximum_fusion.3), channel_id=1, source_target_pairs={{0,16},{8,24},{16,0},{24,8},{1,17},{9,25},{17,1},{25,9},{2,18},{10... | collective-permute-start | bytes 3538952 | tf_op jit(solution)/shard_map/ppermute | solution.py:262
  197.0 487.6 %all-gather.4.cloned.1.call-start = ((), (), s32[]{:S(2)}) async-start(), calls=%async_computation.2 | async-start | bytes 26542080 | tf_op jit(solution)/shard_map/all_gather | solution.py:648
  500.8 13.2 %collective-permute-start.11 = (f32[592,256]{1,0:T(8,128)S(1)}, f32[592,256]{1,0:T(8,128)S(1)}, u32[]{:S(2)}, u32[]{:S(2)}) collective-permute-start(f32[592,256]{1,0:T(8,128)S(1)} %dynamic-slice_bitcast_fusion.4), channel_id=1, source_target_pairs={{0,8},{8,0},{16,24},{24,16},{1,9},{9,1},{17,25},{25,17},{2,10},{10... | collective-permute-start | bytes 1818632 | tf_op jit(solution)/shard_map/ppermute | solution.py:262
  522.8 33.1 %collective-permute-start.14 = (f32[296,256]{1,0:T(8,128)S(1)}, f32[296,256]{1,0:T(8,128)S(1)}, u32[]{:S(2)}, u32[]{:S(2)}) collective-permute-start(f32[296,256]{1,0:T(8,128)S(1)} %add.324), channel_id=1, source_target_pairs={{0,2},{1,3},{2,0},{3,1},{4,6},{5,7},{6,4},{7,5},{8,10},{9,11},{10,... | collective-permute-start | bytes 909320 | tf_op jit(solution)/shard_map/ppermute | solution.py:262
  556.0 31.1 %collective-permute-start.15 = (f32[296,256]{1,0:T(8,128)S(1)}, f32[296,256]{1,0:T(8,128)S(1)}, u32[]{:S(2)}, u32[]{:S(2)}) collective-permute-start(f32[296,256]{1,0:T(8,128)S(1)} %add.325), channel_id=1, source_target_pairs={{0,4},{1,5},{2,6},{3,7},{4,0},{5,1},{6,2},{7,3},{8,12},{9,13},{10,... | collective-permute-start | bytes 909320 | tf_op jit(solution)/shard_map/ppermute | solution.py:262
  587.1 8.5 collective-permute-start.16
  595.7 14.1 %collective-permute-start.17 = (f32[592,256]{1,0:T(8,128)S(1)}, f32[592,256]{1,0:T(8,128)S(1)}, u32[]{:S(2)}, u32[]{:S(2)}) collective-permute-start(f32[592,256]{1,0:T(8,128)S(1)} %pad_maximum_fusion.5), channel_id=1, source_target_pairs={{0,8},{8,0},{16,24},{24,16},{1,9},{9,1},{17,25},{25,17},{2,10},{10... | collective-permute-start | bytes 1818632 | tf_op jit(solution)/shard_map/ppermute | solution.py:262
  743.8 47.5 %collective-permute-start.18 = (f32[24,80,256]{2,1,0:T(8,128)S(1)}, f32[24,80,256]{2,1,0:T(8,128)}, u32[]{:S(2)}, u32[]{:S(2)}) collective-permute-start(f32[24,80,256]{2,1,0:T(8,128)S(1)} %dynamic-slice_bitcast_fusion.1), channel_id=1, source_target_pairs={{0,8},{8,0},{16,24},{24,16},{1,9},{9,1},{17,25},{25,17},{2,10},{10... | collective-permute-start | bytes 5898248 | tf_op jit(solution)/shard_map/ppermute | solution.py:262
  747.4 48.3 %collective-permute-start.20 = (f32[24,80,256]{2,1,0:T(8,128)}, f32[24,80,256]{2,1,0:T(8,128)}, u32[]{:S(2)}, u32[]{:S(2)}) collective-permute-start(f32[24,80,256]{2,1,0:T(8,128)} %dynamic-slice_bitcast_fusion), channel_id=1, source_target_pairs={{0,16},{8,24},{16,0},{24,8},{1,17},{9,25},{17,1},{25,9},{2,18},{10... | collective-permute-start | bytes 5898248 | tf_op jit(solution)/shard_map/ppermute | solution.py:262
  765.6 24.1 %collective-permute-start.27 = (f32[40,256]{1,0:T(8,128)S(1)}, f32[40,256]{1,0:T(8,128)S(1)}, u32[]{:S(2)}, u32[]{:S(2)}) collective-permute-start(f32[40,256]{1,0:T(8,128)S(1)} %dynamic-slice_bitcast_fusion.13), channel_id=1, source_target_pairs={{0,8},{8,0},{16,24},{24,16},{1,9},{9,1},{17,25},{25,17},{2,10},{10... | collective-permute-start | bytes 122888 | tf_op jit(solution)/shard_map/ppermute | solution.py:262
  789.7 10.4 %collective-permute-start.28 = (f32[20,256]{1,0:T(8,128)S(1)}, f32[20,256]{1,0:T(8,128)S(1)}, u32[]{:S(2)}, u32[]{:S(2)}) collective-permute-start(f32[20,256]{1,0:T(8,128)S(1)} %dynamic-slice_bitcast_fusion.14), channel_id=1, source_target_pairs={{0,16},{8,24},{16,0},{24,8},{1,17},{9,25},{17,1},{25,9},{2,18},{10... | collective-permute-start | bytes 61448 | tf_op jit(solution)/shard_map/ppermute | solution.py:262
  794.8 23.5 %collective-permute-start.19 = (f32[12,80,256]{2,1,0:T(8,128)}, f32[12,80,256]{2,1,0:T(8,128)}, u32[]{:S(2)}, u32[]{:S(2)}) collective-permute-start(f32[12,80,256]{2,1,0:T(8,128)} %dynamic-slice_bitcast_fusion.3), channel_id=1, source_target_pairs={{0,16},{8,24},{16,0},{24,8},{1,17},{9,25},{17,1},{25,9},{2,18},{10... | collective-permute-start | bytes 2949128 | tf_op jit(solution)/shard_map/ppermute | solution.py:262
  798.7 22.9 %collective-permute-start.21 = (f32[12,80,256]{2,1,0:T(8,128)}, f32[12,80,256]{2,1,0:T(8,128)}, u32[]{:S(2)}, u32[]{:S(2)}) collective-permute-start(f32[12,80,256]{2,1,0:T(8,128)} %dynamic-slice_bitcast_fusion.2), channel_id=1, source_target_pairs={{0,8},{8,0},{16,24},{24,16},{1,9},{9,1},{17,25},{25,17},{2,10},{10... | collective-permute-start | bytes 2949128 | tf_op jit(solution)/shard_map/ppermute | solution.py:262
  810.0 10.7 %collective-permute-start.32 = (f32[20,256]{1,0:T(8,128)S(1)}, f32[20,256]{1,0:T(8,128)S(1)}, u32[]{:S(2)}, u32[]{:S(2)}) collective-permute-start(f32[20,256]{1,0:T(8,128)S(1)} %add.341), channel_id=1, source_target_pairs={{0,16},{8,24},{16,0},{24,8},{1,17},{9,25},{17,1},{25,9},{2,18},{10... | collective-permute-start | bytes 61448 | tf_op jit(solution)/shard_map/ppermute | solution.py:262
  819.9 27.7 %collective-permute-start.34 = (f32[12,80,256]{2,1,0:T(8,128)S(1)}, f32[12,80,256]{2,1,0:T(8,128)S(1)}, u32[]{:S(2)}, u32[]{:S(2)}) collective-permute-start(f32[12,80,256]{2,1,0:T(8,128)S(1)} %bitcast_add_fusion.4), channel_id=1, source_target_pairs={{0,16},{8,24},{16,0},{24,8},{1,17},{9,25},{17,1},{25,9},{2,18},{10... | collective-permute-start | bytes 2949128 | tf_op jit(solution)/shard_map/ppermute | solution.py:262
  823.8 25.7 %collective-permute-start.36 = (f32[12,80,256]{2,1,0:T(8,128)}, f32[12,80,256]{2,1,0:T(8,128)}, u32[]{:S(2)}, u32[]{:S(2)}) collective-permute-start(f32[12,80,256]{2,1,0:T(8,128)} %bitcast_add_fusion.3), channel_id=1, source_target_pairs={{0,8},{8,0},{16,24},{24,16},{1,9},{9,1},{17,25},{25,17},{2,10},{10... | collective-permute-start | bytes 2949128 | tf_op jit(solution)/shard_map/ppermute | solution.py:262
  831.6 14.6 %collective-permute-start.22 = (f32[8,128]{1,0:T(8,128)S(1)}, f32[8,128]{1,0:T(8,128)S(1)}, u32[]{:S(2)}, u32[]{:S(2)}) collective-permute-start(f32[8,128]{1,0:T(8,128)S(1)} %broadcast_in_dim.71), channel_id=1, source_target_pairs={{0,8},{8,0},{16,24},{24,16},{1,9},{9,1},{17,25},{25,17},{2,10},{10... | collective-permute-start | bytes 12296 | tf_op jit(solution)/shard_map/ppermute | solution.py:262
  832.2 21.1 %collective-permute-start.33 = (f32[40,256]{1,0:T(8,128)S(1)}, f32[40,256]{1,0:T(8,128)S(1)}, u32[]{:S(2)}, u32[]{:S(2)}) collective-permute-start(f32[40,256]{1,0:T(8,128)S(1)} %pad_maximum_fusion.8), channel_id=1, source_target_pairs={{0,8},{8,0},{16,24},{24,16},{1,9},{9,1},{17,25},{25,17},{2,10},{10... | collective-permute-start | bytes 122888 | tf_op jit(solution)/shard_map/ppermute | solution.py:262
  848.0 60.7 %collective-permute-start.35 = (f32[24,80,256]{2,1,0:T(8,128)S(1)}, f32[24,80,256]{2,1,0:T(8,128)}, u32[]{:S(2)}, u32[]{:S(2)}) collective-permute-start(f32[24,80,256]{2,1,0:T(8,128)S(1)} %pad_maximum_fusion), channel_id=1, source_target_pairs={{0,8},{8,0},{16,24},{24,16},{1,9},{9,1},{17,25},{25,17},{2,10},{10... | collective-permute-start | bytes 5898248 | tf_op jit(solution)/shard_map/ppermute | solution.py:262
  852.7 56.0 %collective-permute-start.37 = (f32[24,80,256]{2,1,0:T(8,128)}, f32[24,80,256]{2,1,0:T(8,128)}, u32[]{:S(2)}, u32[]{:S(2)}) collective-permute-start(f32[24,80,256]{2,1,0:T(8,128)} %pad_maximum_fusion.1), channel_id=1, source_target_pairs={{0,16},{8,24},{16,0},{24,8},{1,17},{9,25},{17,1},{25,9},{2,18},{10... | collective-permute-start | bytes 5898248 | tf_op jit(solution)/shard_map/ppermute | solution.py:262
  (50 other events, 1223.3 us)
Sparse Core Ops, SparseCore 0:
  58.7 78.9 all-gather.5
  197.1 230.9 reduce-scatter.1
  466.3 218.2 all-gather.3

commit v5 on v4

--- a/solution.py
+++ b/solution.py
@@ -66,7 +66,7 @@
 
 
 def steps(count):
-    return max(size for size in range(1, 6) if count % size == 0)
+    return max(size for size in range(1, 16) if count % size == 0)
 
 
 def group_rows(group):

time: 954 us -> 941 us (0.986)
  Pallas kernels: 189 us -> 175 us
where the time goes in v5:
time: 941 us; the launch traced here: 935 us
  waiting for transfers between devices  505 us (54%)
  Pallas kernels  175 us (19%)
  matrix products  100 us (11%)
  local copies, waits for them, and re-layouts  55.9 us (6%)
  starting transfers between devices  48.8 us (5%)
  other arithmetic  29.7 us (3%)
  between operations  20.8 us (2%)
    reduce_scatter x1, waiting for transfers between devices, body(): lax.psum_scatter(grid_coef, 'wide', scatter_dimension=0, tiled=True)  227 us
    ppermute x38, waiting for transfers between devices, exchange(): return lax.ppermute(value, axis, [(i, i ^ bit) for i in range(count)])  187 us
    dot_general x17, matrix products, dot(): return jnp.einsum(spec, left, right, precision=HIGH)  95.2 us
    all_gather x1, waiting for transfers between devices, body(): grid_grad = lax.all_gather(grid_grad, 'wide', axis=0, tiled=True)  74.8 us
    pallas_call x2, Pallas kernels, spectral_adam(): pl.pallas_call(functools.partial(adam_kernel, first_steps), grid_spec=plt...  62.3 us
    pallas_call x1, Pallas kernels, spectral_forward(): pl.pallas_call(functools.partial(forward_kernel, lat_dev, fields), grid=(...  52.2 us
    pallas_call x1, Pallas kernels, spectral_backward(): pl.pallas_call(functools.partial(backward_kernel, degrees, lat_dev, field...  49.1 us
    ppermute x38, starting transfers between devices, exchange(): return lax.ppermute(value, axis, [(i, i ^ bit) for i in range(count)])  48.5 us
  transfers between devices with their start and end apart: 41, of which 24 were waited for; matrix products, arithmetic and copies ran while one was open for 14% of the time, Pallas kernels for 4%

profile of v5, /device:TPU:0, one launch (start us, length us, event | category | flops | bytes accessed | tf_op | source)
XLA Modules:
  0.0 934.9 jit_solution(5589220276570885864)
XLA Ops:
  7.3 6.4 copy.107.inverse_ref
  28.7 14.9 %convolution_bitcast_fusion.folded_ref = f32[45,2,80,256]{3,2,1,0:T(8,128)} fusion(f32[45,2,256,256]{3,2,1,0:T(8,128)} %refs_2_.3, f32[80,256]{1,0:T(8,128)S(1)} %maximum_maximum_fusion.2.encoder_ref), kind=kOutput, calls=%fused_computation.20 | convolution fusion | flops 2831155200 | bytes 31047680 | tf_op jit(solution)/shard_map/cd,tpdk->tpck/dot_general | solution.py:32
  58.8 4.2 collective-permute-start.9
  64.6 12.2 %collective-permute-done.9 = f32[1,4,24,1536]{3,2,1,0:T(8,128)S(1)} collective-permute-done((f32[1,4,24,1536]{3,2,1,0:T(8,128)S(1)}, f32[1,4,24,1536]{3,2,1,0:T(8,128)S(1)}, u32[]{:S(2)}, u32[]{:S(2)}) %collective-permute-start.9) | collective-permute-done | bytes 589856 | tf_op jit(solution)/shard_map/ppermute | solution.py:262
  86.8 18.9 %collective-permute-done.10 = f32[2,4,24,1536]{3,2,1,0:T(8,128)} collective-permute-done((f32[2,4,24,1536]{3,2,1,0:T(8,128)}, f32[2,4,24,1536]{3,2,1,0:T(8,128)}, u32[]{:S(2)}, u32[]{:S(2)}) %collective-permute-start.10) | collective-permute-done | bytes 1179680 | tf_op jit(solution)/shard_map/ppermute | solution.py:262
  109.7 10.2 %table_rows.1 = (f32[45,46,256]{2,1,0:T(8,128)S(1)}, f32[45,46,256]{2,1,0:T(8,128)S(1)}) custom-call(s32[2]{0:T(128)S(1)} %pad_add_fusion.me_ref, s32[360]{0:T(512)S(1)} %get-tuple-element.36.slot_ref, f32[4,8,24,1536]{3,2,1,0:T(8,128)S(1)} %maximum_maximum_fusion.wire_ref, s32[48,1]{1,0:T(8,128)S(1)} %copy.110.degree_ref, bf16[256,256]{1,0:T(8,128)(2,1)S(1)} %copy-done.4), custom_call_target="tpu_custom_call" | custom-call | tf_op jit(solution)/shard_map/table_rows/pallas_call | solution.py:250
  122.7 15.2 %all-gather.6.cloned.1.call-done = f32[2880,640]{1,0:T(8,128)} async-done(((f32[360,640]{1,0:T(8,128)}), f32[2880,640]{1,0:T(8,128)}) %all-gather.6.cloned.1.call-update) | async-done | bytes 7372816 | tf_op jit(solution)/shard_map/all_gather | solution.py:619
  137.8 52.2 %spectral_forward.1 = f32[32,360,512]{2,1,0:T(8,128)} custom-call(f32[8,360,640]{2,1,0:T(8,128)} %bitcast.215, f32[45,46,256]{2,1,0:T(8,128)} %copy-done.1, f32[45,46,256]{2,1,0:T(8,128)} %copy-done.2, f32[45,2,80,256]{3,2,1,0:T(8,128)} %convolution_bitcast_fusion.folded_ref), custom_call_target="tpu_custom_call" | custom-call | tf_op jit(solution)/shard_map/spectral_forward/pallas_call | solution.py:416
  193.8 227.4 %reduce-scatter.2.cloned.1.call-done = f32[4,360,512]{2,1,0:T(8,128)} async-done(((f32[32,360,512]{2,1,0:T(8,128)}), f32[4,360,512]{2,1,0:T(8,128)}) %reduce-scatter.2.cloned.1.call-update) | async-done | bytes 2949136 | tf_op jit(solution)/shard_map/reduce_scatter | solution.py:621
  421.1 7.2 bitcast_add_fusion
  430.9 4.3 add_add_fusion
  439.6 10.1 %fusion.93 = (f32[512]{0:T(512)}, f32[4,720,512]{2,1,0:T(8,128)S(1)}) fusion(f32[4,720,512]{2,1,0:T(8,128)S(1)} %fusion.38, f32[512]{0:T(512)S(1)} %slice.101, f32[4,720,256]{2,1,0:T(8,128)S(1)} %get-tuple-element.160, f32[2,256,512]{2,1,0:T(8,128)S(1)} %copy-done.20), kind=kOutput, calls=%fused_computation.187 | convolution fusion | flops 2295889408 | bytes 15273984 | tf_op jit(solution)/shard_map/ajk,kh->ajh/dot_general | solution.py:32
  453.0 3.9 fusion.16
  458.9 6.1 convolution_bitcast_fusion.3
  466.3 10.4 %fusion.25 = f32[256,512]{1,0:T(8,128)} fusion(f32[4,720,256]{2,1,0:T(8,128)} %copy-done.12, f32[4,720,512]{2,1,0:T(8,128)} %copy-done.19, f32[512]{0:T(512)} %copy-done.39), kind=kOutput, calls=%fused_computation.40 | convolution fusion | flops 2278195200 | bytes 9373696 | tf_op jit(solution)/shard_map/ajk,ajh->kh/dot_general | solution.py:32
  494.8 11.8 %collective-permute-done.11 = f32[592,256]{1,0:T(8,128)S(1)} collective-permute-done((f32[592,256]{1,0:T(8,128)S(1)}, f32[592,256]{1,0:T(8,128)S(1)}, u32[]{:S(2)}, u32[]{:S(2)}) %collective-permute-start.11) | collective-permute-done | bytes 606240 | tf_op jit(solution)/shard_map/ppermute | solution.py:262
  508.2 5.3 collective-permute-done.12
  515.3 4.4 collective-permute-start.14
  519.7 28.8 %collective-permute-done.14 = f32[296,256]{1,0:T(8,128)S(1)} collective-permute-done((f32[296,256]{1,0:T(8,128)S(1)}, f32[296,256]{1,0:T(8,128)S(1)}, u32[]{:S(2)}, u32[]{:S(2)}) %collective-permute-start.14) | collective-permute-done | bytes 303136 | tf_op jit(solution)/shard_map/ppermute | solution.py:262
  548.9 30.8 %collective-permute-done.15 = f32[296,256]{1,0:T(8,128)S(1)} collective-permute-done((f32[296,256]{1,0:T(8,128)S(1)}, f32[296,256]{1,0:T(8,128)S(1)}, u32[]{:S(2)}, u32[]{:S(2)}) %collective-permute-start.15) | collective-permute-done | bytes 303136 | tf_op jit(solution)/shard_map/ppermute | solution.py:262
  581.3 6.9 collective-permute-done.16
  590.1 12.3 %collective-permute-done.17 = f32[592,256]{1,0:T(8,128)S(1)} collective-permute-done((f32[592,256]{1,0:T(8,128)S(1)}, f32[592,256]{1,0:T(8,128)S(1)}, u32[]{:S(2)}, u32[]{:S(2)}) %collective-permute-start.17) | collective-permute-done | bytes 606240 | tf_op jit(solution)/shard_map/ppermute | solution.py:262
  602.6 74.8 %all-gather.4.cloned.1.call-done.grid_ref = f32[32,360,512]{2,1,0:T(8,128)} async-done(((f32[4,360,512]{2,1,0:T(8,128)}), f32[32,360,512]{2,1,0:T(8,128)}) %all-gather.4.cloned.1.call-update) | async-done | bytes 23592976 | tf_op jit(solution)/shard_map/all_gather | solution.py:648
  677.4 49.1 %spectral_backward.1 = f32[48,2,80,256]{3,2,1,0:T(8,128)} custom-call(f32[32,360,512]{2,1,0:T(8,128)} %all-gather.4.cloned.1.call-done.grid_ref, f32[8,360,640]{2,1,0:T(8,128)} %bitcast.216, f32[45,46,256]{2,1,0:T(8,128)} %copy-done.1, f32[45,46,256]{2,1,0:T(8,128)} %copy-done.2), custom_call_target="tpu_custom_call" | custom-call | tf_op jit(solution)/shard_map/spectral_backward/pallas_call | solution.py:448
  726.4 3.9 fusion.88
  735.6 16.8 %fusion = f32[80,256,1,1]{1,0,3,2:T(8,128)S(1)} fusion(f32[45,2,256,256]{3,2,1,0:T(8,128)} %refs_2_.3, f32[48,2,80,256]{3,2,1,0:T(8,128)} %spectral_backward.1), kind=kOutput, calls=%fused_computation | convolution fusion | flops 2831155200 | bytes 31047680 | tf_op jit(solution)/shard_map/tpck,tpdk->cd/dot_general | solution.py:32
  754.0 22.5 %collective-permute-done.27 = f32[40,256]{1,0:T(8,128)S(1)} collective-permute-done((f32[40,256]{1,0:T(8,128)S(1)}, f32[40,256]{1,0:T(8,128)S(1)}, u32[]{:S(2)}, u32[]{:S(2)}) %collective-permute-start.27) | collective-permute-done | bytes 40992 | tf_op jit(solution)/shard_map/ppermute | solution.py:262
  798.0 7.1 collective-permute-done.19
  820.6 12.5 %collective-permute-done.22 = f32[8,128]{1,0:T(8,128)S(1)} collective-permute-done((f32[8,128]{1,0:T(8,128)S(1)}, f32[8,128]{1,0:T(8,128)S(1)}, u32[]{:S(2)}, u32[]{:S(2)}) %collective-permute-start.22) | collective-permute-done | bytes 4128 | tf_op jit(solution)/shard_map/ppermute | solution.py:262
  860.2 4.3 fusion.83
  864.5 30.9 %spectral_adam.2 = (f32[45,2,256,256]{3,2,1,0:T(8,128)}, f32[45,2,256,256]{3,2,1,0:T(8,128)}, f32[45,2,256,256]{3,2,1,0:T(8,128)}, bf16[45,2,256,256]{3,2,1,0:T(8,128)(2,1)}) custom-call(s32[8]{0:T(128)S(1)} %get-tuple-element.165.block_ref, s32[8]{0:T(128)S(1)} %get-tuple-element.164.thin_block_ref, f32[1]{0:T(128)} %bitcast.88.factor_ref, ...), custom_call_target="tpu_custom_call" | custom-call | tf_op jit(solution)/shard_map/spectral_adam/pallas_call | solution.py:489
  895.4 31.4 %spectral_adam.3 = (f32[45,2,256,256]{3,2,1,0:T(8,128)}, f32[45,2,256,256]{3,2,1,0:T(8,128)}, f32[45,2,256,256]{3,2,1,0:T(8,128)}, bf16[45,2,256,256]{3,2,1,0:T(8,128)(2,1)}) custom-call(s32[8]{0:T(128)S(1)} %get-tuple-element.163.block_ref, ...), custom_call_target="tpu_custom_call", output_to_operand_aliasing={{0}: (9, {}), {1}: (10, {}), {2}: (11, {}), {3}: (12, {})} | custom-call | tf_op jit(solution)/shard_map/spectral_adam/pallas_call | solution.py:489
  (268 shorter events, 157.2 us)
Async XLA Ops:
  7.2 130.6 %all-gather.6.cloned.1.call-start = ((), (), s32[]{:S(2)}) async-start(), calls=%async_computation.3 | async-start | bytes 8294400 | tf_op jit(solution)/shard_map/all_gather | solution.py:619
  19.0 24.8 %collective-permute-start = (f32[24,1536]{1,0:T(8,128)}, f32[24,1536]{1,0:T(8,128)}, u32[]{:S(2)}, u32[]{:S(2)}) collective-permute-start(f32[24,1536]{1,0:T(8,128)} %get-tuple-element.143), channel_id=1, source_target_pairs={{0,1},{1,0},{2,3},{3,2},{4,5},{5,4},{6,7},{7,6},{8,9},{9,8},{10,11... | collective-permute-start | bytes 442376 | tf_op jit(solution)/shard_map/ppermute | solution.py:262
  19.5 29.5 %collective-permute-start.1 = (f32[24,1536]{1,0:T(8,128)}, f32[24,1536]{1,0:T(8,128)}, u32[]{:S(2)}, u32[]{:S(2)}) collective-permute-start(f32[24,1536]{1,0:T(8,128)} %get-tuple-element.142), channel_id=1, source_target_pairs={{0,2},{1,3},{2,0},{3,1},{4,6},{5,7},{6,4},{7,5},{8,10},{9,11},{10,... | collective-permute-start | bytes 442376 | tf_op jit(solution)/shard_map/ppermute | solution.py:262
  22.0 28.6 %collective-permute-start.2 = (f32[24,1536]{1,0:T(8,128)}, f32[24,1536]{1,0:T(8,128)}, u32[]{:S(2)}, u32[]{:S(2)}) collective-permute-start(f32[24,1536]{1,0:T(8,128)} %get-tuple-element.141), channel_id=1, source_target_pairs={{0,3},{1,2},{2,1},{3,0},{4,7},{5,6},{6,5},{7,4},{8,11},{9,10},{10,... | collective-permute-start | bytes 442376 | tf_op jit(solution)/shard_map/ppermute | solution.py:262
  22.2 30.1 %collective-permute-start.3 = (f32[24,1536]{1,0:T(8,128)}, f32[24,1536]{1,0:T(8,128)}, u32[]{:S(2)}, u32[]{:S(2)}) collective-permute-start(f32[24,1536]{1,0:T(8,128)} %get-tuple-element.140), channel_id=1, source_target_pairs={{0,4},{1,5},{2,6},{3,7},{4,0},{5,1},{6,2},{7,3},{8,12},{9,13},{10,... | collective-permute-start | bytes 442376 | tf_op jit(solution)/shard_map/ppermute | solution.py:262
  24.9 28.9 %collective-permute-start.4 = (f32[24,1536]{1,0:T(8,128)}, f32[24,1536]{1,0:T(8,128)}, u32[]{:S(2)}, u32[]{:S(2)}) collective-permute-start(f32[24,1536]{1,0:T(8,128)} %get-tuple-element.139), channel_id=1, source_target_pairs={{0,5},{1,4},{2,7},{3,6},{4,1},{5,0},{6,3},{7,2},{8,13},{9,12},{10,... | collective-permute-start | bytes 442376 | tf_op jit(solution)/shard_map/ppermute | solution.py:262
  43.8 11.7 %collective-permute-start.5 = (f32[24,1536]{1,0:T(8,128)S(1)}, f32[24,1536]{1,0:T(8,128)S(1)}, u32[]{:S(2)}, u32[]{:S(2)}) collective-permute-start(f32[24,1536]{1,0:T(8,128)S(1)} %get-tuple-element.138), channel_id=1, source_target_pairs={{0,6},{1,7},{2,4},{3,5},{4,2},{5,3},{6,0},{7,1},{8,14},{9,15},{10,... | collective-permute-start | bytes 442376 | tf_op jit(solution)/shard_map/ppermute | solution.py:262
  49.0 7.7 collective-permute-start.6
  58.6 362.5 %reduce-scatter.2.cloned.1.call-start = ((), (), s32[]{:S(2)}) async-start(), calls=%async_computation.1 | async-start | bytes 26542080 | tf_op jit(solution)/shard_map/reduce_scatter | solution.py:621
  58.8 17.9 %collective-permute-start.9 = (f32[1,4,24,1536]{3,2,1,0:T(8,128)S(1)}, f32[1,4,24,1536]{3,2,1,0:T(8,128)S(1)}, u32[]{:S(2)}, u32[]{:S(2)}) collective-permute-start(f32[1,4,24,1536]{3,2,1,0:T(8,128)S(1)} %get-tuple-element.134), channel_id=1, source_target_pairs={{0,16},{8,24},{16,0},{24,8},{1,17},{9,25},{17,1},{25,9},{2,18},{10... | collective-permute-start | bytes 1769480 | tf_op jit(solution)/shard_map/ppermute | solution.py:262
  63.1 16.2 %collective-permute-start.7 = (f32[1,4,24,1536]{3,2,1,0:T(8,128)S(1)}, f32[1,4,24,1536]{3,2,1,0:T(8,128)S(1)}, u32[]{:S(2)}, u32[]{:S(2)}) collective-permute-start(f32[1,4,24,1536]{3,2,1,0:T(8,128)S(1)} %get-tuple-element.133), channel_id=1, source_target_pairs={{0,8},{8,0},{16,24},{24,16},{1,9},{9,1},{17,25},{25,17},{2,10},{10... | collective-permute-start | bytes 1769480 | tf_op jit(solution)/shard_map/ppermute | solution.py:262
  77.8 27.9 %collective-permute-start.10 = (f32[2,4,24,1536]{3,2,1,0:T(8,128)}, f32[2,4,24,1536]{3,2,1,0:T(8,128)}, u32[]{:S(2)}, u32[]{:S(2)}) collective-permute-start(f32[2,4,24,1536]{3,2,1,0:T(8,128)} %pad_maximum_fusion.4), channel_id=1, source_target_pairs={{0,8},{8,0},{16,24},{24,16},{1,9},{9,1},{17,25},{25,17},{2,10},{10... | collective-permute-start | bytes 3538952 | tf_op jit(solution)/shard_map/ppermute | solution.py:262
  80.4 27.7 %collective-permute-start.8 = (f32[2,4,24,1536]{3,2,1,0:T(8,128)}, f32[2,4,24,1536]{3,2,1,0:T(8,128)}, u32[]{:S(2)}, u32[]{:S(2)}) collective-permute-start(f32[2,4,24,1536]{3,2,1,0:T(8,128)} %pad_maximum_fusion.3), channel_id=1, source_target_pairs={{0,16},{8,24},{16,0},{24,8},{1,17},{9,25},{17,1},{25,9},{2,18},{10... | collective-permute-start | bytes 3538952 | tf_op jit(solution)/shard_map/ppermute | solution.py:262
  190.0 487.4 %all-gather.4.cloned.1.call-start = ((), (), s32[]{:S(2)}) async-start(), calls=%async_computation.2 | async-start | bytes 26542080 | tf_op jit(solution)/shard_map/all_gather | solution.py:648
  493.4 13.2 %collective-permute-start.11 = (f32[592,256]{1,0:T(8,128)S(1)}, f32[592,256]{1,0:T(8,128)S(1)}, u32[]{:S(2)}, u32[]{:S(2)}) collective-permute-start(f32[592,256]{1,0:T(8,128)S(1)} %dynamic-slice_bitcast_fusion.4), channel_id=1, source_target_pairs={{0,8},{8,0},{16,24},{24,16},{1,9},{9,1},{17,25},{25,17},{2,10},{10... | collective-permute-start | bytes 1818632 | tf_op jit(solution)/shard_map/ppermute | solution.py:262
  515.3 33.2 %collective-permute-start.14 = (f32[296,256]{1,0:T(8,128)S(1)}, f32[296,256]{1,0:T(8,128)S(1)}, u32[]{:S(2)}, u32[]{:S(2)}) collective-permute-start(f32[296,256]{1,0:T(8,128)S(1)} %add.324), channel_id=1, source_target_pairs={{0,2},{1,3},{2,0},{3,1},{4,6},{5,7},{6,4},{7,5},{8,10},{9,11},{10,... | collective-permute-start | bytes 909320 | tf_op jit(solution)/shard_map/ppermute | solution.py:262
  548.6 31.1 %collective-permute-start.15 = (f32[296,256]{1,0:T(8,128)S(1)}, f32[296,256]{1,0:T(8,128)S(1)}, u32[]{:S(2)}, u32[]{:S(2)}) collective-permute-start(f32[296,256]{1,0:T(8,128)S(1)} %add.325), channel_id=1, source_target_pairs={{0,4},{1,5},{2,6},{3,7},{4,0},{5,1},{6,2},{7,3},{8,12},{9,13},{10,... | collective-permute-start | bytes 909320 | tf_op jit(solution)/shard_map/ppermute | solution.py:262
  579.7 8.5 collective-permute-start.16
  588.3 14.1 %collective-permute-start.17 = (f32[592,256]{1,0:T(8,128)S(1)}, f32[592,256]{1,0:T(8,128)S(1)}, u32[]{:S(2)}, u32[]{:S(2)}) collective-permute-start(f32[592,256]{1,0:T(8,128)S(1)} %pad_maximum_fusion.5), channel_id=1, source_target_pairs={{0,8},{8,0},{16,24},{24,16},{1,9},{9,1},{17,25},{25,17},{2,10},{10... | collective-permute-start | bytes 1818632 | tf_op jit(solution)/shard_map/ppermute | solution.py:262
  730.5 47.5 %collective-permute-start.18 = (f32[24,80,256]{2,1,0:T(8,128)S(1)}, f32[24,80,256]{2,1,0:T(8,128)}, u32[]{:S(2)}, u32[]{:S(2)}) collective-permute-start(f32[24,80,256]{2,1,0:T(8,128)S(1)} %dynamic-slice_bitcast_fusion.1), channel_id=1, source_target_pairs={{0,8},{8,0},{16,24},{24,16},{1,9},{9,1},{17,25},{25,17},{2,10},{10... | collective-permute-start | bytes 5898248 | tf_op jit(solution)/shard_map/ppermute | solution.py:262
  734.2 48.3 %collective-permute-start.20 = (f32[24,80,256]{2,1,0:T(8,128)}, f32[24,80,256]{2,1,0:T(8,128)}, u32[]{:S(2)}, u32[]{:S(2)}) collective-permute-start(f32[24,80,256]{2,1,0:T(8,128)} %dynamic-slice_bitcast_fusion), channel_id=1, source_target_pairs={{0,16},{8,24},{16,0},{24,8},{1,17},{9,25},{17,1},{25,9},{2,18},{10... | collective-permute-start | bytes 5898248 | tf_op jit(solution)/shard_map/ppermute | solution.py:262
  752.4 24.0 %collective-permute-start.27 = (f32[40,256]{1,0:T(8,128)S(1)}, f32[40,256]{1,0:T(8,128)S(1)}, u32[]{:S(2)}, u32[]{:S(2)}) collective-permute-start(f32[40,256]{1,0:T(8,128)S(1)} %dynamic-slice_bitcast_fusion.13), channel_id=1, source_target_pairs={{0,8},{8,0},{16,24},{24,16},{1,9},{9,1},{17,25},{25,17},{2,10},{10... | collective-permute-start | bytes 122888 | tf_op jit(solution)/shard_map/ppermute | solution.py:262
  776.5 10.4 %collective-permute-start.28 = (f32[20,256]{1,0:T(8,128)S(1)}, f32[20,256]{1,0:T(8,128)S(1)}, u32[]{:S(2)}, u32[]{:S(2)}) collective-permute-start(f32[20,256]{1,0:T(8,128)S(1)} %dynamic-slice_bitcast_fusion.14), channel_id=1, source_target_pairs={{0,16},{8,24},{16,0},{24,8},{1,17},{9,25},{17,1},{25,9},{2,18},{10... | collective-permute-start | bytes 61448 | tf_op jit(solution)/shard_map/ppermute | solution.py:262
  781.6 23.5 %collective-permute-start.19 = (f32[12,80,256]{2,1,0:T(8,128)}, f32[12,80,256]{2,1,0:T(8,128)}, u32[]{:S(2)}, u32[]{:S(2)}) collective-permute-start(f32[12,80,256]{2,1,0:T(8,128)} %dynamic-slice_bitcast_fusion.3), channel_id=1, source_target_pairs={{0,16},{8,24},{16,0},{24,8},{1,17},{9,25},{17,1},{25,9},{2,18},{10... | collective-permute-start | bytes 2949128 | tf_op jit(solution)/shard_map/ppermute | solution.py:262
  785.5 22.9 %collective-permute-start.21 = (f32[12,80,256]{2,1,0:T(8,128)}, f32[12,80,256]{2,1,0:T(8,128)}, u32[]{:S(2)}, u32[]{:S(2)}) collective-permute-start(f32[12,80,256]{2,1,0:T(8,128)} %dynamic-slice_bitcast_fusion.2), channel_id=1, source_target_pairs={{0,8},{8,0},{16,24},{24,16},{1,9},{9,1},{17,25},{25,17},{2,10},{10... | collective-permute-start | bytes 2949128 | tf_op jit(solution)/shard_map/ppermute | solution.py:262
  796.8 10.7 %collective-permute-start.32 = (f32[20,256]{1,0:T(8,128)S(1)}, f32[20,256]{1,0:T(8,128)S(1)}, u32[]{:S(2)}, u32[]{:S(2)}) collective-permute-start(f32[20,256]{1,0:T(8,128)S(1)} %add.341), channel_id=1, source_target_pairs={{0,16},{8,24},{16,0},{24,8},{1,17},{9,25},{17,1},{25,9},{2,18},{10... | collective-permute-start | bytes 61448 | tf_op jit(solution)/shard_map/ppermute | solution.py:262
  806.7 27.7 %collective-permute-start.34 = (f32[12,80,256]{2,1,0:T(8,128)S(1)}, f32[12,80,256]{2,1,0:T(8,128)S(1)}, u32[]{:S(2)}, u32[]{:S(2)}) collective-permute-start(f32[12,80,256]{2,1,0:T(8,128)S(1)} %bitcast_add_fusion.4), channel_id=1, source_target_pairs={{0,16},{8,24},{16,0},{24,8},{1,17},{9,25},{17,1},{25,9},{2,18},{10... | collective-permute-start | bytes 2949128 | tf_op jit(solution)/shard_map/ppermute | solution.py:262
  810.6 25.7 %collective-permute-start.36 = (f32[12,80,256]{2,1,0:T(8,128)}, f32[12,80,256]{2,1,0:T(8,128)}, u32[]{:S(2)}, u32[]{:S(2)}) collective-permute-start(f32[12,80,256]{2,1,0:T(8,128)} %bitcast_add_fusion.3), channel_id=1, source_target_pairs={{0,8},{8,0},{16,24},{24,16},{1,9},{9,1},{17,25},{25,17},{2,10},{10... | collective-permute-start | bytes 2949128 | tf_op jit(solution)/shard_map/ppermute | solution.py:262
  818.4 14.6 %collective-permute-start.22 = (f32[8,128]{1,0:T(8,128)S(1)}, f32[8,128]{1,0:T(8,128)S(1)}, u32[]{:S(2)}, u32[]{:S(2)}) collective-permute-start(f32[8,128]{1,0:T(8,128)S(1)} %broadcast_in_dim.71), channel_id=1, source_target_pairs={{0,8},{8,0},{16,24},{24,16},{1,9},{9,1},{17,25},{25,17},{2,10},{10... | collective-permute-start | bytes 12296 | tf_op jit(solution)/shard_map/ppermute | solution.py:262
  819.0 21.1 %collective-permute-start.33 = (f32[40,256]{1,0:T(8,128)S(1)}, f32[40,256]{1,0:T(8,128)S(1)}, u32[]{:S(2)}, u32[]{:S(2)}) collective-permute-start(f32[40,256]{1,0:T(8,128)S(1)} %pad_maximum_fusion.8), channel_id=1, source_target_pairs={{0,8},{8,0},{16,24},{24,16},{1,9},{9,1},{17,25},{25,17},{2,10},{10... | collective-permute-start | bytes 122888 | tf_op jit(solution)/shard_map/ppermute | solution.py:262
  834.7 60.7 %collective-permute-start.35 = (f32[24,80,256]{2,1,0:T(8,128)S(1)}, f32[24,80,256]{2,1,0:T(8,128)}, u32[]{:S(2)}, u32[]{:S(2)}) collective-permute-start(f32[24,80,256]{2,1,0:T(8,128)S(1)} %pad_maximum_fusion), channel_id=1, source_target_pairs={{0,8},{8,0},{16,24},{24,16},{1,9},{9,1},{17,25},{25,17},{2,10},{10... | collective-permute-start | bytes 5898248 | tf_op jit(solution)/shard_map/ppermute | solution.py:262
  839.4 56.0 %collective-permute-start.37 = (f32[24,80,256]{2,1,0:T(8,128)}, f32[24,80,256]{2,1,0:T(8,128)}, u32[]{:S(2)}, u32[]{:S(2)}) collective-permute-start(f32[24,80,256]{2,1,0:T(8,128)} %pad_maximum_fusion.1), channel_id=1, source_target_pairs={{0,16},{8,24},{16,0},{24,8},{1,17},{9,25},{17,1},{25,9},{2,18},{10... | collective-permute-start | bytes 5898248 | tf_op jit(solution)/shard_map/ppermute | solution.py:262
  (50 other events, 1221.8 us)
Sparse Core Ops, SparseCore 0:
  58.8 78.9 all-gather.5
  190.1 230.9 reduce-scatter.1
  459.1 218.2 all-gather.3

commit v6 on v5

--- a/solution.py
+++ b/solution.py
@@ -265,45 +265,25 @@
 def wire_kernel(degrees, me_ref, forward_ref, inverse_ref, wire_ref, turned_ref):
     own, lat, order_count = forward_ref.shape
     owners, half, lanes = wire_ref.shape
-    per_tile = 128 // lat
     me = me_ref[0]
 
-    @pl.when(me < 2)
-    def _():
+    def turn(table_ref):
         turned_ref[order_count:] = jnp.zeros((turned_ref.shape[0] - order_count, lanes), jnp.float32)
-        turned_ref[:order_count, : own * lat] = forward_ref[...].reshape(own * lat, order_count).T
+        turned_ref[:order_count, : own * lat] = table_ref[...].reshape(own * lat, order_count).T
         if lanes > own * lat:
             turned_ref[:order_count, own * lat :] = jnp.zeros(
                 (order_count, lanes - own * lat), jnp.float32
             )
 
-    def forward_part(part):
+    def hand_out(part):
         for owner in range(owners):
             first = owner * degrees + part * half
             wire_ref[owner] = turned_ref[first : first + half, :]
 
-    def inverse_part(part):
-        lane = lax.broadcasted_iota(jnp.int32, (half, 128), 1) // lat
-        for owner in range(owners):
-            first = owner * degrees + part * half
-            rows = min(half, order_count - first)
-            for tile in range(lanes // 128):
-                value = jnp.zeros((rows, 128), jnp.float32)
-                for place in range(per_tile):
-                    slot = tile * per_tile + place
-                    if slot < own:
-                        found = inverse_ref[slot, first : first + rows, :]
-                        found = jnp.concatenate([found] * per_tile, axis=1)
-                        value = jnp.where(lane[:rows] == place, found, value)
-                columns = slice(tile * 128, tile * 128 + 128)
-                wire_ref[owner, :rows, columns] = value
-                if rows < half:
-                    wire_ref[owner, rows:, columns] = jnp.zeros((half - rows, 128), jnp.float32)
-
-    pl.when(me == 0)(functools.partial(forward_part, 0))
-    pl.when(me == 1)(functools.partial(forward_part, 1))
-    pl.when(me == 2)(functools.partial(inverse_part, 0))
-    pl.when(me == 3)(functools.partial(inverse_part, 1))
+    pl.when(me < 2)(functools.partial(turn, forward_ref))
+    pl.when(me >= 2)(functools.partial(turn, inverse_ref))
+    pl.when(me % 2 == 0)(functools.partial(hand_out, 0))
+    pl.when(me % 2 == 1)(functools.partial(hand_out, 1))
 
 
 def tables_to_degrees(forward_table, inverse_table, wide_count, degree_slots, beside):
@@ -320,7 +300,7 @@
         scratch_shapes=[pltpu.VMEM((order_count + 2 * half - degree_slots + 8, lanes), jnp.float32)],
         compiler_params=pltpu.CompilerParams(vmem_limit_bytes=32 * 2**20),
         name="table_wire",
-    )(lax.axis_index("dp")[None], forward_table, inverse_table)
+    )(lax.axis_index("dp")[None], forward_table, inverse_table.transpose(0, 2, 1))
     me = lax.axis_index("wide")
     pieces = [lax.dynamic_index_in_dim(wire, me ^ k, 0, keepdims=False) for k in range(wide_count)]
     pieces = [pieces[0]] + [exchange(pieces[k], "wide", wide_count, k) for k in range(1, wide_count)]

time: 941 us -> 933 us (level)
    unnamed x92 -> x91, local copies, waits for them, and re-layouts: 25.1 us -> 18.3 us
where the time goes in v6:
time: 933 us; the launch traced here: 925 us
  waiting for transfers between devices  505 us (54%)
  Pallas kernels  174 us (19%)
  matrix products  100 us (11%)
  local copies, waits for them, and re-layouts  49.1 us (5%)
  starting transfers between devices  46.4 us (5%)
  other arithmetic  29.7 us (3%)
  between operations  20.8 us (2%)
    reduce_scatter x1, waiting for transfers between devices, body(): lax.psum_scatter(grid_coef, 'wide', scatter_dimension=0, tiled=True)  227 us
    ppermute x38, waiting for transfers between devices, exchange(): return lax.ppermute(value, axis, [(i, i ^ bit) for i in range(count)])  187 us
    dot_general x17, matrix products, dot(): return jnp.einsum(spec, left, right, precision=HIGH)  95.2 us
    all_gather x1, waiting for transfers between devices, body(): grid_grad = lax.all_gather(grid_grad, 'wide', axis=0, tiled=True)  74.7 us
    pallas_call x2, Pallas kernels, spectral_adam(): pl.pallas_call(functools.partial(adam_kernel, first_steps), grid_spec=plt...  62.3 us
    pallas_call x1, Pallas kernels, spectral_forward(): pl.pallas_call(functools.partial(forward_kernel, lat_dev, fields), grid=(...  51.8 us
    pallas_call x1, Pallas kernels, spectral_backward(): pl.pallas_call(functools.partial(backward_kernel, degrees, lat_dev, field...  49.1 us
    ppermute x38, starting transfers between devices, exchange(): return lax.ppermute(value, axis, [(i, i ^ bit) for i in range(count)])  45.7 us
  transfers between devices with their start and end apart: 41, of which 24 were waited for; matrix products, arithmetic and copies ran while one was open for 14% of the time, Pallas kernels for 4%

profile of v6, /device:TPU:0, one launch (start us, length us, event | category | flops | bytes accessed | tf_op | source)
XLA Modules:
  0.0 925.0 jit_solution(138053932943108367)
XLA Ops:
  22.0 14.9 %convolution_bitcast_fusion.folded_ref = f32[45,2,80,256]{3,2,1,0:T(8,128)} fusion(f32[45,2,256,256]{3,2,1,0:T(8,128)} %refs_2_.3, f32[80,256]{1,0:T(8,128)S(1)} %maximum_maximum_fusion.2.encoder_ref), kind=kOutput, calls=%fused_computation.20 | convolution fusion | flops 2831155200 | bytes 31047680 | tf_op jit(solution)/shard_map/cd,tpdk->tpck/dot_general | solution.py:32
  55.4 12.4 %collective-permute-done.9 = f32[1,4,24,1536]{3,2,1,0:T(8,128)S(1)} collective-permute-done((f32[1,4,24,1536]{3,2,1,0:T(8,128)S(1)}, f32[1,4,24,1536]{3,2,1,0:T(8,128)S(1)}, u32[]{:S(2)}, u32[]{:S(2)}) %collective-permute-start.9) | collective-permute-done | bytes 589856 | tf_op jit(solution)/shard_map/ppermute | solution.py:262
  73.8 3.8 sort.17
  77.6 18.8 %collective-permute-done.10 = f32[2,4,24,1536]{3,2,1,0:T(8,128)} collective-permute-done((f32[2,4,24,1536]{3,2,1,0:T(8,128)}, f32[2,4,24,1536]{3,2,1,0:T(8,128)}, u32[]{:S(2)}, u32[]{:S(2)}) %collective-permute-start.10) | collective-permute-done | bytes 1179680 | tf_op jit(solution)/shard_map/ppermute | solution.py:262
  100.4 10.2 %table_rows.1 = (f32[45,46,256]{2,1,0:T(8,128)S(1)}, f32[45,46,256]{2,1,0:T(8,128)S(1)}) custom-call(s32[2]{0:T(128)S(1)} %pad_add_fusion.me_ref, s32[360]{0:T(512)S(1)} %get-tuple-element.36.slot_ref, f32[4,8,24,1536]{3,2,1,0:T(8,128)S(1)} %maximum_maximum_fusion.wire_ref, s32[48,1]{1,0:T(8,128)S(1)} %copy.106.degree_ref, bf16[256,256]{1,0:T(8,128)(2,1)S(1)} %copy-done.4), custom_call_target="tpu_custom_call" | custom-call | tf_op jit(solution)/shard_map/table_rows/pallas_call | solution.py:250
  113.4 15.0 %all-gather.6.cloned.1.call-done = f32[2880,640]{1,0:T(8,128)} async-done(((f32[360,640]{1,0:T(8,128)}), f32[2880,640]{1,0:T(8,128)}) %all-gather.6.cloned.1.call-update) | async-done | bytes 7372816 | tf_op jit(solution)/shard_map/all_gather | solution.py:599
  128.4 51.8 %spectral_forward.1 = f32[32,360,512]{2,1,0:T(8,128)} custom-call(f32[8,360,640]{2,1,0:T(8,128)} %bitcast.217, f32[45,46,256]{2,1,0:T(8,128)} %copy-done, f32[45,46,256]{2,1,0:T(8,128)} %copy-done.1, f32[45,2,80,256]{3,2,1,0:T(8,128)} %convolution_bitcast_fusion.folded_ref), custom_call_target="tpu_custom_call" | custom-call | tf_op jit(solution)/shard_map/spectral_forward/pallas_call | solution.py:396
  183.9 227.4 %reduce-scatter.2.cloned.1.call-done = f32[4,360,512]{2,1,0:T(8,128)} async-done(((f32[32,360,512]{2,1,0:T(8,128)}), f32[4,360,512]{2,1,0:T(8,128)}) %reduce-scatter.2.cloned.1.call-update) | async-done | bytes 2949136 | tf_op jit(solution)/shard_map/reduce_scatter | solution.py:601
  411.3 7.2 bitcast_add_fusion
  421.1 4.3 add_add_fusion
  429.7 10.1 %fusion.93 = (f32[512]{0:T(512)}, f32[4,720,512]{2,1,0:T(8,128)S(1)}) fusion(f32[4,720,512]{2,1,0:T(8,128)S(1)} %fusion.38, f32[512]{0:T(512)S(1)} %slice.101, f32[4,720,256]{2,1,0:T(8,128)S(1)} %get-tuple-element.160, f32[2,256,512]{2,1,0:T(8,128)S(1)} %copy-done.20), kind=kOutput, calls=%fused_computation.187 | convolution fusion | flops 2295889408 | bytes 15273984 | tf_op jit(solution)/shard_map/ajk,kh->ajh/dot_general | solution.py:32
  443.1 3.9 fusion.16
  449.1 6.1 convolution_bitcast_fusion.3
  456.4 10.4 %fusion.25 = f32[256,512]{1,0:T(8,128)} fusion(f32[4,720,256]{2,1,0:T(8,128)} %copy-done.12, f32[4,720,512]{2,1,0:T(8,128)} %copy-done.19, f32[512]{0:T(512)} %copy-done.39), kind=kOutput, calls=%fused_computation.40 | convolution fusion | flops 2278195200 | bytes 9373696 | tf_op jit(solution)/shard_map/ajk,ajh->kh/dot_general | solution.py:32
  474.1 3.7 convolution_bitcast_fusion.4
  485.0 11.8 %collective-permute-done.11 = f32[592,256]{1,0:T(8,128)S(1)} collective-permute-done((f32[592,256]{1,0:T(8,128)S(1)}, f32[592,256]{1,0:T(8,128)S(1)}, u32[]{:S(2)}, u32[]{:S(2)}) %collective-permute-start.11) | collective-permute-done | bytes 606240 | tf_op jit(solution)/shard_map/ppermute | solution.py:262
  498.4 5.3 collective-permute-done.12
  505.5 4.4 collective-permute-start.14
  509.9 28.8 %collective-permute-done.14 = f32[296,256]{1,0:T(8,128)S(1)} collective-permute-done((f32[296,256]{1,0:T(8,128)S(1)}, f32[296,256]{1,0:T(8,128)S(1)}, u32[]{:S(2)}, u32[]{:S(2)}) %collective-permute-start.14) | collective-permute-done | bytes 303136 | tf_op jit(solution)/shard_map/ppermute | solution.py:262
  539.1 30.8 %collective-permute-done.15 = f32[296,256]{1,0:T(8,128)S(1)} collective-permute-done((f32[296,256]{1,0:T(8,128)S(1)}, f32[296,256]{1,0:T(8,128)S(1)}, u32[]{:S(2)}, u32[]{:S(2)}) %collective-permute-start.15) | collective-permute-done | bytes 303136 | tf_op jit(solution)/shard_map/ppermute | solution.py:262
  571.4 6.9 collective-permute-done.16
  580.3 12.3 %collective-permute-done.17 = f32[592,256]{1,0:T(8,128)S(1)} collective-permute-done((f32[592,256]{1,0:T(8,128)S(1)}, f32[592,256]{1,0:T(8,128)S(1)}, u32[]{:S(2)}, u32[]{:S(2)}) %collective-permute-start.17) | collective-permute-done | bytes 606240 | tf_op jit(solution)/shard_map/ppermute | solution.py:262
  592.8 74.7 %all-gather.4.cloned.1.call-done.grid_ref = f32[32,360,512]{2,1,0:T(8,128)} async-done(((f32[4,360,512]{2,1,0:T(8,128)}), f32[32,360,512]{2,1,0:T(8,128)}) %all-gather.4.cloned.1.call-update) | async-done | bytes 23592976 | tf_op jit(solution)/shard_map/all_gather | solution.py:628
  667.5 49.1 %spectral_backward.1 = f32[48,2,80,256]{3,2,1,0:T(8,128)} custom-call(f32[32,360,512]{2,1,0:T(8,128)} %all-gather.4.cloned.1.call-done.grid_ref, f32[8,360,640]{2,1,0:T(8,128)} %bitcast.218, f32[45,46,256]{2,1,0:T(8,128)} %copy-done, f32[45,46,256]{2,1,0:T(8,128)} %copy-done.1), custom_call_target="tpu_custom_call" | custom-call | tf_op jit(solution)/shard_map/spectral_backward/pallas_call | solution.py:428
  716.6 3.9 fusion.88
  725.8 16.8 %fusion = f32[80,256,1,1]{1,0,3,2:T(8,128)S(1)} fusion(f32[45,2,256,256]{3,2,1,0:T(8,128)} %refs_2_.3, f32[48,2,80,256]{3,2,1,0:T(8,128)} %spectral_backward.1), kind=kOutput, calls=%fused_computation | convolution fusion | flops 2831155200 | bytes 31047680 | tf_op jit(solution)/shard_map/tpck,tpdk->cd/dot_general | solution.py:32
  744.1 22.5 %collective-permute-done.27 = f32[40,256]{1,0:T(8,128)S(1)} collective-permute-done((f32[40,256]{1,0:T(8,128)S(1)}, f32[40,256]{1,0:T(8,128)S(1)}, u32[]{:S(2)}, u32[]{:S(2)}) %collective-permute-start.27) | collective-permute-done | bytes 40992 | tf_op jit(solution)/shard_map/ppermute | solution.py:262
  788.1 7.1 collective-permute-done.19
  810.7 12.5 %collective-permute-done.22 = f32[8,128]{1,0:T(8,128)S(1)} collective-permute-done((f32[8,128]{1,0:T(8,128)S(1)}, f32[8,128]{1,0:T(8,128)S(1)}, u32[]{:S(2)}, u32[]{:S(2)}) %collective-permute-start.22) | collective-permute-done | bytes 4128 | tf_op jit(solution)/shard_map/ppermute | solution.py:262
  850.4 4.3 fusion.83
  854.6 30.9 %spectral_adam.2 = (f32[45,2,256,256]{3,2,1,0:T(8,128)}, f32[45,2,256,256]{3,2,1,0:T(8,128)}, f32[45,2,256,256]{3,2,1,0:T(8,128)}, bf16[45,2,256,256]{3,2,1,0:T(8,128)(2,1)}) custom-call(s32[8]{0:T(128)S(1)} %get-tuple-element.165.block_ref, s32[8]{0:T(128)S(1)} %get-tuple-element.164.thin_block_ref, f32[1]{0:T(128)} %bitcast.89.factor_ref, ...), custom_call_target="tpu_custom_call" | custom-call | tf_op jit(solution)/shard_map/spectral_adam/pallas_call | solution.py:469
  885.6 31.4 %spectral_adam.3 = (f32[45,2,256,256]{3,2,1,0:T(8,128)}, f32[45,2,256,256]{3,2,1,0:T(8,128)}, f32[45,2,256,256]{3,2,1,0:T(8,128)}, bf16[45,2,256,256]{3,2,1,0:T(8,128)(2,1)}) custom-call(s32[8]{0:T(128)S(1)} %get-tuple-element.163.block_ref, ...), custom_call_target="tpu_custom_call", output_to_operand_aliasing={{0}: (9, {}), {1}: (10, {}), {2}: (11, {}), {3}: (12, {})} | custom-call | tf_op jit(solution)/shard_map/spectral_adam/pallas_call | solution.py:469
  (267 shorter events, 150.9 us)
Async XLA Ops:
  7.2 121.2 %all-gather.6.cloned.1.call-start = ((), (), s32[]{:S(2)}) async-start(), calls=%async_computation.3 | async-start | bytes 8294400 | tf_op jit(solution)/shard_map/all_gather | solution.py:599
  12.3 24.8 %collective-permute-start = (f32[24,1536]{1,0:T(8,128)}, f32[24,1536]{1,0:T(8,128)}, u32[]{:S(2)}, u32[]{:S(2)}) collective-permute-start(f32[24,1536]{1,0:T(8,128)} %get-tuple-element.143), channel_id=1, source_target_pairs={{0,1},{1,0},{2,3},{3,2},{4,5},{5,4},{6,7},{7,6},{8,9},{9,8},{10,11... | collective-permute-start | bytes 442376 | tf_op jit(solution)/shard_map/ppermute | solution.py:262
  12.7 29.5 %collective-permute-start.1 = (f32[24,1536]{1,0:T(8,128)}, f32[24,1536]{1,0:T(8,128)}, u32[]{:S(2)}, u32[]{:S(2)}) collective-permute-start(f32[24,1536]{1,0:T(8,128)} %get-tuple-element.142), channel_id=1, source_target_pairs={{0,2},{1,3},{2,0},{3,1},{4,6},{5,7},{6,4},{7,5},{8,10},{9,11},{10,... | collective-permute-start | bytes 442376 | tf_op jit(solution)/shard_map/ppermute | solution.py:262
  15.3 28.6 %collective-permute-start.2 = (f32[24,1536]{1,0:T(8,128)}, f32[24,1536]{1,0:T(8,128)}, u32[]{:S(2)}, u32[]{:S(2)}) collective-permute-start(f32[24,1536]{1,0:T(8,128)} %get-tuple-element.141), channel_id=1, source_target_pairs={{0,3},{1,2},{2,1},{3,0},{4,7},{5,6},{6,5},{7,4},{8,11},{9,10},{10,... | collective-permute-start | bytes 442376 | tf_op jit(solution)/shard_map/ppermute | solution.py:262
  15.4 30.1 %collective-permute-start.3 = (f32[24,1536]{1,0:T(8,128)}, f32[24,1536]{1,0:T(8,128)}, u32[]{:S(2)}, u32[]{:S(2)}) collective-permute-start(f32[24,1536]{1,0:T(8,128)} %get-tuple-element.140), channel_id=1, source_target_pairs={{0,4},{1,5},{2,6},{3,7},{4,0},{5,1},{6,2},{7,3},{8,12},{9,13},{10,... | collective-permute-start | bytes 442376 | tf_op jit(solution)/shard_map/ppermute | solution.py:262
  18.2 28.9 %collective-permute-start.4 = (f32[24,1536]{1,0:T(8,128)}, f32[24,1536]{1,0:T(8,128)}, u32[]{:S(2)}, u32[]{:S(2)}) collective-permute-start(f32[24,1536]{1,0:T(8,128)} %get-tuple-element.139), channel_id=1, source_target_pairs={{0,5},{1,4},{2,7},{3,6},{4,1},{5,0},{6,3},{7,2},{8,13},{9,12},{10,... | collective-permute-start | bytes 442376 | tf_op jit(solution)/shard_map/ppermute | solution.py:262
  37.0 11.7 %collective-permute-start.5 = (f32[24,1536]{1,0:T(8,128)S(1)}, f32[24,1536]{1,0:T(8,128)S(1)}, u32[]{:S(2)}, u32[]{:S(2)}) collective-permute-start(f32[24,1536]{1,0:T(8,128)S(1)} %get-tuple-element.138), channel_id=1, source_target_pairs={{0,6},{1,7},{2,4},{3,5},{4,2},{5,3},{6,0},{7,1},{8,14},{9,15},{10,... | collective-permute-start | bytes 442376 | tf_op jit(solution)/shard_map/ppermute | solution.py:262
  42.2 7.7 collective-permute-start.6
  51.9 359.4 %reduce-scatter.2.cloned.1.call-start = ((), (), s32[]{:S(2)}) async-start(), calls=%async_computation.1 | async-start | bytes 26542080 | tf_op jit(solution)/shard_map/reduce_scatter | solution.py:601
  52.3 15.5 %collective-permute-start.9 = (f32[1,4,24,1536]{3,2,1,0:T(8,128)S(1)}, f32[1,4,24,1536]{3,2,1,0:T(8,128)S(1)}, u32[]{:S(2)}, u32[]{:S(2)}) collective-permute-start(f32[1,4,24,1536]{3,2,1,0:T(8,128)S(1)} %get-tuple-element.134), channel_id=1, source_target_pairs={{0,16},{8,24},{16,0},{24,8},{1,17},{9,25},{17,1},{25,9},{2,18},{10... | collective-permute-start | bytes 1769480 | tf_op jit(solution)/shard_map/ppermute | solution.py:262
  53.9 16.4 %collective-permute-start.7 = (f32[1,4,24,1536]{3,2,1,0:T(8,128)S(1)}, f32[1,4,24,1536]{3,2,1,0:T(8,128)S(1)}, u32[]{:S(2)}, u32[]{:S(2)}) collective-permute-start(f32[1,4,24,1536]{3,2,1,0:T(8,128)S(1)} %get-tuple-element.133), channel_id=1, source_target_pairs={{0,8},{8,0},{16,24},{24,16},{1,9},{9,1},{17,25},{25,17},{2,10},{10... | collective-permute-start | bytes 1769480 | tf_op jit(solution)/shard_map/ppermute | solution.py:262
  68.8 27.6 %collective-permute-start.10 = (f32[2,4,24,1536]{3,2,1,0:T(8,128)}, f32[2,4,24,1536]{3,2,1,0:T(8,128)}, u32[]{:S(2)}, u32[]{:S(2)}) collective-permute-start(f32[2,4,24,1536]{3,2,1,0:T(8,128)} %pad_maximum_fusion.4), channel_id=1, source_target_pairs={{0,8},{8,0},{16,24},{24,16},{1,9},{9,1},{17,25},{25,17},{2,10},{10... | collective-permute-start | bytes 3538952 | tf_op jit(solution)/shard_map/ppermute | solution.py:262
  71.4 27.3 %collective-permute-start.8 = (f32[2,4,24,1536]{3,2,1,0:T(8,128)}, f32[2,4,24,1536]{3,2,1,0:T(8,128)}, u32[]{:S(2)}, u32[]{:S(2)}) collective-permute-start(f32[2,4,24,1536]{3,2,1,0:T(8,128)} %pad_maximum_fusion.3), channel_id=1, source_target_pairs={{0,16},{8,24},{16,0},{24,8},{1,17},{9,25},{17,1},{25,9},{2,18},{10... | collective-permute-start | bytes 3538952 | tf_op jit(solution)/shard_map/ppermute | solution.py:262
  180.2 487.3 %all-gather.4.cloned.1.call-start = ((), (), s32[]{:S(2)}) async-start(), calls=%async_computation.2 | async-start | bytes 26542080 | tf_op jit(solution)/shard_map/all_gather | solution.py:628
  483.5 13.2 %collective-permute-start.11 = (f32[592,256]{1,0:T(8,128)S(1)}, f32[592,256]{1,0:T(8,128)S(1)}, u32[]{:S(2)}, u32[]{:S(2)}) collective-permute-start(f32[592,256]{1,0:T(8,128)S(1)} %dynamic-slice_bitcast_fusion.4), channel_id=1, source_target_pairs={{0,8},{8,0},{16,24},{24,16},{1,9},{9,1},{17,25},{25,17},{2,10},{10... | collective-permute-start | bytes 1818632 | tf_op jit(solution)/shard_map/ppermute | solution.py:262
  505.5 33.2 %collective-permute-start.14 = (f32[296,256]{1,0:T(8,128)S(1)}, f32[296,256]{1,0:T(8,128)S(1)}, u32[]{:S(2)}, u32[]{:S(2)}) collective-permute-start(f32[296,256]{1,0:T(8,128)S(1)} %add.324), channel_id=1, source_target_pairs={{0,2},{1,3},{2,0},{3,1},{4,6},{5,7},{6,4},{7,5},{8,10},{9,11},{10,... | collective-permute-start | bytes 909320 | tf_op jit(solution)/shard_map/ppermute | solution.py:262
  538.7 31.1 %collective-permute-start.15 = (f32[296,256]{1,0:T(8,128)S(1)}, f32[296,256]{1,0:T(8,128)S(1)}, u32[]{:S(2)}, u32[]{:S(2)}) collective-permute-start(f32[296,256]{1,0:T(8,128)S(1)} %add.325), channel_id=1, source_target_pairs={{0,4},{1,5},{2,6},{3,7},{4,0},{5,1},{6,2},{7,3},{8,12},{9,13},{10,... | collective-permute-start | bytes 909320 | tf_op jit(solution)/shard_map/ppermute | solution.py:262
  569.9 8.5 collective-permute-start.16
  578.4 14.1 %collective-permute-start.17 = (f32[592,256]{1,0:T(8,128)S(1)}, f32[592,256]{1,0:T(8,128)S(1)}, u32[]{:S(2)}, u32[]{:S(2)}) collective-permute-start(f32[592,256]{1,0:T(8,128)S(1)} %pad_maximum_fusion.5), channel_id=1, source_target_pairs={{0,8},{8,0},{16,24},{24,16},{1,9},{9,1},{17,25},{25,17},{2,10},{10... | collective-permute-start | bytes 1818632 | tf_op jit(solution)/shard_map/ppermute | solution.py:262
  720.7 47.5 %collective-permute-start.18 = (f32[24,80,256]{2,1,0:T(8,128)S(1)}, f32[24,80,256]{2,1,0:T(8,128)}, u32[]{:S(2)}, u32[]{:S(2)}) collective-permute-start(f32[24,80,256]{2,1,0:T(8,128)S(1)} %dynamic-slice_bitcast_fusion.1), channel_id=1, source_target_pairs={{0,8},{8,0},{16,24},{24,16},{1,9},{9,1},{17,25},{25,17},{2,10},{10... | collective-permute-start | bytes 5898248 | tf_op jit(solution)/shard_map/ppermute | solution.py:262
  724.3 48.3 %collective-permute-start.20 = (f32[24,80,256]{2,1,0:T(8,128)}, f32[24,80,256]{2,1,0:T(8,128)}, u32[]{:S(2)}, u32[]{:S(2)}) collective-permute-start(f32[24,80,256]{2,1,0:T(8,128)} %dynamic-slice_bitcast_fusion), channel_id=1, source_target_pairs={{0,16},{8,24},{16,0},{24,8},{1,17},{9,25},{17,1},{25,9},{2,18},{10... | collective-permute-start | bytes 5898248 | tf_op jit(solution)/shard_map/ppermute | solution.py:262
  742.6 24.0 %collective-permute-start.27 = (f32[40,256]{1,0:T(8,128)S(1)}, f32[40,256]{1,0:T(8,128)S(1)}, u32[]{:S(2)}, u32[]{:S(2)}) collective-permute-start(f32[40,256]{1,0:T(8,128)S(1)} %dynamic-slice_bitcast_fusion.13), channel_id=1, source_target_pairs={{0,8},{8,0},{16,24},{24,16},{1,9},{9,1},{17,25},{25,17},{2,10},{10... | collective-permute-start | bytes 122888 | tf_op jit(solution)/shard_map/ppermute | solution.py:262
  766.7 10.4 %collective-permute-start.28 = (f32[20,256]{1,0:T(8,128)S(1)}, f32[20,256]{1,0:T(8,128)S(1)}, u32[]{:S(2)}, u32[]{:S(2)}) collective-permute-start(f32[20,256]{1,0:T(8,128)S(1)} %dynamic-slice_bitcast_fusion.14), channel_id=1, source_target_pairs={{0,16},{8,24},{16,0},{24,8},{1,17},{9,25},{17,1},{25,9},{2,18},{10... | collective-permute-start | bytes 61448 | tf_op jit(solution)/shard_map/ppermute | solution.py:262
  771.7 23.5 %collective-permute-start.19 = (f32[12,80,256]{2,1,0:T(8,128)}, f32[12,80,256]{2,1,0:T(8,128)}, u32[]{:S(2)}, u32[]{:S(2)}) collective-permute-start(f32[12,80,256]{2,1,0:T(8,128)} %dynamic-slice_bitcast_fusion.3), channel_id=1, source_target_pairs={{0,16},{8,24},{16,0},{24,8},{1,17},{9,25},{17,1},{25,9},{2,18},{10... | collective-permute-start | bytes 2949128 | tf_op jit(solution)/shard_map/ppermute | solution.py:262
  775.6 22.9 %collective-permute-start.21 = (f32[12,80,256]{2,1,0:T(8,128)}, f32[12,80,256]{2,1,0:T(8,128)}, u32[]{:S(2)}, u32[]{:S(2)}) collective-permute-start(f32[12,80,256]{2,1,0:T(8,128)} %dynamic-slice_bitcast_fusion.2), channel_id=1, source_target_pairs={{0,8},{8,0},{16,24},{24,16},{1,9},{9,1},{17,25},{25,17},{2,10},{10... | collective-permute-start | bytes 2949128 | tf_op jit(solution)/shard_map/ppermute | solution.py:262
  786.9 10.7 %collective-permute-start.32 = (f32[20,256]{1,0:T(8,128)S(1)}, f32[20,256]{1,0:T(8,128)S(1)}, u32[]{:S(2)}, u32[]{:S(2)}) collective-permute-start(f32[20,256]{1,0:T(8,128)S(1)} %add.341), channel_id=1, source_target_pairs={{0,16},{8,24},{16,0},{24,8},{1,17},{9,25},{17,1},{25,9},{2,18},{10... | collective-permute-start | bytes 61448 | tf_op jit(solution)/shard_map/ppermute | solution.py:262
  796.8 27.7 %collective-permute-start.34 = (f32[12,80,256]{2,1,0:T(8,128)S(1)}, f32[12,80,256]{2,1,0:T(8,128)S(1)}, u32[]{:S(2)}, u32[]{:S(2)}) collective-permute-start(f32[12,80,256]{2,1,0:T(8,128)S(1)} %bitcast_add_fusion.4), channel_id=1, source_target_pairs={{0,16},{8,24},{16,0},{24,8},{1,17},{9,25},{17,1},{25,9},{2,18},{10... | collective-permute-start | bytes 2949128 | tf_op jit(solution)/shard_map/ppermute | solution.py:262
  800.8 25.7 %collective-permute-start.36 = (f32[12,80,256]{2,1,0:T(8,128)}, f32[12,80,256]{2,1,0:T(8,128)}, u32[]{:S(2)}, u32[]{:S(2)}) collective-permute-start(f32[12,80,256]{2,1,0:T(8,128)} %bitcast_add_fusion.3), channel_id=1, source_target_pairs={{0,8},{8,0},{16,24},{24,16},{1,9},{9,1},{17,25},{25,17},{2,10},{10... | collective-permute-start | bytes 2949128 | tf_op jit(solution)/shard_map/ppermute | solution.py:262
  808.5 14.6 %collective-permute-start.22 = (f32[8,128]{1,0:T(8,128)S(1)}, f32[8,128]{1,0:T(8,128)S(1)}, u32[]{:S(2)}, u32[]{:S(2)}) collective-permute-start(f32[8,128]{1,0:T(8,128)S(1)} %broadcast_in_dim.71), channel_id=1, source_target_pairs={{0,8},{8,0},{16,24},{24,16},{1,9},{9,1},{17,25},{25,17},{2,10},{10... | collective-permute-start | bytes 12296 | tf_op jit(solution)/shard_map/ppermute | solution.py:262
  809.2 21.1 %collective-permute-start.33 = (f32[40,256]{1,0:T(8,128)S(1)}, f32[40,256]{1,0:T(8,128)S(1)}, u32[]{:S(2)}, u32[]{:S(2)}) collective-permute-start(f32[40,256]{1,0:T(8,128)S(1)} %pad_maximum_fusion.8), channel_id=1, source_target_pairs={{0,8},{8,0},{16,24},{24,16},{1,9},{9,1},{17,25},{25,17},{2,10},{10... | collective-permute-start | bytes 122888 | tf_op jit(solution)/shard_map/ppermute | solution.py:262
  824.9 60.7 %collective-permute-start.35 = (f32[24,80,256]{2,1,0:T(8,128)S(1)}, f32[24,80,256]{2,1,0:T(8,128)}, u32[]{:S(2)}, u32[]{:S(2)}) collective-permute-start(f32[24,80,256]{2,1,0:T(8,128)S(1)} %pad_maximum_fusion), channel_id=1, source_target_pairs={{0,8},{8,0},{16,24},{24,16},{1,9},{9,1},{17,25},{25,17},{2,10},{10... | collective-permute-start | bytes 5898248 | tf_op jit(solution)/shard_map/ppermute | solution.py:262
  829.6 56.0 %collective-permute-start.37 = (f32[24,80,256]{2,1,0:T(8,128)}, f32[24,80,256]{2,1,0:T(8,128)}, u32[]{:S(2)}, u32[]{:S(2)}) collective-permute-start(f32[24,80,256]{2,1,0:T(8,128)} %pad_maximum_fusion.1), channel_id=1, source_target_pairs={{0,16},{8,24},{16,0},{24,8},{1,17},{9,25},{17,1},{25,9},{2,18},{10... | collective-permute-start | bytes 5898248 | tf_op jit(solution)/shard_map/ppermute | solution.py:262
  (50 other events, 1212.2 us)
Sparse Core Ops, SparseCore 0:
  52.0 76.3 all-gather.5
  180.3 230.9 reduce-scatter.1
  449.2 218.2 all-gather.3
